TPU v7x, 32 devices: a whole 2x2x4 slice. The times are simulated.
32 devices in a mesh: fsdp: 4 (over z), seq: 8 (over y, x, core).
Axes of the slice: x: 2, y: 2, z: 4, core: 2. Of those that a mesh axis runs over, the one named last changes fastest.
Arguments:
- tokens: bfloat16 [4096, 2048], P(('fsdp', 'seq')), may hold values from -6 to 6
- cotangent: bfloat16 [4096, 2048], P(('fsdp', 'seq')), may hold values from -6 to 6
- adapter_index: int32 [4], replicated, may hold values from 0 to 7, as said below
- qkv_weight: bfloat16 [3, 2048, 2048], P(None, 'fsdp', 'seq'), may hold values from -0.125 to 0.125
- dense_weight: bfloat16 [2048, 2048], P('seq', 'fsdp'), may hold values from -2 to 2
- inner_weight: bfloat16 [2048, 8192], P('fsdp', 'seq'), may hold values from -0.125 to 0.125
- outer_weight: bfloat16 [8192, 2048], P('seq', 'fsdp'), may hold values from -0.0625 to 0.0625
- qkv_bias: bfloat16 [6144], replicated, may hold values from -2 to 2
- dense_bias: bfloat16 [2048], replicated, may hold values from -2 to 2
- inner_bias: bfloat16 [8192], replicated, may hold values from -2 to 2
- outer_bias: bfloat16 [2048], replicated, may hold values from -2 to 2
- norm_gain: bfloat16 [2048], replicated, may hold values from 0.25 to 1.75
- norm_bias: bfloat16 [2048], replicated, may hold values from -2 to 2
- qkv_down: bfloat16 [2048, 128], P(('fsdp', 'seq')), may hold values from -0.125 to 0.125
- qkv_up: bfloat16 [6144, 128], P(('fsdp', 'seq')), may hold values from -0.75 to 0.75
- dense_down: bfloat16 [2048, 128], P(('fsdp', 'seq')), may hold values from -0.125 to 0.125
- dense_up: bfloat16 [2048, 128], P(('fsdp', 'seq')), may hold values from -3 to 3
- inner_down: bfloat16 [2048, 128], P(('fsdp', 'seq')), may hold values from -0.125 to 0.125
- inner_up: bfloat16 [8192, 128], P(('fsdp', 'seq')), may hold values from -0.75 to 0.75
- outer_down: bfloat16 [8192, 128], P(('fsdp', 'seq')), may hold values from -0.0625 to 0.0625
- outer_up: bfloat16 [2048, 128], P(('fsdp', 'seq')), may hold values from -0.75 to 0.75
Outputs:
- layer_out: bfloat16 [4096, 2048], P(('fsdp', 'seq'))
- input_grad: float32 [4096, 2048], P(('fsdp', 'seq'))
- qkv_down_grad: float32 [2048, 128], P(('fsdp', 'seq'))
- qkv_up_grad: float32 [6144, 128], P(('fsdp', 'seq'))
- dense_down_grad: float32 [2048, 128], P(('fsdp', 'seq'))
- dense_up_grad: float32 [2048, 128], P(('fsdp', 'seq'))
- inner_down_grad: float32 [2048, 128], P(('fsdp', 'seq'))
- inner_up_grad: float32 [8192, 128], P(('fsdp', 'seq'))
- outer_down_grad: float32 [8192, 128], P(('fsdp', 'seq'))
- outer_up_grad: float32 [2048, 128], P(('fsdp', 'seq'))
Inputs may be any that keep to these rules, and one draw needn't show every extreme that they name: `adapter_index`: the adapter of each sequence; 0 and 7 each belong to some sequence.
All inputs are finite; a program needn't handle non-finite values.
Results may differ from a plain program's by a relative error of at most 0.011.
The roundings to bfloat16 on the way count: a program that leaves them out, or rounds other values in their place, can miss the bound.
Values may be sent and summed in bfloat16 or wider, within the bound.
A program may use at most 320 MiB of HBM per device.

v0:
```python
import jax
import jax.numpy as jnp
from jax import lax
from jax.sharding import PartitionSpec as P

H = 32
HD = 64
ROT = 32
RANK = 16
ADAPT = 8
BLOCK = 256
QBLK = 512


EPSILON = 1e-05
ADAPTER_SCALE = 2.0
ROPE_BASE = 10000.0
MASKED = -1e30
CONTRACT_LAST = (((1,), (1,)), ((), ()))
CONTRACT_FIRST = (((0,), (0,)), ((), ()))


def norm_layer(values, scale_gain, offset_bias):
    row_mean = jnp.mean(values, axis=-1, keepdims=True)
    centred = values - row_mean
    spread = jnp.mean(centred * centred, axis=-1, keepdims=True)
    return centred * lax.rsqrt(spread + EPSILON) * scale_gain + offset_bias


def rope_tables(positions):
    frequency = ROPE_BASE ** (-2.0 * jnp.arange(ROT // 2, dtype=jnp.float32) / ROT)
    angles = positions.astype(jnp.float32)[:, None] * frequency[None, :]
    return (jnp.cos(angles)[:, None, :], jnp.sin(angles)[:, None, :])


def rotate(values, cos_table, sin_table):
    first_half = values[..., : ROT // 2]
    second_half = values[..., ROT // 2 : ROT]
    return jnp.concatenate(
        [
            first_half * cos_table - second_half * sin_table,
            second_half * cos_table + first_half * sin_table,
            values[..., ROT:],
        ],
        axis=-1,
    )


def rope_rows(flat_rows, cos_table, sin_table, count, heads):
    pieces = flat_rows.reshape(count, 3, heads, HD)
    turned = jnp.stack(
        [
            rotate(pieces[:, 0], cos_table, sin_table),
            rotate(pieces[:, 1], cos_table, sin_table),
            pieces[:, 2],
        ],
        axis=1,
    )
    return turned.reshape(flat_rows.shape)


def product_trailing_axis(left_side, right_side):
    return lax.dot_general(left_side, right_side, CONTRACT_LAST, preferred_element_type=jnp.float32)


def product_leading_axis(left_side, right_side):
    return lax.dot_general(
        left_side, right_side, CONTRACT_FIRST, preferred_element_type=jnp.float32
    )


def on_device(
    tokens,
    cotangent,
    adapter_index,
    qkv_weight,
    dense_weight,
    inner_weight,
    outer_weight,
    qkv_bias,
    dense_bias,
    inner_bias,
    outer_bias,
    norm_gain,
    norm_bias,
    qkv_down,
    qkv_up,
    dense_down,
    dense_up,
    inner_down,
    inner_up,
    outer_down,
    outer_up,
):
    groups = lax.axis_size("seq")
    row_count = tokens.shape[0]
    model_width = tokens.shape[1]
    length = row_count * groups
    head_count = H // groups
    per_group = head_count * HD
    columns = ADAPT * RANK
    score_scale = HD ** (-0.5)
    seq_place = lax.axis_index("seq")
    chosen = adapter_index[lax.axis_index("fsdp")]
    column_mask = (jnp.arange(columns) // RANK == chosen).astype(jnp.float32)
    frozen_local = (
        lax.all_gather(qkv_weight, "fsdp", axis=1, tiled=True),
        lax.all_gather(dense_weight, "fsdp", axis=1, tiled=True),
        lax.all_gather(inner_weight, "fsdp", axis=0, tiled=True),
        lax.all_gather(outer_weight, "fsdp", axis=1, tiled=True),
    )
    adapters = (
        lax.all_gather(qkv_down, ("fsdp", "seq"), axis=0, tiled=True),
        lax.all_gather(qkv_up, ("fsdp", "seq"), axis=0, tiled=True),
        lax.all_gather(dense_down, ("fsdp", "seq"), axis=0, tiled=True),
        lax.all_gather(dense_up, ("fsdp", "seq"), axis=0, tiled=True),
        lax.all_gather(inner_down, ("fsdp", "seq"), axis=0, tiled=True),
        lax.all_gather(inner_up, ("fsdp", "seq"), axis=0, tiled=True),
        lax.all_gather(outer_down, ("fsdp", "seq"), axis=0, tiled=True),
        lax.all_gather(outer_up, ("fsdp", "seq"), axis=0, tiled=True),
    )
    down_qkv, query_key_value_up_weight, down_dense, dense_up_weight = (
        adapters[0],
        adapters[1],
        adapters[2],
        adapters[3],
    )
    down_inner, inner_up_weight, down_outer, outer_up_weight = (
        adapters[4],
        adapters[5],
        adapters[6],
        adapters[7],
    )

    def coeff_of(inputs, down_matrix):
        return (
            jnp.dot(inputs, down_matrix, preferred_element_type=jnp.float32) * column_mask
        ).astype(jnp.bfloat16)

    def adapter_backward(
        inputs, adapter_factors, down_matrix, up_projection_matrix, low_rank_gradient
    ):
        up_weight_gradient = ADAPTER_SCALE * product_leading_axis(
            low_rank_gradient, adapter_factors
        )
        coeff_grad = (
            ADAPTER_SCALE
            * jnp.dot(low_rank_gradient, up_projection_matrix, preferred_element_type=jnp.float32)
            * column_mask
        ).astype(jnp.bfloat16)
        down_grad = product_leading_axis(inputs, coeff_grad)
        return (down_grad, up_weight_gradient, product_trailing_axis(coeff_grad, down_matrix))

    key_block = jnp.arange(length) // BLOCK
    starts = jnp.arange(length // QBLK) * QBLK

    def block_scores(query_rows, key_heads, offset):
        scores = (
            jnp.einsum("qhd,khd->hqk", query_rows, key_heads, preferred_element_type=jnp.float32)
            * score_scale
        )
        allowed = key_block[None, :] <= ((offset + jnp.arange(QBLK)) // BLOCK)[:, None]
        return jnp.where(allowed[None], scores, MASKED)

    gain_value = norm_gain.astype(jnp.float32)
    shift_value = norm_bias.astype(jnp.float32)
    source = tokens.astype(jnp.float32)
    normed_low = norm_layer(source, gain_value, shift_value).astype(jnp.bfloat16)
    query_key_value_factor = coeff_of(normed_low, down_qkv)
    inner_adapter_factor = coeff_of(normed_low, down_inner)
    whole = (
        lax.all_gather(frozen_local[0], "seq", axis=2, tiled=True),
        lax.all_gather(frozen_local[1], "seq", axis=0, tiled=True),
        lax.all_gather(frozen_local[2], "seq", axis=1, tiled=True),
        lax.all_gather(frozen_local[3], "seq", axis=0, tiled=True),
    )
    whole_qkv, whole_dense, whole_inner, whole_outer = (whole[0], whole[1], whole[2], whole[3])
    cos_table, sin_table = rope_tables(seq_place * row_count + jnp.arange(row_count))

    def rope_mine(flat_rows):
        return rope_rows(flat_rows, cos_table, sin_table, row_count, H)

    projected = (
        jnp.einsum(
            "td,cde->tce", normed_low, whole_qkv, preferred_element_type=jnp.float32
        ).reshape(row_count, 3 * model_width)
        + qkv_bias.astype(jnp.float32)
        + ADAPTER_SCALE * product_trailing_axis(query_key_value_factor, query_key_value_up_weight)
    )
    outgoing = rope_mine(projected).astype(jnp.bfloat16).reshape(row_count, 3, groups, per_group)
    head_stack = lax.all_to_all(outgoing, "seq", split_axis=2, concat_axis=0, tiled=True).reshape(
        length, 3, head_count, HD
    )
    query_heads, key_heads, value_heads = (head_stack[:, 0], head_stack[:, 1], head_stack[:, 2])

    def attend(offset):
        query_rows = lax.dynamic_slice_in_dim(query_heads, offset, QBLK, 0)
        scores = block_scores(query_rows, key_heads, offset)
        row_max = jnp.max(scores, axis=-1, keepdims=True)
        exponent = jnp.exp(scores - row_max)
        row_total = jnp.sum(exponent, axis=-1, keepdims=True)
        prob_low = (exponent / row_total).astype(jnp.bfloat16)
        output = jnp.einsum(
            "hqk,khd->qhd", prob_low, value_heads, preferred_element_type=jnp.float32
        )
        return (output.astype(jnp.bfloat16), (row_max + jnp.log(row_total))[..., 0])

    outputs, logsum = lax.map(attend, starts)
    attended_heads, logsum = (outputs.reshape(length, per_group), logsum)
    attended = lax.all_to_all(
        attended_heads.reshape(length, 1, per_group), "seq", split_axis=0, concat_axis=1, tiled=True
    ).reshape(row_count, model_width)
    dense_adapter_factor = coeff_of(attended, down_dense)
    attn_branch = (
        jnp.dot(attended, whole_dense, preferred_element_type=jnp.float32)
        + dense_bias.astype(jnp.float32)
        + ADAPTER_SCALE * product_trailing_axis(dense_adapter_factor, dense_up_weight)
    )
    pre_act = (
        jnp.dot(normed_low, whole_inner, preferred_element_type=jnp.float32)
        + inner_bias.astype(jnp.float32)
        + ADAPTER_SCALE * product_trailing_axis(inner_adapter_factor, inner_up_weight)
    )
    activated = jax.nn.gelu(pre_act, approximate=True).astype(jnp.bfloat16)
    outer_adapter_factor = coeff_of(activated, down_outer)
    mlp_branch = (
        jnp.dot(activated, whole_outer, preferred_element_type=jnp.float32)
        + outer_bias.astype(jnp.float32)
        + ADAPTER_SCALE * product_trailing_axis(outer_adapter_factor, outer_up_weight)
    )
    layer_out = (source + attn_branch + mlp_branch).astype(jnp.bfloat16)
    outer_down_grad, outer_up_grad, outer_input = adapter_backward(
        activated, outer_adapter_factor, down_outer, outer_up_weight, cotangent
    )
    act_grad = product_trailing_axis(cotangent, whole_outer) + outer_input
    unused_out, gelu_back = jax.vjp(
        lambda inner_value: jax.nn.gelu(inner_value, approximate=True), pre_act
    )
    pre_grad = gelu_back(act_grad)[0].astype(jnp.bfloat16)
    inner_down_grad, inner_up_grad, inner_input = adapter_backward(
        normed_low, inner_adapter_factor, down_inner, inner_up_weight, pre_grad
    )
    dense_down_grad, dense_up_grad, dense_input = adapter_backward(
        attended, dense_adapter_factor, down_dense, dense_up_weight, cotangent
    )
    attended_grad = (
        (product_trailing_axis(cotangent, whole_dense) + dense_input)
        .astype(jnp.bfloat16)
        .reshape(row_count, groups, per_group)
    )
    head_grad = lax.all_to_all(
        attended_grad, "seq", split_axis=1, concat_axis=0, tiled=True
    ).reshape(length, head_count, HD)

    def attend_back(grads_pair, block_input):
        offset, block_logsum = block_input
        query_rows = lax.dynamic_slice_in_dim(query_heads, offset, QBLK, 0)
        out_rows = lax.dynamic_slice_in_dim(head_grad, offset, QBLK, 0)
        probability = jnp.exp(block_scores(query_rows, key_heads, offset) - block_logsum[..., None])
        prob_low = probability.astype(jnp.bfloat16)
        value_grad = grads_pair[1] + jnp.einsum(
            "hqk,qhd->khd", prob_low, out_rows, preferred_element_type=jnp.float32
        )
        prob_grad = jnp.einsum(
            "qhd,khd->hqk", out_rows, value_heads, preferred_element_type=jnp.float32
        )
        row_dot = jnp.sum(prob_grad * probability, axis=-1, keepdims=True)
        score_grad = (probability * (prob_grad - row_dot)).astype(jnp.bfloat16)
        query_grad = (
            jnp.einsum("hqk,khd->qhd", score_grad, key_heads, preferred_element_type=jnp.float32)
            * score_scale
        )
        key_grad = (
            grads_pair[0]
            + jnp.einsum("hqk,qhd->khd", score_grad, query_rows, preferred_element_type=jnp.float32)
            * score_scale
        )
        return ((key_grad, value_grad), query_grad.astype(jnp.bfloat16))

    zero_grads = jnp.zeros((length, head_count, HD), jnp.float32)
    final_pair, query_blocks = lax.scan(attend_back, (zero_grads, zero_grads), (starts, logsum))
    back_stack = jnp.stack(
        [
            query_blocks.reshape(length, per_group),
            final_pair[0].astype(jnp.bfloat16).reshape(length, per_group),
            final_pair[1].astype(jnp.bfloat16).reshape(length, per_group),
        ],
        axis=1,
    )[:, :, None, :]
    returned = lax.all_to_all(back_stack, "seq", split_axis=0, concat_axis=2, tiled=True).reshape(
        row_count, 3 * model_width
    )
    unused_rope, rope_back = jax.vjp(rope_mine, projected)
    qkv_grad = rope_back(returned.astype(jnp.float32))[0].astype(jnp.bfloat16)
    qkv_down_grad, qkv_up_grad, qkv_input = adapter_backward(
        normed_low, query_key_value_factor, down_qkv, query_key_value_up_weight, qkv_grad
    )
    normed_grad = (
        jnp.einsum(
            "tce,cde->td",
            qkv_grad.reshape(row_count, 3, model_width),
            whole_qkv,
            preferred_element_type=jnp.float32,
        )
        + qkv_input
        + product_trailing_axis(pre_grad, whole_inner)
        + inner_input
    )
    unused_norm, norm_back = jax.vjp(
        lambda inner_value: norm_layer(inner_value, gain_value, shift_value), source
    )
    input_grad = cotangent.astype(jnp.float32) + norm_back(normed_grad)[0]
    all_grads = (
        qkv_down_grad,
        qkv_up_grad,
        dense_down_grad,
        dense_up_grad,
        inner_down_grad,
        inner_up_grad,
        outer_down_grad,
        outer_up_grad,
    )
    summed_grads = (
        lax.psum_scatter(all_grads[0], ("fsdp", "seq"), scatter_dimension=0, tiled=True),
        lax.psum_scatter(all_grads[1], ("fsdp", "seq"), scatter_dimension=0, tiled=True),
        lax.psum_scatter(all_grads[2], ("fsdp", "seq"), scatter_dimension=0, tiled=True),
        lax.psum_scatter(all_grads[3], ("fsdp", "seq"), scatter_dimension=0, tiled=True),
        lax.psum_scatter(all_grads[4], ("fsdp", "seq"), scatter_dimension=0, tiled=True),
        lax.psum_scatter(all_grads[5], ("fsdp", "seq"), scatter_dimension=0, tiled=True),
        lax.psum_scatter(all_grads[6], ("fsdp", "seq"), scatter_dimension=0, tiled=True),
        lax.psum_scatter(all_grads[7], ("fsdp", "seq"), scatter_dimension=0, tiled=True),
    )
    return (
        layer_out,
        input_grad,
        summed_grads[0],
        summed_grads[1],
        summed_grads[2],
        summed_grads[3],
        summed_grads[4],
        summed_grads[5],
        summed_grads[6],
        summed_grads[7],
    )


def solution(mesh):
    placed = (
        P(("fsdp", "seq"), None),
        P(("fsdp", "seq"), None),
        P(),
        P(None, "fsdp", "seq"),
        P("seq", "fsdp"),
        P("fsdp", "seq"),
        P("seq", "fsdp"),
        P(),
        P(),
        P(),
        P(),
        P(),
        P(),
        P(("fsdp", "seq"), None),
        P(("fsdp", "seq"), None),
        P(("fsdp", "seq"), None),
        P(("fsdp", "seq"), None),
        P(("fsdp", "seq"), None),
        P(("fsdp", "seq"), None),
        P(("fsdp", "seq"), None),
        P(("fsdp", "seq"), None),
    )
    return jax.shard_map(
        on_device,
        mesh=mesh,
        in_specs=placed,
        out_specs=(
            P(("fsdp", "seq"), None),
            P(("fsdp", "seq"), None),
            P(("fsdp", "seq"), None),
            P(("fsdp", "seq"), None),
            P(("fsdp", "seq"), None),
            P(("fsdp", "seq"), None),
            P(("fsdp", "seq"), None),
            P(("fsdp", "seq"), None),
            P(("fsdp", "seq"), None),
            P(("fsdp", "seq"), None),
        ),
        check_vma=False,
    )
```

profile of v0, /device:TPU:0, one launch (start us, length us, event | category | flops | bytes accessed | tf_op | source)
XLA Modules:
  0.0 2076.0 jit_solution(3318004089724453644)
XLA Ops:
  10.0 65.8 %all-gather.12.cloned.1.call-done = bf16[3,2048,256]{2,1,0:T(8,128)(2,1)} async-done(((bf16[3,512,256]{2,1,0:T(8,128)(2,1)}), bf16[3,2048,256]{2,1,0:T(8,128)(2,1)}) %all-gather.12.cloned.1.call-update) | async-done | bytes 3145744 | tf_op jit(solution)/shard_map/all_gather | solution.py:107
  76.4 27.6 %all-gather.18.cloned.1.call-done = bf16[256,2048]{1,0:T(8,128)(2,1)} async-done(((bf16[256,512]{1,0:T(8,128)(2,1)}), bf16[256,2048]{1,0:T(8,128)(2,1)}) %all-gather.18.cloned.1.call-update) | async-done | bytes 1048592 | tf_op jit(solution)/shard_map/all_gather | solution.py:108
  104.1 81.8 %all-gather.22.cloned.1.call-done = bf16[2048,1024]{1,0:T(8,128)(2,1)} async-done(((bf16[512,1024]{1,0:T(8,128)(2,1)}), bf16[2048,1024]{1,0:T(8,128)(2,1)}) %all-gather.22.cloned.1.call-update) | async-done | bytes 4194320 | tf_op jit(solution)/shard_map/all_gather | solution.py:109
  186.7 79.9 %all-gather.28.cloned.1.call-done = bf16[1024,2048]{1,0:T(8,128)(2,1)} async-done(((bf16[1024,512]{1,0:T(8,128)(2,1)}), bf16[1024,2048]{1,0:T(8,128)(2,1)}) %all-gather.28.cloned.1.call-update) | async-done | bytes 4194320 | tf_op jit(solution)/shard_map/all_gather | solution.py:110
  269.8 41.2 %all_gather.50 = bf16[2048,128]{1,0:T(8,128)(2,1)S(1)} all-gather(bf16[64,128]{1,0:T(8,128)(2,1)S(1)} %copy-done.38), channel_id=1, replica_groups=mesh['fsdp'=4,'seq'=8] {'fsdp','seq'}, dimensions={0}, use_global_device_ids=true | all-gather | bytes 540672 | tf_op jit(solution)/shard_map/all_gather | solution.py:113
  311.0 41.3 %all_gather.55 = bf16[2048,128]{1,0:T(8,128)(2,1)} all-gather(bf16[64,128]{1,0:T(8,128)(2,1)S(1)} %copy-done.39), channel_id=1, replica_groups=mesh['fsdp'=4,'seq'=8] {'fsdp','seq'}, dimensions={0}, use_global_device_ids=true | all-gather | bytes 540672 | tf_op jit(solution)/shard_map/all_gather | solution.py:116
  354.0 50.0 %all-gather.14.cloned.1.call-done = bf16[3,2048,2048]{2,1,0:T(8,128)(2,1)} async-done(((bf16[3,2048,256]{2,1,0:T(8,128)(2,1)}), bf16[3,2048,2048]{2,1,0:T(8,128)(2,1)}) %all-gather.14.cloned.1.call-update) | async-done | bytes 25165840 | tf_op jit(solution)/shard_map/all_gather | solution.py:172
  404.0 14.8 fusion.90
  421.2 39.9 %all-gather.16.cloned.1.call-done = bf16[6144,128]{1,0:T(8,128)(2,1)} async-done(((bf16[192,128]{1,0:T(8,128)(2,1)}), bf16[6144,128]{1,0:T(8,128)(2,1)}) %all-gather.16.cloned.1.call-update) | async-done | bytes 1572880 | tf_op jit(solution)/shard_map/all_gather | solution.py:114
  476.0 59.6 %all_gather.54 = bf16[2048,128]{1,0:T(8,128)(2,1)S(1)} all-gather(bf16[64,128]{1,0:T(8,128)(2,1)S(1)} %copy-done.40), channel_id=1, replica_groups=mesh['fsdp'=4,'seq'=8] {'fsdp','seq'}, dimensions={0}, use_global_device_ids=true | all-gather | bytes 540672 | tf_op jit(solution)/shard_map/all_gather | solution.py:115
  535.6 6.4 fusion.95
  543.2 4.2 all-to-all-start.2
  553.4 23.2 %while.32 = (s32[]{:T(128)}, bf16[2,512,4,64]{1,3,2,0:T(8,128)(2,1)S(1)}, f32[2,4,512]{2,1,0:T(4,128)S(1)}, s32[2]{0:T(128)S(1)}, bf16[1024,4,64]{0,2,1:T(8,128)...) while((s32[]{:T(128)}, ...), condition=%wide.region_5.6_spmd.clone, body=%wide.region_2.5_spmd.clone.sunk | while | flops 562706432 | bytes 28913828 | solution.py:208
  578.0 3.9 reshape.305
  582.4 3.8 reduce
  587.2 4.1 all-to-all-start.1
  591.3 8.8 reduce-scatter.25.cloned.1.call-start
  619.6 52.1 %while.33 = (s32[]{:T(128)}, f32[1024,4,64]{0,2,1:T(8,128)S(1)}, f32[1024,4,64]{0,2,1:T(8,128)}, bf16[2,512,4,64]{1,3,2,0:T(8,128)(2,1)}, s32[2]{0:T(128)S(1)}, ...) while((s32[]{:T(128)}, f32[1024,4,64]{0,2,1:T(8,128)S(1)}, ...), condition=%wide.region_8.9_spmd.clone, body=%wide.region_6.8_spmd.clone.sunk | while | flops 1375746048 | bytes 143463248 | solution.py:281
  624.6 4.7 multiply_reduce_fusion.2
  636.4 5.1 fusion.207
  650.1 4.7 multiply_reduce_fusion.2
  658.6 3.8 fusion.205
  662.4 4.6 fusion.207
  667.0 4.6 fusion.206
  679.6 4.0 all-to-all-start.3
  685.0 42.2 %all-to-all-done.3 = bf16[1024,3,1,256]{3,1,2,0:T(4,128)(2,1)S(1)} async-done(((bf16[1024,3,1,256]{3,1,2,0:T(4,128)(2,1)}), bf16[1024,3,1,256]{3,1,2,0:T(4,128)(2,1)S(1)}, u32[]{:S(2)}, u32[]{:S(2)}) %all-to-all-start.3) | async-done | bytes 1572896 | tf_op jit(solution)/shard_map/all_to_all | solution.py:290
  738.9 41.3 %all_gather.58 = bf16[2048,128]{1,0:T(8,128)(2,1)S(1)} all-gather(bf16[64,128]{1,0:T(8,128)(2,1)S(1)} %copy-done.42), channel_id=1, replica_groups=mesh['fsdp'=4,'seq'=8] {'fsdp','seq'}, dimensions={0}, use_global_device_ids=true | all-gather | bytes 540672 | tf_op jit(solution)/shard_map/all_gather | solution.py:117
  781.3 38.7 %all_gather.63 = bf16[2048,128]{1,0:T(8,128)(2,1)S(1)} all-gather(bf16[64,128]{1,0:T(8,128)(2,1)S(1)} %copy-done.43), channel_id=1, replica_groups=mesh['fsdp'=4,'seq'=8] {'fsdp','seq'}, dimensions={0}, use_global_device_ids=true | all-gather | bytes 540672 | tf_op jit(solution)/shard_map/all_gather | solution.py:120
  823.3 17.1 convolution_add_fusion.1
  840.4 7.4 multiply_convert_fusion.1
  847.8 105.1 %all-gather.30.cloned.1.call-done = bf16[8192,2048]{1,0:T(8,128)(2,1)} async-done(((bf16[1024,2048]{1,0:T(8,128)(2,1)}), bf16[8192,2048]{1,0:T(8,128)(2,1)}) %all-gather.30.cloned.1.call-update) | async-done | bytes 33554448 | tf_op jit(solution)/shard_map/all_gather | solution.py:175
  952.9 17.5 fusion.96
  970.4 41.8 %all-gather.32.cloned.1.call-done = bf16[8192,128]{1,0:T(8,128)(2,1)} async-done(((bf16[256,128]{1,0:T(8,128)(2,1)}), bf16[8192,128]{1,0:T(8,128)(2,1)}) %all-gather.32.cloned.1.call-update) | async-done | bytes 2097168 | tf_op jit(solution)/shard_map/all_gather | solution.py:119
  1012.2 6.6 fusion.62
  1029.2 4.3 convolution_multiply_fusion.2
  1033.6 4.4 fusion.101
  1038.7 4.7 convolution_add_fusion.6
  1044.8 14.2 convolution_bitcast_fusion
  1059.0 16.5 fusion.97
  1077.2 13.2 convolution_add_fusion.5
  1092.9 55.6 %reduce-scatter.25.cloned.1.call-done = f32[64,128]{1,0:T(8,128)} async-done(((f32[2048,128]{1,0:T(8,128)}), f32[64,128]{1,0:T(8,128)}) %reduce-scatter.25.cloned.1.call-update) | async-done | bytes 32784
  1148.6 133.7 %reduce-scatter.17.cloned.1.call-done = f32[64,128]{1,0:T(8,128)} async-done(((f32[2048,128]{1,0:T(8,128)}), f32[64,128]{1,0:T(8,128)}) %reduce-scatter.17.cloned.1.call-update) | async-done | bytes 32784 | tf_op jit(solution)/shard_map/reduce_scatter | solution.py:326
  1282.2 133.4 %reduce-scatter.13.cloned.1.call-done = f32[64,128]{1,0:T(8,128)} async-done(((f32[2048,128]{1,0:T(8,128)}), f32[64,128]{1,0:T(8,128)}) %reduce-scatter.13.cloned.1.call-update) | async-done | bytes 32784 | tf_op jit(solution)/shard_map/reduce_scatter | solution.py:324
  1415.7 104.2 %reduce-scatter.15.cloned.1.call-done = f32[192,128]{1,0:T(8,128)} async-done(((f32[6144,128]{1,0:T(8,128)}), f32[192,128]{1,0:T(8,128)}) %reduce-scatter.15.cloned.1.call-update) | async-done | bytes 98320 | tf_op jit(solution)/shard_map/reduce_scatter | solution.py:325
  1519.9 136.6 %reduce-scatter.19.cloned.1.call-done = f32[64,128]{1,0:T(8,128)} async-done(((f32[2048,128]{1,0:T(8,128)}), f32[64,128]{1,0:T(8,128)}) %reduce-scatter.19.cloned.1.call-update) | async-done | bytes 32784 | tf_op jit(solution)/shard_map/reduce_scatter | solution.py:328
  1656.5 133.4 %reduce-scatter.27.cloned.1.call-done = f32[64,128]{1,0:T(8,128)} async-done(((f32[2048,128]{1,0:T(8,128)}), f32[64,128]{1,0:T(8,128)}) %reduce-scatter.27.cloned.1.call-update) | async-done | bytes 32784
  1789.9 139.6 %reduce-scatter.21.cloned.1.call-done = f32[256,128]{1,0:T(8,128)} async-done(((f32[8192,128]{1,0:T(8,128)}), f32[256,128]{1,0:T(8,128)}) %reduce-scatter.21.cloned.1.call-update) | async-done | bytes 131088 | tf_op jit(solution)/shard_map/reduce_scatter | solution.py:329
  1929.5 139.8 %reduce-scatter.23.cloned.1.call-done = f32[256,128]{1,0:T(8,128)} async-done(((f32[8192,128]{1,0:T(8,128)}), f32[256,128]{1,0:T(8,128)}) %reduce-scatter.23.cloned.1.call-update) | async-done | bytes 131088 | tf_op jit(solution)/shard_map/reduce_scatter | solution.py:330
  (287 shorter events, 136.7 us)
Async XLA Ops:
  7.2 68.6 %all-gather.12.cloned.1.call-start = ((), (), s32[]{:S(2)}) async-start(), calls=%async_computation.12 | async-start | bytes 3932160 | tf_op jit(solution)/shard_map/all_gather | solution.py:107
  7.9 96.1 %all-gather.18.cloned.1.call-start = ((), (), s32[]{:S(2)}) async-start(), calls=%async_computation.15 | async-start | bytes 1310720 | tf_op jit(solution)/shard_map/all_gather | solution.py:108
  8.7 177.2 %all-gather.22.cloned.1.call-start = ((), (), s32[]{:S(2)}) async-start(), calls=%async_computation.17 | async-start | bytes 5242880 | tf_op jit(solution)/shard_map/all_gather | solution.py:109
  9.4 257.2 %all-gather.28.cloned.1.call-start = ((), (), s32[]{:S(2)}) async-start(), calls=%async_computation.20 | async-start | bytes 5242880 | tf_op jit(solution)/shard_map/all_gather | solution.py:110
  10.0 394.0 %all-gather.14.cloned.1.call-start = ((), (), s32[]{:S(2)}) async-start(), calls=%async_computation.13 | async-start | bytes 28311552 | tf_op jit(solution)/shard_map/all_gather | solution.py:172
  75.8 385.3 %all-gather.16.cloned.1.call-start = ((), (), s32[]{:S(2)}) async-start(), calls=%async_computation.14 | async-start | bytes 1622016 | tf_op jit(solution)/shard_map/all_gather | solution.py:114
  76.4 459.2 %all-gather.20.cloned.1.call-start = ((), (), s32[]{:S(2)}) async-start(), calls=%async_computation.16 | async-start | bytes 9437184 | tf_op jit(solution)/shard_map/all_gather | solution.py:173
  104.0 719.3 %all-gather.24.cloned.1.call-start = ((), (), s32[]{:S(2)}) async-start(), calls=%async_computation.18 | async-start | bytes 37748736 | tf_op jit(solution)/shard_map/all_gather | solution.py:174
  185.9 81.5 %copy-start.7 = (bf16[128,2048]{1,0:T(8,128)(2,1)S(1)}, bf16[128,2048]{1,0:T(8,128)(2,1)}, u32[]{:S(2)}) copy-start(bf16[128,2048]{1,0:T(8,128)(2,1)} %param.25) | copy-start | bytes 1572868
  185.9 82.6 %copy-start.51 = (bf16[2048]{0:T(1024)(128)(2,1)S(1)}, bf16[2048]{0:T(1024)(128)(2,1)}, u32[]{:S(2)}) copy-start(bf16[2048]{0:T(1024)(128)(2,1)} %param.36) | copy-start | bytes 12292
  185.9 82.6 %copy-start.52 = (bf16[2048]{0:T(1024)(128)(2,1)S(1)}, bf16[2048]{0:T(1024)(128)(2,1)}, u32[]{:S(2)}) copy-start(bf16[2048]{0:T(1024)(128)(2,1)} %param.37) | copy-start | bytes 12292
  185.9 82.6 %copy-start.57 = (s32[4]{0:T(128)S(1)}, s32[4]{0:T(128)}, u32[]{:S(2)}) copy-start(s32[4]{0:T(128)} %param.27) | copy-start | bytes 52
  185.9 83.9 %copy-start.38 = (bf16[64,128]{1,0:T(8,128)(2,1)S(1)}, bf16[64,128]{1,0:T(8,128)(2,1)}, u32[]{:S(2)}) copy-start(bf16[64,128]{1,0:T(8,128)(2,1)} %param.38) | copy-start | bytes 49156
  185.9 125.1 %copy-start.46 = (bf16[6144]{0:T(1024)(128)(2,1)S(1)}, bf16[6144]{0:T(1024)(128)(2,1)}, u32[]{:S(2)}) copy-start(bf16[6144]{0:T(1024)(128)(2,1)} %param.32) | copy-start | bytes 36868
  185.9 125.1 %copy-start.39 = (bf16[64,128]{1,0:T(8,128)(2,1)S(1)}, bf16[64,128]{1,0:T(8,128)(2,1)}, u32[]{:S(2)}) copy-start(bf16[64,128]{1,0:T(8,128)(2,1)} %param.41) | copy-start | bytes 49156
  185.9 654.5 %all-gather.26.cloned.1.call-start = ((), (), s32[]{:S(2)}) async-start(), calls=%async_computation.19 | async-start | bytes 2162688 | tf_op jit(solution)/shard_map/all_gather | solution.py:118
  186.7 766.2 %all-gather.30.cloned.1.call-start = ((), (), s32[]{:S(2)}) async-start(), calls=%async_computation.21 | async-start | bytes 37748736 | tf_op jit(solution)/shard_map/all_gather | solution.py:175
  266.6 745.5 %all-gather.32.cloned.1.call-start = ((), (), s32[]{:S(2)}) async-start(), calls=%async_computation.22 | async-start | bytes 2162688 | tf_op jit(solution)/shard_map/all_gather | solution.py:119
  267.6 86.4 %copy-start.44 = (f32[128]{0:T(128)}, f32[128]{0:T(128)S(1)}, u32[]{:S(2)}) copy-start(f32[128]{0:T(128)S(1)} %broadcast_multiply_fusion) | copy-start | bytes 1540
  268.5 150.4 %copy-start.49 = (f32[128]{0:T(128)}, f32[128]{0:T(128)S(1)}, u32[]{:S(2)}) copy-start(f32[128]{0:T(128)S(1)} %fusion.92) | copy-start | bytes 1540
  268.5 85.5 %copy-start.32 = (f32[2048]{0:T(1024)}, f32[2048]{0:T(1024)S(1)}, u32[]{:S(2)}) copy-start(f32[2048]{0:T(1024)S(1)} %convert_element_type.145) | copy-start | bytes 24580
  310.9 43.0 %copy-start.14 = (bf16[2048,128]{1,0:T(8,128)(2,1)}, bf16[2048,128]{1,0:T(8,128)(2,1)S(1)}, u32[]{:S(2)}) copy-start(bf16[2048,128]{1,0:T(8,128)(2,1)S(1)} %all_gather.50) | copy-start | bytes 1572868
  352.4 117.1 %copy-start.34 = (f32[128,16]{0,1:T(8,128)}, f32[128,16]{0,1:T(8,128)S(1)}, u32[]{:S(2)}) copy-start(f32[128,16]{0,1:T(8,128)S(1)} %get-tuple-element.427) | copy-start | bytes 24580
  352.4 117.1 %copy-start.36 = (f32[128,16]{0,1:T(8,128)}, f32[128,16]{0,1:T(8,128)S(1)}, u32[]{:S(2)}) copy-start(f32[128,16]{0,1:T(8,128)S(1)} %get-tuple-element.428) | copy-start | bytes 24580
  354.0 107.1 %copy-start.26 = (bf16[128,128]{1,0:T(8,128)(2,1)}, bf16[128,128]{1,0:T(8,128)(2,1)S(1)}, u32[]{:S(2)}) copy-start(bf16[128,128]{1,0:T(8,128)(2,1)S(1)} %fusion.77) | copy-start | bytes 98308
  471.4 71.9 %all-to-all-start = ((bf16[128,3,8,256]{0,3,1,2:T(8,128)(2,1)}), bf16[128,3,8,256]{0,3,1,2:T(8,128)(2,1)S(1)}, u32[]{:S(2)}, u32[]{:S(2)}) async-start(bf16[128,3,8,256]{0,3,1,2:T(8,128)(2,1)} %copy.82), calls=%async_computation | async-start | bytes 3145728 | tf_op jit(solution)/shard_map/all_to_all | solution.py:191
  475.6 66.4 %copy-start.47 = (f32[128]{0:T(128)}, f32[128]{0:T(128)S(1)}, u32[]{:S(2)}) copy-start(f32[128]{0:T(128)S(1)} %compare_select_fusion) | copy-start | bytes 1540
  476.0 66.1 %copy-start.30 = (bf16[128,128]{1,0:T(8,128)(2,1)}, bf16[128,128]{1,0:T(8,128)(2,1)S(1)}, u32[]{:S(2)}) copy-start(bf16[128,128]{1,0:T(8,128)(2,1)S(1)} %fusion.81) | copy-start | bytes 98308
  543.2 44.0 %all-to-all-start.2 = ((bf16[128,8,256]{2,0,1:T(8,128)(2,1)}), bf16[128,8,256]{2,0,1:T(8,128)(2,1)}, u32[]{:S(2)}, u32[]{:S(2)}) async-start(bf16[128,8,256]{2,0,1:T(8,128)(2,1)} %bitcast.165), calls=%async_computation.2 | async-start | bytes 1048576 | tf_op jit(solution)/shard_map/all_to_all | solution.py:251
  587.2 19.8 all-to-all-start.1
  591.3 557.3 %reduce-scatter.25.cloned.1.call-start = ((), (), s32[]{:S(2)}) async-start(), calls=%async_computation.29 | async-start | bytes 1081344
  679.6 47.6 %all-to-all-start.3 = ((bf16[1024,3,1,256]{3,1,2,0:T(4,128)(2,1)}), bf16[1024,3,1,256]{3,1,2,0:T(4,128)(2,1)S(1)}, u32[]{:S(2)}, u32[]{:S(2)}) async-start(bf16[1024,3,1,256]{3,1,2,0:T(4,128)(2,1)} %copy.90), calls=%async_computation.3 | async-start | bytes 4194304 | tf_op jit(solution)/shard_map/all_to_all | solution.py:290
  683.6 598.7 %reduce-scatter.17.cloned.1.call-start = ((), (), s32[]{:S(2)}) async-start(), calls=%async_computation.25 | async-start | bytes 1081344 | tf_op jit(solution)/shard_map/reduce_scatter | solution.py:326
  685.0 730.7 %reduce-scatter.13.cloned.1.call-start = ((), (), s32[]{:S(2)}) async-start(), calls=%async_computation.23 | async-start | bytes 1081344 | tf_op jit(solution)/shard_map/reduce_scatter | solution.py:324
  736.0 45.2 %copy-start.43 = (bf16[64,128]{1,0:T(8,128)(2,1)S(1)}, bf16[64,128]{1,0:T(8,128)(2,1)}, u32[]{:S(2)}) copy-start(bf16[64,128]{1,0:T(8,128)(2,1)} %param.45) | copy-start | bytes 49156
  736.8 84.2 %copy-start.27 = (bf16[128,128]{1,0:T(8,128)(2,1)S(1)}, bf16[128,128]{1,0:T(8,128)(2,1)}, u32[]{:S(2)}) copy-start(bf16[128,128]{1,0:T(8,128)(2,1)} %copy-done.26) | copy-start | bytes 98308
  738.8 781.1 %reduce-scatter.15.cloned.1.call-start = ((), (), s32[]{:S(2)}) async-start(), calls=%async_computation.24 | async-start | bytes 3244032 | tf_op jit(solution)/shard_map/reduce_scatter | solution.py:325
  823.2 833.2 %reduce-scatter.19.cloned.1.call-start = ((), (), s32[]{:S(2)}) async-start(), calls=%async_computation.26 | async-start | bytes 1081344 | tf_op jit(solution)/shard_map/reduce_scatter | solution.py:328
  1022.1 767.8 %reduce-scatter.27.cloned.1.call-start = ((), (), s32[]{:S(2)}) async-start(), calls=%async_computation.30 | async-start | bytes 1081344
  1029.0 900.5 %reduce-scatter.21.cloned.1.call-start = ((), (), s32[]{:S(2)}) async-start(), calls=%async_computation.27 | async-start | bytes 4325376 | tf_op jit(solution)/shard_map/reduce_scatter | solution.py:329
  1033.5 1035.8 %reduce-scatter.23.cloned.1.call-start = ((), (), s32[]{:S(2)}) async-start(), calls=%async_computation.28 | async-start | bytes 4325376 | tf_op jit(solution)/shard_map/reduce_scatter | solution.py:330
  1059.0 16.5 copy-start.15
  1059.0 16.5 copy-start.24
  1059.0 16.9 copy-start.22
  1059.0 16.9 copy-start.33
  1059.0 16.9 copy-start.45
  1077.2 13.3 copy-start.19
  1077.2 13.3 copy-start.23
  (37 other events, 135.2 us)
Sparse Core Ops, SparseCore 0:
  9.6 66.1 all-gather.11
  77.3 26.6 all-gather.17
  105.6 80.2 all-gather.21
  187.3 79.2 all-gather.27
  268.3 135.6 all-gather.13
  406.7 54.2 all-gather.15
  462.9 72.3 all-gather.19
  537.2 187.0 all-gather.23
  727.2 63.3 all-gather.25
  792.3 160.5 all-gather.29
  955.8 56.3 all-gather.31
  1014.8 133.6 reduce-scatter.24
  1151.5 130.7 reduce-scatter.16
  1284.9 130.7 reduce-scatter.12
  1422.4 97.4 reduce-scatter.14
  1522.6 133.7 reduce-scatter.18
  1659.1 130.7 reduce-scatter.26
  1792.7 136.7 reduce-scatter.20
  1932.4 136.8 reduce-scatter.22
where the time goes:
time: 2090 us; the launch traced here: 2080 us
  waiting for transfers between devices  1520 us (73%)
  blocking collectives  222 us (11%)
  matrix products  198 us (9%)
  local copies, waits for them, and re-layouts  59.6 us (3%)
  other arithmetic  29.9 us (1%)
  starting transfers between devices  25.5 us (1%)
    unnamed x21, waiting for transfers between devices  194 us
    reduce_scatter x1, waiting for transfers between devices, on_device(): lax.psum_scatter(all_grads[6], ('fsdp', 'seq'), scatter_dimension=0, tile...  140 us
    reduce_scatter x1, waiting for transfers between devices, on_device(): lax.psum_scatter(all_grads[5], ('fsdp', 'seq'), scatter_dimension=0, tile...  140 us
    reduce_scatter x1, waiting for transfers between devices, on_device(): lax.psum_scatter(all_grads[4], ('fsdp', 'seq'), scatter_dimension=0, tile...  137 us
    reduce_scatter x1, waiting for transfers between devices, on_device(): lax.psum_scatter(all_grads[2], ('fsdp', 'seq'), scatter_dimension=0, tile...  134 us
    reduce_scatter x1, waiting for transfers between devices, on_device(): lax.psum_scatter(all_grads[0], ('fsdp', 'seq'), scatter_dimension=0, tile...  133 us
    all_gather x1, waiting for transfers between devices, on_device(): lax.all_gather(frozen_local[3], 'seq', axis=0, tiled=True)  105 us
    reduce_scatter x1, waiting for transfers between devices, on_device(): lax.psum_scatter(all_grads[1], ('fsdp', 'seq'), scatter_dimension=0, tile...  104 us
  transfers between devices with their start and end apart: 23, of which 18 were waited for; matrix products, arithmetic and copies ran while one was open for 14% of the time, Pallas kernels for 0%

commit v1 on v0

v1 whole, which is shorter than its diff:
```python
import jax
import jax.numpy as jnp
from jax import lax
from jax.sharding import PartitionSpec as P

H = 32
HD = 64
ROT = 32
RANK = 16
ADAPT = 8
BLOCK = 256
EPSILON = 1e-05
ADAPTER_SCALE = 2.0
ROPE_BASE = 10000.0
MASKED = -1e30
F32 = jnp.float32
BF16 = jnp.bfloat16


def dot(a, b, dims=((1,), (0,))):
    return lax.dot_general(a, b, (dims, ((), ())), preferred_element_type=F32)


def dot_nt(a, b):
    return dot(a, b, ((1,), (1,)))


def dot_tn(a, b):
    return dot(a, b, ((0,), (0,)))


def norm_layer(values, scale_gain, offset_bias):
    row_mean = jnp.mean(values, axis=-1, keepdims=True)
    centred = values - row_mean
    spread = jnp.mean(centred * centred, axis=-1, keepdims=True)
    return centred * lax.rsqrt(spread + EPSILON) * scale_gain + offset_bias


def rope_tables(length, heads):
    frequency = ROPE_BASE ** (-2.0 * jnp.arange(ROT // 2, dtype=F32) / ROT)
    angles = jnp.arange(length).astype(F32)[:, None] * frequency[None, :]
    return jnp.cos(angles)[:, None, :], jnp.sin(angles)[:, None, :]


def rotate(values, cos_table, sin_table):
    a = values[..., : ROT // 2]
    b = values[..., ROT // 2 : ROT]
    return jnp.concatenate(
        [a * cos_table - b * sin_table, b * cos_table + a * sin_table, values[..., ROT:]], axis=-1
    )


def on_device(
    tokens,
    cotangent,
    adapter_index,
    qkv_weight,
    dense_weight,
    inner_weight,
    outer_weight,
    qkv_bias,
    dense_bias,
    inner_bias,
    outer_bias,
    norm_gain,
    norm_bias,
    *maps,
):
    planes = lax.axis_size("fsdp")
    groups = lax.axis_size("seq")
    rows, width = tokens.shape
    length = rows * groups
    heads = H // groups
    mine = heads * HD
    units = inner_weight.shape[1]
    s = lax.axis_index("seq")

    counts = [m.shape[0] for m in maps]
    stacked = jnp.concatenate(maps, axis=0)
    wanted = (adapter_index[:, None] * RANK + jnp.arange(RANK)[None, :]).reshape(-1)
    pick = (wanted[:, None] == jnp.arange(ADAPT * RANK)[None, :]).astype(BF16)
    chosen = dot_nt(pick, stacked).astype(BF16).reshape(planes, RANK, -1)
    chosen = lax.all_to_all(chosen, "fsdp", split_axis=0, concat_axis=0, tiled=True)
    chosen = lax.all_gather(chosen, "seq", axis=1, tiled=False)
    full = []
    at = 0
    for n in counts:
        part = chosen[:, :, :, at : at + n]
        full.append(part.transpose(2, 0, 1, 3).reshape(RANK, -1))
        at += n
    qkv_down, qkv_up, dense_down, dense_up, inner_down, inner_up, outer_down, outer_up = full

    def own(m, n):
        return lax.dynamic_slice_in_dim(m, s * n, n, axis=1)

    qkv_up = jnp.concatenate(
        [own(qkv_up[:, c * width : (c + 1) * width], mine) for c in range(3)], axis=1
    )
    dense_down = own(dense_down, mine)
    inner_up = own(inner_up, units)
    outer_down = own(outer_down, units)

    wqkv = lax.all_gather(qkv_weight, "fsdp", axis=1, tiled=True)
    wdense = lax.all_gather(dense_weight, "fsdp", axis=1, tiled=True)
    winner = lax.all_gather(inner_weight, "fsdp", axis=0, tiled=True)
    wouter = lax.all_gather(outer_weight, "fsdp", axis=1, tiled=True)

    gain = norm_gain.astype(F32)
    shift = norm_bias.astype(F32)
    source = tokens.astype(F32)
    normed_own = norm_layer(source, gain, shift).astype(BF16)
    normed = lax.all_gather(normed_own, "seq", axis=0, tiled=True)
    cot = lax.all_gather(cotangent, "seq", axis=0, tiled=True)

    coeffs = dot_nt(normed, jnp.concatenate([qkv_down, inner_down], axis=0)).astype(BF16)
    qkv_coeff, inner_coeff = coeffs[:, :RANK], coeffs[:, RANK:]
    cgs = (
        ADAPTER_SCALE * dot_nt(cot, jnp.concatenate([dense_up, outer_up], axis=0))
    ).astype(BF16)
    dense_cg, outer_cg = cgs[:, :RANK], cgs[:, RANK:]

    bias = jnp.stack([own(qkv_bias.reshape(3, width)[c : c + 1], mine)[0] for c in range(3)])
    projected = (
        jnp.concatenate([dot(normed, wqkv[c]) for c in range(3)], axis=1)
        + bias.reshape(-1).astype(F32)
        + ADAPTER_SCALE * dot(qkv_coeff, qkv_up)
    ).reshape(length, 3, heads, HD)
    cos_table, sin_table = rope_tables(length, heads)
    query = rotate(projected[:, 0], cos_table, sin_table).astype(BF16).transpose(1, 0, 2)
    key = rotate(projected[:, 1], cos_table, sin_table).astype(BF16).transpose(1, 0, 2)
    value = projected[:, 2].astype(BF16).transpose(1, 0, 2)
    attended_grad = (dot_nt(cot, wdense) + dot(dense_cg, dense_down)).astype(BF16)
    head_grad = attended_grad.reshape(length, heads, HD).transpose(1, 0, 2)

    scale = HD ** (-0.5)

    def bmm(spec, a, b):
        return jnp.einsum(spec, a, b, preferred_element_type=F32)

    key_grad = jnp.zeros((heads, length, HD), F32)
    value_grad = jnp.zeros((heads, length, HD), F32)
    attended_parts = []
    query_parts = []
    for b in range(length // BLOCK):
        lo, hi = b * BLOCK, (b + 1) * BLOCK
        q = query[:, lo:hi]
        k = key[:, :hi]
        v = value[:, :hi]
        g = head_grad[:, lo:hi]
        scores = bmm("hqd,hkd->hqk", q, k) * scale
        row_max = jnp.max(scores, axis=-1, keepdims=True)
        exponent = jnp.exp(scores - row_max)
        prob = exponent / jnp.sum(exponent, axis=-1, keepdims=True)
        prob_low = prob.astype(BF16)
        attended_parts.append(bmm("hqk,hkd->hqd", prob_low, v).astype(BF16))
        prob_grad = bmm("hqd,hkd->hqk", g, v)
        row_dot = jnp.sum(prob_grad * prob, axis=-1, keepdims=True)
        score_grad = (prob * (prob_grad - row_dot)).astype(BF16)
        query_parts.append((bmm("hqk,hkd->hqd", score_grad, k) * scale).astype(BF16))
        key_grad = key_grad.at[:, :hi].add(bmm("hqk,hqd->hkd", score_grad, q) * scale)
        value_grad = value_grad.at[:, :hi].add(bmm("hqk,hqd->hkd", prob_low, g))

    def rows_first(x):
        return x.transpose(1, 0, 2)

    attended = rows_first(jnp.concatenate(attended_parts, axis=1)).reshape(length, mine)
    query_grad = rows_first(jnp.concatenate(query_parts, axis=1)).astype(F32)
    key_back = rows_first(key_grad.astype(BF16)).astype(F32)
    value_back = rows_first(value_grad.astype(BF16)).reshape(length, mine)
    projected_grad = jnp.concatenate(
        [
            rotate(query_grad, cos_table, -sin_table).astype(BF16).reshape(length, mine),
            rotate(key_back, cos_table, -sin_table).astype(BF16).reshape(length, mine),
            value_back,
        ],
        axis=1,
    )

    pre_act = (
        dot(normed, winner)
        + own(inner_bias[None], units).astype(F32)
        + ADAPTER_SCALE * dot(inner_coeff, inner_up)
    )
    act32, gelu_back = jax.vjp(lambda v: jax.nn.gelu(v, approximate=True), pre_act)
    activated = act32.astype(BF16)
    act_grad = dot_nt(cot, wouter) + dot(outer_cg, outer_down)
    pre_grad = gelu_back(act_grad)[0].astype(BF16)

    def scatter(x):
        return lax.psum_scatter(x, "seq", scatter_dimension=0, tiled=True)

    branch = scatter((dot(attended, wdense) + dot(activated, wouter)))
    coeff_sum = scatter(
        jnp.concatenate([dot_nt(attended, dense_down), dot_nt(activated, outer_down)], axis=1)
    )
    back = dot_nt(pre_grad, winner)
    for c in range(3):
        back = back + dot_nt(projected_grad[:, c * mine : (c + 1) * mine], wqkv[c])
    back = scatter(back)
    cg_sum = scatter(
        ADAPTER_SCALE
        * jnp.concatenate([dot_nt(projected_grad, qkv_up), dot_nt(pre_grad, inner_up)], axis=1)
    )
    late_own = jnp.concatenate([coeff_sum, cg_sum], axis=1).astype(BF16)
    late = lax.all_gather(late_own, "seq", axis=0, tiled=True)

    layer_out = (
        source
        + branch
        + dense_bias.astype(F32)
        + outer_bias.astype(F32)
        + ADAPTER_SCALE
        * dot(late_own[:, : 2 * RANK], jnp.concatenate([dense_up, outer_up], axis=0))
    ).astype(BF16)
    normed_grad = back + dot(
        late_own[:, 2 * RANK :], jnp.concatenate([qkv_down, inner_down], axis=0)
    )
    row_mean = jnp.mean(source, axis=-1, keepdims=True)
    centred = source - row_mean
    inv = lax.rsqrt(jnp.mean(centred * centred, axis=-1, keepdims=True) + EPSILON)
    xhat = centred * inv
    e = normed_grad * gain
    input_grad = cotangent.astype(F32) + inv * (
        e
        - jnp.mean(e, axis=-1, keepdims=True)
        - xhat * jnp.mean(e * xhat, axis=-1, keepdims=True)
    )

    share = width // groups
    cot_mine = own(cot, share)
    normed_mine = own(normed, share)
    qkv_up_g = ADAPTER_SCALE * dot_tn(qkv_coeff, projected_grad)
    inner_up_g = ADAPTER_SCALE * dot_tn(inner_coeff, pre_grad)
    dense_down_g = dot_tn(dense_cg, attended)
    outer_down_g = dot_tn(outer_cg, activated)
    ups = ADAPTER_SCALE * dot_tn(late[:, : 2 * RANK], cot_mine)
    downs = dot_tn(late[:, 2 * RANK :], normed_mine)
    mine_grads = [
        downs[:RANK],
        qkv_up_g,
        dense_down_g,
        ups[:RANK],
        downs[RANK:],
        inner_up_g,
        outer_down_g,
        ups[RANK:],
    ]
    packed = jnp.concatenate(mine_grads, axis=1)
    everyone = lax.all_gather(packed, "seq", axis=0, tiled=False)
    owned = []
    at = 0
    for i, (n, g) in enumerate(zip(counts, mine_grads)):
        w = g.shape[1]
        part = everyone[:, :, at : at + w]
        at += w
        blocks = 3 if i == 1 else 1
        part = part.reshape(groups, RANK, blocks, w // blocks).transpose(1, 2, 0, 3)
        part = part.reshape(RANK, planes, groups, n)
        owned.append(lax.dynamic_index_in_dim(part, s, 2, keepdims=False))
    owned = jnp.concatenate(owned, axis=2).transpose(1, 0, 2)
    arrived = lax.all_to_all(owned, "fsdp", split_axis=0, concat_axis=0, tiled=True)
    place = pick.astype(F32).reshape(planes * RANK, ADAPT * RANK)
    spread = lax.dot_general(
        arrived.reshape(planes * RANK, -1),
        place,
        (((0,), (0,)), ((), ())),
        precision=lax.Precision.HIGHEST,
        preferred_element_type=F32,
    )
    outs = []
    at = 0
    for n in counts:
        outs.append(spread[at : at + n])
        at += n
    return (layer_out, input_grad, *outs)


def solution(mesh):
    both = P(("fsdp", "seq"), None)
    placed = (
        both,
        both,
        P(),
        P(None, "fsdp", "seq"),
        P("seq", "fsdp"),
        P("fsdp", "seq"),
        P("seq", "fsdp"),
    ) + (P(),) * 6 + (both,) * 8
    return jax.shard_map(
        on_device, mesh=mesh, in_specs=placed, out_specs=(both,) * 10, check_vma=False
    )
```

time: 2090 us -> 689 us (0.33)
  waiting for transfers between devices: 1520 us -> 434 us
  blocking collectives: 222 us -> 21.3 us
  matrix products: 198 us -> 142 us
  local copies, waits for them, and re-layouts: 59.6 us -> 35.6 us
    reduce_scatter x6 -> x4, waiting for transfers between devices: 787 us -> 178 us  [scatter(): return lax.psum_scatter(x, 'seq', scatter_dimension=0, tiled=True)]
    all_gather x11 -> x8, waiting for transfers between devices: 492 us -> 244 us  [the longest x1 57 us: on_device(): wqkv = lax.all_gather(qkv_weight, 'fsdp', axis=1, tiled=True)]
    all_gather x5 -> x1, blocking collectives: 222 us -> 9.02 us  [on_device(): late = lax.all_gather(late_own, 'seq', axis=0, tiled=True)]
    unnamed x21 -> x12, waiting for transfers between devices: 194 us -> 3.09 us
    dot_general x46 -> x53, matrix products: 198 us -> 135 us  [the longest x31 91.8 us: dot(): return lax.dot_general(a, b, (dims, ((), ())), preferred_element_type=F32)]
    all_to_all x4 -> x1, waiting for transfers between devices: 44.9 us -> 9.49 us  [on_device(): lax.all_to_all(owned, 'fsdp', split_axis=0, concat_axis=0, tiled=True)]
  transfers between devices with their start and end apart: 23 -> 13, of which waited for: 18 -> 12; matrix products, arithmetic and copies ran while one was open for 14% -> 23% of each run, Pallas kernels for 0% -> 0%
where the time goes in v1:
time: 689 us; the launch traced here: 678 us
  waiting for transfers between devices  434 us (63%)
  matrix products  142 us (21%)
  local copies, waits for them, and re-layouts  35.6 us (5%)
  other arithmetic  23.7 us (3%)
  blocking collectives  21.3 us (3%)
  between operations  16.1 us (2%)
    reduce_scatter x4, waiting for transfers between devices, scatter(): return lax.psum_scatter(x, 'seq', scatter_dimension=0, tiled=True)  178 us
    dot_general x31, matrix products, dot(): return lax.dot_general(a, b, (dims, ((), ())), preferred_element_type=F32)  91.8 us
    all_gather x1, waiting for transfers between devices, on_device(): wqkv = lax.all_gather(qkv_weight, 'fsdp', axis=1, tiled=True)  57 us
    all_gather x1, waiting for transfers between devices, on_device(): wouter = lax.all_gather(outer_weight, 'fsdp', axis=1, tiled=True)  53.9 us
    dot_general x21, matrix products, bmm(): return jnp.einsum(spec, a, b, preferred_element_type=F32)  42.3 us
    all_gather x1, waiting for transfers between devices, on_device(): normed = lax.all_gather(normed_own, 'seq', axis=0, tiled=True)  37.9 us
    all_gather x1, waiting for transfers between devices, on_device(): winner = lax.all_gather(inner_weight, 'fsdp', axis=0, tiled=True)  32.4 us
    all_gather x1, waiting for transfers between devices, on_device(): cot = lax.all_gather(cotangent, 'seq', axis=0, tiled=True)  26 us
  transfers between devices with their start and end apart: 13, of which 12 were waited for; matrix products, arithmetic and copies ran while one was open for 23% of the time, Pallas kernels for 0%

profile of v1, /device:TPU:0, one launch (start us, length us, event | category | flops | bytes accessed | tf_op | source)
XLA Modules:
  0.0 678.0 jit_solution(5243107930825763967)
XLA Ops:
  14.5 12.3 %all_to_all.10 = bf16[4,16,1024]{2,1,0:T(8,128)(2,1)} all-to-all(bf16[4,16,1024]{2,1,0:T(8,128)(2,1)S(1)} %bitcast.265), channel_id=1, replica_groups=mesh['fsdp'=4,'seq'=8] {'fsdp'}, dimensions={0} | all-to-all | bytes 262144 | tf_op jit(solution)/shard_map/all_to_all | solution.py:83
  39.0 10.6 %all-gather.23.cloned.1.call-done = bf16[4,128,1024]{2,1,0:T(8,128)(2,1)} async-done(((bf16[4,16,1024]{2,1,0:T(8,128)(2,1)}), bf16[4,128,1024]{2,1,0:T(8,128)(2,1)}) %all-gather.23.cloned.1.call-update) | async-done | bytes 1048592 | tf_op jit(solution)/shard_map/all_gather | solution.py:84
  57.6 57.0 %all-gather.13.cloned.1.call-done = bf16[3,2048,256]{2,1,0:T(8,128)(2,1)} async-done(((bf16[3,512,256]{2,1,0:T(8,128)(2,1)}), bf16[3,2048,256]{2,1,0:T(8,128)(2,1)}) %all-gather.13.cloned.1.call-update) | async-done | bytes 3145744 | tf_op jit(solution)/shard_map/all_gather | solution.py:103
  114.6 37.9 %all-gather.11.cloned.1.call-done = bf16[1024,2048]{1,0:T(8,128)(2,1)} async-done(((bf16[128,2048]{1,0:T(8,128)(2,1)}), bf16[1024,2048]{1,0:T(8,128)(2,1)}) %all-gather.11.cloned.1.call-update) | async-done | bytes 4194320 | tf_op jit(solution)/shard_map/all_gather | solution.py:112
  152.5 3.9 fusion.67
  165.0 26.0 %all-gather.21.cloned.1.call-done = bf16[1024,2048]{1,0:T(8,128)(2,1)} async-done(((bf16[128,2048]{1,0:T(8,128)(2,1)}), bf16[1024,2048]{1,0:T(8,128)(2,1)}) %all-gather.21.cloned.1.call-update) | async-done | bytes 4194320 | tf_op jit(solution)/shard_map/all_gather | solution.py:113
  191.0 3.5 fusion.48
  194.6 25.8 %all-gather.15.cloned.1.call-done = bf16[256,2048]{1,0:T(8,128)(2,1)} async-done(((bf16[256,512]{1,0:T(8,128)(2,1)}), bf16[256,2048]{1,0:T(8,128)(2,1)}) %all-gather.15.cloned.1.call-update) | async-done | bytes 1048592 | tf_op jit(solution)/shard_map/all_gather | solution.py:104
  220.4 3.8 fusion.256
  228.9 2.7 fusion.240
  231.6 1.7 fusion.83
  235.6 2.8 convolution_convert_fusion.2
  238.4 3.1 fusion.40
  241.4 3.6 multiply_reduce_fusion.4
  245.1 2.3 fusion.239
  247.3 3.7 convolution_convert_fusion.4
  251.1 3.7 multiply_convert_fusion.3
  254.7 2.4 convolution_convert_fusion
  257.1 2.3 fusion.46
  259.5 4.2 fusion.32
  263.6 3.0 multiply_reduce_fusion.2
  269.7 32.4 %all-gather.17.cloned.1.call-done = bf16[2048,1024]{1,0:T(8,128)(2,1)} async-done(((bf16[512,1024]{1,0:T(8,128)(2,1)}), bf16[2048,1024]{1,0:T(8,128)(2,1)}) %all-gather.17.cloned.1.call-update) | async-done | bytes 4194320 | tf_op jit(solution)/shard_map/all_gather | solution.py:105
  302.1 7.7 %fusion.252 = f32[1024,1024]{1,0:T(8,128)S(1)} fusion(bf16[1024,2048]{1,0:T(8,128)(2,1)} %all-gather.11.cloned.1.call-done, bf16[2048,1024]{1,0:T(8,128)(2,1)} %all-gather.17.cloned.1.call-done), kind=kOutput, calls=%fused_computation.309 | convolution fusion | flops 4294967296 | bytes 12582912 | tf_op jit(solution)/shard_map/dot_general | solution.py:21
  309.9 4.9 multiply_convert_fusion.1
  317.5 3.4 fusion.234
  320.9 4.2 convolution_convert_fusion.1
  325.0 4.1 multiply_reduce_fusion
  329.1 53.9 %all-gather.19.cloned.1.call-done = bf16[1024,2048]{1,0:T(8,128)(2,1)} async-done(((bf16[1024,512]{1,0:T(8,128)(2,1)}), bf16[1024,2048]{1,0:T(8,128)(2,1)}) %all-gather.19.cloned.1.call-update) | async-done | bytes 4194320 | tf_op jit(solution)/shard_map/all_gather | solution.py:106
  383.0 7.7 %fusion.254 = f32[1024,1024]{1,0:T(8,128)S(1)} fusion(bf16[1024,2048]{1,0:T(8,128)(2,1)} %all-gather.21.cloned.1.call-done, bf16[1024,2048]{1,0:T(8,128)(2,1)} %all-gather.19.cloned.1.call-done), kind=kOutput, calls=%fused_computation.311 | convolution fusion | flops 4294967296 | bytes 12582912 | tf_op jit(solution)/shard_map/dot_general | solution.py:21
  390.8 4.4 fusion.10
  399.6 4.1 multiply_convert_fusion
  407.8 23.8 %reduce-scatter.7.cloned.1.call-done = f32[128,32]{0,1:T(8,128)} async-done(((f32[1024,32]{0,1:T(8,128)}), f32[128,32]{0,1:T(8,128)}) %reduce-scatter.7.cloned.1.call-update) | async-done | bytes 16400 | tf_op jit(solution)/shard_map/reduce_scatter | solution.py:190
  432.3 36.5 %reduce-scatter.11.cloned.1.call-done = f32[128,32]{0,1:T(8,128)} async-done(((f32[1024,32]{0,1:T(8,128)}), f32[128,32]{0,1:T(8,128)}) %reduce-scatter.11.cloned.1.call-update) | async-done | bytes 16400 | tf_op jit(solution)/shard_map/reduce_scatter | solution.py:190
  469.5 9.0 %all_gather.41 = bf16[1024,64]{0,1:T(8,128)(2,1)S(1)} all-gather(bf16[128,64]{0,1:T(8,128)(2,1)S(1)} %pad_maximum_fusion.6), channel_id=1, replica_groups=mesh['fsdp'=4,'seq'=8] {'seq'}, dimensions={0}, use_global_device_ids=true | all-gather | bytes 147456 | tf_op jit(solution)/shard_map/all_gather | solution.py:205
  480.4 2.5 fusion.50
  486.2 2.6 fusion.49
  490.5 2.6 fusion.63
  493.1 2.7 fusion.65
  496.3 6.7 fusion.255
  503.0 9.0 %add_add_fusion = f32[1024,2048]{1,0:T(8,128)} fusion(f32[1024,2048]{1,0:T(8,128)S(1)} %fusion.65, f32[1024,2048]{1,0:T(8,128)} %fusion.255, f32[1024,2048]{1,0:T(8,128)S(1)} %fusion.63, bf16[1024,256]{0,1:T(8,128)(2,1)} %bitcast.252, bf16[3,2048,256]{2,1,0:T(8,128)(2,1)} %all-gather.13.cloned.1.call-done), kind=kOutput, calls=%fused_computation.4 | convolution fusion | flops 1080033280 | bytes 35127296 | tf_op jit(solution)/shard_map/dot_general | solution.py:21
  512.1 6.6 fusion.253
  518.7 4.6 convolution_add_fusion
  530.7 4.5 all-to-all-start.1
  535.2 9.5 %all-to-all-done.1 = f32[4,16,1024]{2,1,0:T(8,128)S(1)} async-done(((f32[4,16,1024]{2,1,0:T(8,128)}), f32[4,16,1024]{2,1,0:T(8,128)S(1)}, u32[]{:S(2)}, u32[]{:S(2)}) %all-to-all-start.1) | async-done | bytes 262176 | tf_op jit(solution)/shard_map/all_to_all | solution.py:261
  547.3 46.0 %reduce-scatter.9.cloned.1.call-done = f32[128,2048]{1,0:T(8,128)} async-done(((f32[1024,2048]{1,0:T(8,128)}), f32[128,2048]{1,0:T(8,128)}) %reduce-scatter.9.cloned.1.call-update) | async-done | bytes 1048592 | tf_op jit(solution)/shard_map/reduce_scatter | solution.py:190
  593.3 1.7 fusion.227
  596.5 71.8 %reduce-scatter.5.cloned.1.call-done = f32[128,2048]{1,0:T(8,128)} async-done(((f32[1024,2048]{1,0:T(8,128)}), f32[128,2048]{1,0:T(8,128)}) %reduce-scatter.5.cloned.1.call-update) | async-done | bytes 1048592 | tf_op jit(solution)/shard_map/reduce_scatter | solution.py:190
  668.3 2.4 fusion.20
  (326 shorter events, 76.3 us)
Async XLA Ops:
  7.2 24.9 %copy-start = (bf16[128,2048]{1,0:T(8,128)(2,1)S(1)}, bf16[128,2048]{1,0:T(8,128)(2,1)}, u32[]{:S(2)}) copy-start(bf16[128,2048]{1,0:T(8,128)(2,1)} %param.41) | copy-start | bytes 1572868
  7.2 42.4 %all-gather.23.cloned.1.call-start = ((), (), s32[]{:S(2)}) async-start(), calls=%async_computation.16 | async-start | bytes 1179648 | tf_op jit(solution)/shard_map/all_gather | solution.py:84
  8.1 18.7 %copy-start.62 = (s32[64]{0:T(128)}, s32[64]{0:T(128)S(1)}, u32[]{:S(2)}) copy-start(s32[64]{0:T(128)S(1)} %add.230) | copy-start | bytes 772
  26.8 9.1 %copy-start.59 = (bf16[6144]{0:T(1024)(128)(2,1)S(1)}, bf16[6144]{0:T(1024)(128)(2,1)}, u32[]{:S(2)}) copy-start(bf16[6144]{0:T(1024)(128)(2,1)} %param.48) | copy-start | bytes 36868
  26.8 87.8 %all-gather.13.cloned.1.call-start = ((), (), s32[]{:S(2)}) async-start(), calls=%async_computation.7 | async-start | bytes 3932160 | tf_op jit(solution)/shard_map/all_gather | solution.py:103
  27.6 125.0 %all-gather.11.cloned.1.call-start = ((), (), s32[]{:S(2)}) async-start(), calls=%async_computation.6 | async-start | bytes 4718592 | tf_op jit(solution)/shard_map/all_gather | solution.py:112
  33.3 157.7 %all-gather.21.cloned.1.call-start = ((), (), s32[]{:S(2)}) async-start(), calls=%async_computation.13 | async-start | bytes 4718592 | tf_op jit(solution)/shard_map/all_gather | solution.py:113
  33.9 186.5 %all-gather.15.cloned.1.call-start = ((), (), s32[]{:S(2)}) async-start(), calls=%async_computation.8 | async-start | bytes 1310720 | tf_op jit(solution)/shard_map/all_gather | solution.py:104
  34.5 267.6 %all-gather.17.cloned.1.call-start = ((), (), s32[]{:S(2)}) async-start(), calls=%async_computation.9 | async-start | bytes 5242880 | tf_op jit(solution)/shard_map/all_gather | solution.py:105
  35.1 348.0 %all-gather.19.cloned.1.call-start = ((), (), s32[]{:S(2)}) async-start(), calls=%async_computation.10 | async-start | bytes 5242880 | tf_op jit(solution)/shard_map/all_gather | solution.py:106
  35.8 395.7 %reduce-scatter.7.cloned.1.call-start = ((), (), s32[]{:S(2)}) async-start(), calls=%async_computation.12 | async-start | bytes 147456 | tf_op jit(solution)/shard_map/reduce_scatter | solution.py:190
  57.6 133.4 %copy-start.28 = (bf16[32,2048]{1,0:T(8,128)(2,1)}, bf16[32,2048]{1,0:T(8,128)(2,1)S(1)}, u32[]{:S(2)}) copy-start(bf16[32,2048]{1,0:T(8,128)(2,1)S(1)} %constant_dynamic-update-slice_fusion.10) | copy-start | bytes 393220
  57.6 101.5 %copy-start.30 = (bf16[32,2048]{1,0:T(8,128)(2,1)}, bf16[32,2048]{1,0:T(8,128)(2,1)S(1)}, u32[]{:S(2)}) copy-start(bf16[32,2048]{1,0:T(8,128)(2,1)S(1)} %constant_dynamic-update-slice_fusion.8) | copy-start | bytes 393220
  114.6 41.8 %copy-start.15 = (bf16[3,2048,256]{2,1,0:T(8,128)(2,1)S(1)}, bf16[3,2048,256]{2,1,0:T(8,128)(2,1)}, u32[]{:S(2)}) copy-start(bf16[3,2048,256]{2,1,0:T(8,128)(2,1)} %all-gather.13.cloned.1.call-done) | copy-start | bytes 9437188
  162.8 63.9 %copy-start.35 = (bf16[4,1024,64]{1,2,0:T(8,128)(2,1)}, bf16[4,1024,64]{1,2,0:T(8,128)(2,1)S(1)}, u32[]{:S(2)}) copy-start(bf16[4,1024,64]{1,2,0:T(8,128)(2,1)S(1)} %fusion.71) | copy-start | bytes 1572868
  163.2 31.4 %copy-start.37 = (bf16[1024,4,16]{0,2,1:T(8,128)(2,1)}, bf16[1024,4,16]{0,2,1:T(8,128)(2,1)S(1)}, u32[]{:S(2)}) copy-start(bf16[1024,4,16]{0,2,1:T(8,128)(2,1)S(1)} %get-tuple-element.137) | copy-start | bytes 393220
  163.3 65.6 %copy-start.18 = (bf16[4,1024,64]{1,2,0:T(8,128)(2,1)}, bf16[4,1024,64]{1,2,0:T(8,128)(2,1)S(1)}, u32[]{:S(2)}) copy-start(bf16[4,1024,64]{1,2,0:T(8,128)(2,1)S(1)} %maximum_bitcast_fusion) | copy-start | bytes 1572868
  163.9 65.0 %copy-start.21 = (bf16[4,1024,64]{1,2,0:T(8,128)(2,1)}, bf16[4,1024,64]{1,2,0:T(8,128)(2,1)S(1)}, u32[]{:S(2)}) copy-start(bf16[4,1024,64]{1,2,0:T(8,128)(2,1)S(1)} %maximum_bitcast_fusion.1) | copy-start | bytes 1572868
  194.6 196.2 %copy-start.41 = (bf16[1024,32]{0,1:T(8,128)(2,1)}, bf16[1024,32]{0,1:T(8,128)(2,1)S(1)}, u32[]{:S(2)}) copy-start(bf16[1024,32]{0,1:T(8,128)(2,1)S(1)} %fusion.48) | copy-start | bytes 196612
  194.6 30.7 %copy-start.66 = (f32[4,256]{1,0:T(4,128)S(1)}, f32[4,256]{1,0:T(4,128)}, u32[]{:S(2)}) copy-start(f32[4,256]{1,0:T(4,128)} %get-tuple-element.176) | copy-start | bytes 12292
  269.7 40.1 %copy-start.44 = (bf16[1024,32]{0,1:T(8,128)(2,1)S(1)}, bf16[1024,32]{0,1:T(8,128)(2,1)}, u32[]{:S(2)}) copy-start(bf16[1024,32]{0,1:T(8,128)(2,1)} %copy-done.43) | copy-start | bytes 196612
  269.7 40.1 %copy-start.71 = (f32[1024]{0:T(1024)S(1)}, f32[1024]{0:T(1024)}, u32[]{:S(2)}) copy-start(f32[1024]{0:T(1024)} %dynamic-slice_convert_fusion) | copy-start | bytes 12292
  309.8 6.5 copy-start.3
  309.8 6.5 copy-start.12
  309.8 6.5 copy-start.19
  383.0 7.7 %copy-start.73 = (f32[1024,1024]{1,0:T(8,128)S(1)}, f32[1024,1024]{1,0:T(8,128)}, u32[]{:S(2)}) copy-start(f32[1024,1024]{1,0:T(8,128)} %get-tuple-element.169) | copy-start | bytes 12582916
  390.8 5.9 copy-start.14
  390.8 5.9 copy-start.25
  397.8 8.1 %copy-start.32 = (bf16[4,1024,64]{1,2,0:T(8,128)(2,1)}, bf16[4,1024,64]{1,2,0:T(8,128)(2,1)S(1)}, u32[]{:S(2)}) copy-start(bf16[4,1024,64]{1,2,0:T(8,128)(2,1)S(1)} %fusion.28) | copy-start | bytes 1572868
  399.5 69.3 %reduce-scatter.11.cloned.1.call-start = ((), (), s32[]{:S(2)}) async-start(), calls=%async_computation.15 | async-start | bytes 147456 | tf_op jit(solution)/shard_map/reduce_scatter | solution.py:190
  405.8 74.6 %copy-start.45 = (bf16[1024,32]{0,1:T(8,128)(2,1)S(1)}, bf16[1024,32]{0,1:T(8,128)(2,1)}, u32[]{:S(2)}) copy-start(bf16[1024,32]{0,1:T(8,128)(2,1)} %copy-done.43) | copy-start | bytes 196612
  407.0 75.9 %copy-start.42 = (bf16[1024,32]{0,1:T(8,128)(2,1)S(1)}, bf16[1024,32]{0,1:T(8,128)(2,1)}, u32[]{:S(2)}) copy-start(bf16[1024,32]{0,1:T(8,128)(2,1)} %copy-done.41) | copy-start | bytes 196612
  407.7 115.7 %all-gather.25.cloned.1.call-start = ((), (), s32[]{:S(2)}) async-start(), calls=%async_computation.17 | async-start | bytes 2359296 | tf_op jit(solution)/shard_map/all_gather | solution.py:249
  480.4 8.4 %copy-start.6 = (bf16[1024,1024]{1,0:T(8,128)(2,1)S(1)}, bf16[1024,1024]{1,0:T(8,128)(2,1)}, u32[]{:S(2)}) copy-start(bf16[1024,1024]{1,0:T(8,128)(2,1)} %copy-done.5) | copy-start | bytes 6291460
  490.5 102.9 %reduce-scatter.9.cloned.1.call-start = ((), (), s32[]{:S(2)}) async-start(), calls=%async_computation.14 | async-start | bytes 9437184 | tf_op jit(solution)/shard_map/reduce_scatter | solution.py:190
  512.0 156.3 %reduce-scatter.5.cloned.1.call-start = ((), (), s32[]{:S(2)}) async-start(), calls=%async_computation.11 | async-start | bytes 9437184 | tf_op jit(solution)/shard_map/reduce_scatter | solution.py:190
  512.1 6.6 copy-start.24
  528.3 6.8 %copy-start.69 = (bf16[2048]{0:T(1024)(128)(2,1)S(1)}, bf16[2048]{0:T(1024)(128)(2,1)}, u32[]{:S(2)}) copy-start(bf16[2048]{0:T(1024)(128)(2,1)} %param.49) | copy-start | bytes 12292
  528.3 6.8 %copy-start.70 = (bf16[2048]{0:T(1024)(128)(2,1)S(1)}, bf16[2048]{0:T(1024)(128)(2,1)}, u32[]{:S(2)}) copy-start(bf16[2048]{0:T(1024)(128)(2,1)} %param.51) | copy-start | bytes 12292
  528.4 16.3 %copy-start.63 = (s32[64]{0:T(128)S(1)}, s32[64]{0:T(128)}, u32[]{:S(2)}) copy-start(s32[64]{0:T(128)} %copy-done.62) | copy-start | bytes 772
  528.9 64.4 %copy-start.1 = (bf16[128,2048]{1,0:T(8,128)(2,1)S(1)}, bf16[128,2048]{1,0:T(8,128)(2,1)}, u32[]{:S(2)}) copy-start(bf16[128,2048]{1,0:T(8,128)(2,1)} %param.41) | copy-start | bytes 1572868
  529.0 64.4 %copy-start.31 = (bf16[32,2048]{1,0:T(8,128)(2,1)S(1)}, bf16[32,2048]{1,0:T(8,128)(2,1)}, u32[]{:S(2)}) copy-start(bf16[32,2048]{1,0:T(8,128)(2,1)} %copy-done.30) | copy-start | bytes 393220
  529.0 64.3 %copy-start.55 = (f32[2048]{0:T(1024)S(1)}, f32[2048]{0:T(1024)}, u32[]{:S(2)}) copy-start(f32[2048]{0:T(1024)} %copy-done.54) | copy-start | bytes 24580
  529.0 64.3 %copy-start.61 = (f32[128]{0:T(128)S(1)}, f32[128]{0:T(128)}, u32[]{:S(2)}) copy-start(f32[128]{0:T(128)} %copy-done.60) | copy-start | bytes 1540
  529.0 64.3 %copy-start.65 = (f32[128]{0:T(128)S(1)}, f32[128]{0:T(128)}, u32[]{:S(2)}) copy-start(f32[128]{0:T(128)} %copy-done.64) | copy-start | bytes 1540
  529.8 65.3 %copy-start.23 = (bf16[128,2048]{1,0:T(8,128)(2,1)S(1)}, bf16[128,2048]{1,0:T(8,128)(2,1)}, u32[]{:S(2)}) copy-start(bf16[128,2048]{1,0:T(8,128)(2,1)} %param.42) | copy-start | bytes 1572868
  530.7 14.0 %all-to-all-start.1 = ((f32[4,16,1024]{2,1,0:T(8,128)}), f32[4,16,1024]{2,1,0:T(8,128)S(1)}, u32[]{:S(2)}, u32[]{:S(2)}) async-start(f32[4,16,1024]{2,1,0:T(8,128)} %bitcast.59), calls=%async_computation.5 | async-start | bytes 524288 | tf_op jit(solution)/shard_map/all_to_all | solution.py:261
  546.6 121.7 %copy-start.29 = (bf16[32,2048]{1,0:T(8,128)(2,1)S(1)}, bf16[32,2048]{1,0:T(8,128)(2,1)}, u32[]{:S(2)}) copy-start(bf16[32,2048]{1,0:T(8,128)(2,1)} %copy-done.28) | copy-start | bytes 393220
  (39 other events, 69.7 us)
Sparse Core Ops, SparseCore 0:
  26.9 22.6 all-gather.22
  51.1 63.4 all-gather.12
  117.1 35.3 all-gather.10
  154.3 36.7 all-gather.20
  192.5 27.9 all-gather.14
  221.8 80.2 all-gather.16
  303.7 79.2 all-gather.18
  399.6 31.8 reduce-scatter.6
  435.4 33.3 reduce-scatter.10
  490.6 27.9 all-gather.24
  522.0 71.2 reduce-scatter.8
  597.0 71.2 reduce-scatter.4

commit v2 on v1

--- a/solution.py
+++ b/solution.py
@@ -1,6 +1,11 @@
+import functools
+
 import jax
 import jax.numpy as jnp
+import numpy as np
 from jax import lax
+from jax.experimental import pallas as pl
+from jax.experimental.pallas import tpu as pltpu
 from jax.sharding import PartitionSpec as P
 
 H = 32
@@ -48,6 +53,775 @@
     return jnp.concatenate(
         [a * cos_table - b * sin_table, b * cos_table + a * sin_table, values[..., ROT:]], axis=-1
     )
+
+
+MESH = pl.DeviceIdType.MESH
+TILE = 256
+UNIT = 256
+
+
+def rope_constants(length):
+    frequency = ROPE_BASE ** (-2.0 * np.arange(ROT // 2, dtype=np.float64) / ROT)
+    angles = np.arange(length, dtype=np.float64)[:, None] * frequency[None, :]
+    cos = np.ones((length, HD))
+    sin = np.zeros((length, HD))
+    half = ROT // 2
+    cos[:, :half] = np.cos(angles)
+    cos[:, half:ROT] = np.cos(angles)
+    sin[:, :half] = -np.sin(angles)
+    sin[:, half:ROT] = np.sin(angles)
+    return (
+        jnp.asarray(np.tile(cos, (1, 2)), F32),
+        jnp.asarray(np.tile(sin, (1, 2)), F32),
+    )
+
+
+def turn(x, cos, sin, sign):
+    lane = lax.broadcasted_iota(jnp.int32, x.shape, 1) % HD
+    partner = jnp.where(
+        lane < ROT // 2,
+        pltpu.roll(x, x.shape[1] - ROT // 2, 1),
+        pltpu.roll(x, ROT // 2, 1),
+    )
+    return x * cos + partner * (sin * sign)
+
+
+def turn_all(x, cos, sin, sign):
+    step = cos.shape[1]
+    return jnp.concatenate(
+        [turn(x[:, i : i + step], cos, sin, sign) for i in range(0, x.shape[1], step)], axis=1
+    )
+
+
+def layer_kernel(
+    planes,
+    tok_ref,
+    cotown_ref,
+    wq_in,
+    wd_in,
+    wi_in,
+    wo_in,
+    qb_ref,
+    db_ref,
+    ib_ref,
+    ob_ref,
+    gain_ref,
+    shift_ref,
+    downs_ref,
+    ups_ref,
+    qup_ref,
+    ddown_ref,
+    iup_ref,
+    odown_ref,
+    cos_ref,
+    sin_ref,
+    out_ref,
+    igrad_ref,
+    packed_ref,
+    normed,
+    cot,
+    wq,
+    wd,
+    wi,
+    wo,
+    qkv,
+    hg,
+    att,
+    dk,
+    dv,
+    pg,
+    acc_a,
+    acc_b,
+    pre,
+    act,
+    ag,
+    pgrad,
+    coeff,
+    cgs,
+    coeff_t,
+    cgs_t,
+    res,
+    keep,
+    s1_send,
+    s1_recv,
+    a_send,
+    a_recv,
+    c_send,
+    c_recv,
+    ar_send,
+    ar_recv,
+    local_sem,
+    zs_sem,
+    zr_sem,
+    ag_ssem,
+    ag_rsem,
+    s1_ssem,
+    s1_rsem,
+    a_ssem,
+    a_rsem,
+    c_ssem,
+    c_rsem,
+    ar_ssem,
+    ar_rsem,
+):
+    z = lax.axis_index("fsdp")
+    s = lax.axis_index("seq")
+    core = s % 2
+    chip = s // 2
+    to_core = (z, chip * 2 + (1 - core))
+    chip_x = chip + 1 - 2 * (chip % 2)
+    chip_y = (chip + 2) % 4
+    chip_d = chip_x + 2 - 4 * (chip_x // 2)
+    to_x = (z, chip_x * 2 + core)
+    to_y = (z, chip_y * 2 + core)
+    rows, width = tok_ref.shape
+    length = normed.shape[0]
+    units = act.shape[1]
+    fan = width // planes
+    mine = wq.shape[3]
+    tiles = length // TILE
+
+    def remote(src, dst, ssem, rsem, where):
+        return pltpu.make_async_remote_copy(
+            src_ref=src, dst_ref=dst, send_sem=ssem, recv_sem=rsem, device_id=where,
+            device_id_type=MESH,
+        )
+
+    def block(i, n):
+        return pl.ds(pl.multiple_of(i * n, n), n)
+
+    bar = pltpu.get_barrier_semaphore()
+    for where in (to_core, to_x, to_y):
+        pl.semaphore_signal(bar, inc=1, device_id=where, device_id_type=MESH)
+
+    @pl.when(z > 0)
+    def _():
+        pl.semaphore_signal(bar, inc=1, device_id=(z - 1, s), device_id_type=MESH)
+
+    @pl.when(z < planes - 1)
+    def _():
+        pl.semaphore_signal(bar, inc=1, device_id=(z + 1, s), device_id_type=MESH)
+
+    above = jnp.where(z < planes - 1, 1, 0)
+    pl.semaphore_wait(bar, 3 + above + jnp.where(z > 0, 1, 0))
+
+    chunks = []
+    for c in range(3):
+        chunks.append((wq_in.at[c], lambda j, c=c: wq.at[j, c]))
+    chunks.append((wd_in, lambda j: wd.at[j]))
+    part = fan // 4
+    for i in range(4):
+        chunks.append(
+            (
+                wi_in.at[pl.ds(i * part, part), :],
+                lambda j, i=i: wi.at[j, pl.ds(i * part, part), :],
+            )
+        )
+    deep = units // 2
+    for j2 in range(fan // UNIT):
+        for i in range(2):
+            chunks.append(
+                (
+                    wo_in.at[pl.ds(i * deep, deep), pl.ds(j2 * UNIT, UNIT)],
+                    lambda j, i=i, j2=j2: wo.at[
+                        j, pl.ds(i * deep, deep), pl.ds(j2 * UNIT, UNIT)
+                    ],
+                )
+            )
+    n_chunks = len(chunks)
+    last_step = n_chunks + planes - 1
+
+    def zcopy(c, direction, k):
+        src, place = chunks[c]
+        j = z - k if direction == 0 else z + k
+        return remote(
+            src if k == 0 else place(j),
+            place(j),
+            zs_sem.at[c, direction, k],
+            zr_sem.at[c, j],
+            (z + 1, s) if direction == 0 else (z - 1, s),
+        )
+
+    def zhas(direction, k):
+        if direction == 0:
+            return jnp.logical_and(z - k >= 0, z + 1 < planes)
+        return jnp.logical_and(z + k < planes, z - 1 >= 0)
+
+    def zsend(c, k):
+        for direction in (0, 1):
+
+            @pl.when(zhas(direction, k))
+            def _(direction=direction):
+                zcopy(c, direction, k).start()
+
+    def zwait(c, k):
+        for direction in (0, 1):
+            j = z - k if direction == 0 else z + k
+            there = z - k >= 0 if direction == 0 else z + k < planes
+
+            @pl.when(there)
+            def _(j=j, direction=direction):
+                place = chunks[c][1](j)
+                pltpu.make_async_copy(place, place, zr_sem.at[c, j]).wait()
+
+    def zstep(t):
+        if t == 0:
+            zsend(0, 0)
+            zsend(1, 0)
+        elif t + 1 < n_chunks:
+            zsend(t + 1, 0)
+        for k in range(1, planes):
+            c = t - k
+            if 0 <= c < n_chunks:
+                zwait(c, k)
+                if k < planes - 1:
+                    zsend(c, k)
+
+    own = []
+    for c in range(n_chunks):
+        src, place = chunks[c]
+        own.append(pltpu.make_async_copy(src, place(z), local_sem.at[c]))
+    for copy in own:
+        copy.start()
+
+    zstep(0)
+
+    half = width // 2
+
+    def gather_copies(p, buf):
+        me = buf.at[block(s, rows), :]
+        bx = chip_x * 2 + core
+        by = chip_y * 2 + core
+        bd = chip_d * 2 + core
+        blk_x = buf.at[block(bx, rows), :]
+        blk_y = buf.at[block(by, rows), :]
+        blk_d = buf.at[block(bd, rows), :]
+        x0 = buf.at[block(bx, rows), pl.ds(0, half)]
+        y1 = buf.at[block(by, rows), pl.ds(half, half)]
+        d0 = buf.at[block(bd, rows), pl.ds(0, half)]
+        d1 = buf.at[block(bd, rows), pl.ds(half, half)]
+        ss, rs = ag_ssem.at[p], ag_rsem.at[p]
+
+        def same(ref, i, where):
+            return remote(ref, ref, ss.at[i], rs.at[i], where)
+
+        sends = [
+            same(me, 0, to_x),
+            same(me, 1, to_y),
+            same(me, 2, to_core),
+            same(x0, 3, to_y),
+            same(blk_x, 4, to_core),
+            same(y1, 5, to_x),
+            same(blk_y, 6, to_core),
+            same(blk_d, 7, to_core),
+        ]
+        other = 1 - core
+        into = [
+            blk_x,
+            blk_y,
+            buf.at[block(chip * 2 + other, rows), :],
+            d0,
+            buf.at[block(chip_x * 2 + other, rows), :],
+            d1,
+            buf.at[block(chip_y * 2 + other, rows), :],
+            buf.at[block(chip_d * 2 + other, rows), :],
+        ]
+
+        def arrived(i):
+            pltpu.make_async_copy(into[i], into[i], rs.at[i]).wait()
+
+        return sends, arrived
+
+    cot[block(s, rows), :] = cotown_ref[...]
+    c_sends, c_arrived = gather_copies(0, cot)
+    for i in range(3):
+        c_sends[i].start()
+
+    x = tok_ref[...].astype(F32)
+    mean = jnp.mean(x, axis=-1, keepdims=True)
+    centred = x - mean
+    inv = lax.rsqrt(jnp.mean(centred * centred, axis=-1, keepdims=True) + EPSILON)
+    normed[block(s, rows), :] = (
+        centred * inv * gain_ref[...].astype(F32) + shift_ref[...].astype(F32)
+    ).astype(BF16)
+    n_sends, n_arrived = gather_copies(1, normed)
+    for i in range(3):
+        n_sends[i].start()
+    for sends, arrived in ((c_sends, c_arrived), (n_sends, n_arrived)):
+        arrived(0)
+        sends[3].start()
+        sends[4].start()
+        arrived(1)
+        sends[5].start()
+        sends[6].start()
+    zstep(1)
+    for sends, arrived in ((c_sends, c_arrived), (n_sends, n_arrived)):
+        arrived(3)
+        arrived(5)
+        sends[7].start()
+    for sends, arrived in ((c_sends, c_arrived), (n_sends, n_arrived)):
+        for i in (2, 4, 6, 7):
+            arrived(i)
+    zstep(2)
+
+    def low(t, carry):
+        r = block(t, TILE)
+        c = dot_nt(normed[r, :], downs_ref[...])
+        coeff[r, :] = c.astype(BF16)
+        g = ADAPTER_SCALE * dot_nt(cot[r, :], ups_ref[...])
+        cgs[r, :] = g.astype(BF16)
+        return carry
+
+    lax.fori_loop(0, tiles, low, 0)
+    for copy in own:
+        copy.wait()
+    zstep(3)
+    zstep(4)
+    zstep(5)
+    zstep(6)
+
+    def project(t, carry):
+        r = block(t, TILE)
+        cos = cos_ref[r, :]
+        sin = sin_ref[r, :]
+        for c in range(3):
+            v = ADAPTER_SCALE * dot(coeff[r, :RANK], qup_ref[:, c * mine : (c + 1) * mine])
+            v = v + qb_ref[c : c + 1, block(s, mine)].astype(F32)
+            for j in range(planes):
+                v = v + dot(normed[r, j * fan : (j + 1) * fan], wq[j, c])
+            if c < 2:
+                v = turn_all(v, cos, sin, 1.0)
+            v = v.astype(BF16)
+            if c == 0:
+                v = v * jnp.asarray(HD**-0.5, BF16)
+            qkv[c, r, :] = v
+        g = dot(cgs[r, :RANK], ddown_ref[...])
+        for j in range(planes):
+            g = g + dot_nt(cot[r, j * fan : (j + 1) * fan], wd[j])
+        hg[r, :] = g.astype(BF16)
+        return carry
+
+    lax.fori_loop(0, tiles, project, 0)
+    zstep(7)
+
+    dk[...] = jnp.zeros_like(dk)
+    dv[...] = jnp.zeros_like(dv)
+    heads = mine // HD
+
+    for b in range(length // BLOCK):
+        lo, hi = b * BLOCK, (b + 1) * BLOCK
+        acc_a[...] = jnp.zeros_like(acc_a)
+        acc_b[...] = jnp.zeros_like(acc_b)
+
+        def one_head(h, carry, lo=lo, hi=hi):
+            lane = lax.broadcasted_iota(jnp.int32, (1, mine), 1)
+            mask = (lane // HD == h).astype(BF16)
+            mask32 = (lane // HD == h).astype(F32)
+            q = qkv[0, lo:hi, :] * mask
+            g = hg[lo:hi, :] * mask
+            k = qkv[1, :hi, :]
+            v = qkv[2, :hi, :]
+            sc = dot_nt(q, k)
+            e = jnp.exp(sc - jnp.max(sc, axis=-1, keepdims=True))
+            p = e * (1.0 / jnp.sum(e, axis=-1, keepdims=True))
+            pb = p.astype(BF16)
+            acc_a[...] += dot(pb, v) * mask32
+            dp = dot_nt(g, v)
+            ds = (p * (dp - jnp.sum(dp * p, axis=-1, keepdims=True))).astype(BF16)
+            acc_b[...] += dot(ds, k) * mask32
+            dk[:hi, :] += dot_tn(ds, q)
+            dv[:hi, :] += dot_tn(pb, g)
+            return carry
+
+        lax.fori_loop(0, heads, one_head, 0)
+        att[lo:hi, :] = acc_a[...].astype(BF16)
+        back = (acc_b[...] * (HD**-0.5)).astype(BF16).astype(F32)
+        pg[0, lo:hi, :] = turn_all(back, cos_ref[lo:hi, :], sin_ref[lo:hi, :], -1.0).astype(BF16)
+        if b % 2 == 1:
+            zstep(8 + b // 2)
+
+    def finish(t, carry):
+        r = block(t, TILE)
+        back = dk[r, :].astype(BF16).astype(F32)
+        pg[1, r, :] = turn_all(back, cos_ref[r, :], sin_ref[r, :], -1.0).astype(BF16)
+        pg[2, r, :] = dv[r, :].astype(BF16)
+        return carry
+
+    lax.fori_loop(0, tiles, finish, 0)
+
+    coeff_t[...] = dot_nt(downs_ref[...], normed[...]).astype(BF16)
+    cgs_t[...] = (ADAPTER_SCALE * dot_nt(ups_ref[...], cot[...])).astype(BF16)
+
+    share = width // 8
+    at_qup = share
+    at_ddown = at_qup + 3 * mine
+    at_dup = at_ddown + mine
+    at_idown = at_dup + share
+    at_iup = at_idown + share
+    at_odown = at_iup + units
+    at_oup = at_odown + units
+    for c in range(3):
+        packed_ref[:, at_qup + c * mine : at_qup + (c + 1) * mine] = ADAPTER_SCALE * dot(
+            coeff_t[:RANK, :], pg[c]
+        )
+    packed_ref[:, at_ddown : at_ddown + mine] = dot(cgs_t[:RANK, :], att[...])
+    zstep(10)
+
+    k0 = 0.7978845608028654
+    k1 = 0.044715
+
+    def inner(t, carry):
+        r = block(t, TILE)
+        v = ADAPTER_SCALE * dot(coeff[r, RANK : 2 * RANK], iup_ref[...])
+        v = v + ib_ref[:, block(s, units)].astype(F32)
+        for j in range(planes):
+            v = v + dot(normed[r, j * fan : (j + 1) * fan], wi[j])
+        sq = v * v
+        th = jnp.tanh(k0 * v * (1.0 + k1 * sq))
+        act[r, :] = (0.5 * v * (1.0 + th)).astype(BF16)
+        pre[r, :] = 0.5 * (1.0 + th) + 0.5 * v * (1.0 - th * th) * (k0 * (1.0 + 3.0 * k1 * sq))
+        return carry
+
+    lax.fori_loop(0, tiles, inner, 0)
+    packed_ref[:, at_odown : at_odown + units] = dot(cgs_t[RANK : 2 * RANK, :], act[...])
+    zstep(11)
+
+    partners = (to_core, to_x, to_y)
+
+    def reduce_copy(w, i):
+        return remote(
+            ar_send.at[w], ar_recv.at[w, i], ar_ssem.at[w, i], ar_rsem.at[w, i], partners[i]
+        )
+
+    def reduce_round(w, i):
+        if i > 0:
+            reduce_copy(w, i - 1).wait()
+            ar_send[w] += ar_recv[w, i - 1]
+        if i < 3:
+            reduce_copy(w, i).start()
+
+    ar_send[0, :RANK, :] = dot_nt(ddown_ref[...], att[...])
+    ar_send[0, RANK : 2 * RANK, :] = dot_nt(odown_ref[...], act[...])
+    for i in range(4):
+        reduce_round(0, i)
+    coeff_dense = ar_send[0].astype(BF16)
+    for i in range(2):
+        g = ADAPTER_SCALE * dot(
+            coeff_dense[i * RANK : (i + 1) * RANK, :], cot[:, block(s, share)]
+        )
+        at = (at_dup, at_oup)[i]
+        packed_ref[:, at : at + share] = g
+
+    p_units = width // UNIT
+    per = fan // UNIT
+    early = p_units - planes
+    total = 2 * p_units
+
+    def place_of(n):
+        first = n < p_units
+        j = jnp.where(first, n % planes, (n - p_units) // per)
+        i = jnp.where(first, n // planes, (n - p_units) % per)
+        return j, i
+
+    def keep_split(n, k, r):
+        slot = n % 2
+        a = r[:rows, :]
+        b = r[rows:, :]
+        first = core == 0
+        keep[n % 4, k] = jnp.where(first, a, b)
+        s1_send[slot, k] = jnp.where(first, b, a).astype(BF16)
+
+    def s1_copy(n):
+        return remote(s1_send.at[n % 2], s1_recv.at[n], s1_ssem.at[n % 2], s1_rsem.at[n], to_core)
+
+    def a_copy(n, i):
+        return remote(
+            a_send.at[n % 2, i], a_recv.at[n, i], a_ssem.at[n % 2, i], a_rsem.at[n, i],
+            (to_x, to_y)[i],
+        )
+
+    def c_copy(n, i):
+        return remote(
+            c_send.at[n % 2, i], c_recv.at[n, i], c_ssem.at[n % 2, i], c_rsem.at[n, i],
+            (to_x, to_y)[i],
+        )
+
+    hu = UNIT // 2
+
+    def stage0_branch(n):
+        j, i = place_of(n)
+
+        def tile(k, carry):
+            r = block(k, TILE)
+            cols = block(i, UNIT)
+            keep_split(n, k, dot(act[r, :], wo[j, :, cols]) + dot(att[r, :], wd[j, :, cols]))
+            return carry
+
+        lax.fori_loop(0, tiles, tile, 0)
+        s1_copy(n).start()
+
+    def stage0_back(n):
+        j, i = place_of(n)
+
+        def tile(k, carry):
+            r = block(k, TILE)
+            rws = block(i, UNIT)
+            v = dot_nt(pgrad[r, :], wi[j, rws, :])
+            for c in range(3):
+                v = v + dot_nt(pg[c, r, :], wq[j, c, rws, :])
+            keep_split(n, k, v)
+            return carry
+
+        lax.fori_loop(0, tiles, tile, 0)
+        s1_copy(n).start()
+
+    def stage1(n):
+        s1_copy(n).wait()
+        q = n % 4
+        for k in range(4):
+            keep[q, k] += s1_recv[n, k].astype(F32)
+        far = keep[q, chip_d]
+        a_send[n % 2, 0] = far[:, :hu].astype(BF16)
+        a_send[n % 2, 1] = far[:, hu:].astype(BF16)
+        for i in range(2):
+            a_copy(n, i).start()
+
+    def stage2(n):
+        q = n % 4
+        for i in range(2):
+            a_copy(n, i).wait()
+        keep[q, chip_y, :, :hu] += a_recv[n, 0].astype(F32)
+        keep[q, chip_x, :, hu:] += a_recv[n, 1].astype(F32)
+        c_send[n % 2, 0] = keep[q, chip_x].astype(BF16)
+        c_send[n % 2, 1] = keep[q, chip_y].astype(BF16)
+        for i in range(2):
+            c_copy(n, i).start()
+
+    def stage3(n):
+        q = n % 4
+        for i in range(2):
+            c_copy(n, i).wait()
+        j, i = place_of(n)
+        v = keep[q, chip] + c_recv[n, 0].astype(F32) + c_recv[n, 1].astype(F32)
+        res[n // p_units, :, block(j * per + i, UNIT)] = v
+
+    def pipeline(first, lo, hi, stage0, extra=None):
+        def body(n, carry):
+            if stage0 is not None:
+                stage0(n)
+            for back, stage in ((1, stage1), (2, stage2), (3, stage3)):
+                m = n - back
+                ok = m >= first
+                if stage0 is None:
+                    ok = jnp.logical_and(ok, m < hi - 3)
+
+                @pl.when(ok)
+                def _(m=m, stage=stage):
+                    stage(m)
+
+            if extra is not None:
+                extra(n)
+            return carry
+
+        lax.fori_loop(lo, hi, body, 0)
+
+    zstep(12)
+    pipeline(0, 0, early, stage0_branch)
+    pipeline(0, early, early + 3, None)
+
+    def act_back(t, carry):
+        r = block(t, TILE)
+        v = dot(cgs[r, RANK : 2 * RANK], odown_ref[...])
+        for j in range(planes):
+            for i in range(per - 1):
+                c0 = j * fan + i * UNIT
+                v = v + dot_nt(cot[r, c0 : c0 + UNIT], wo[j, :, i * UNIT : (i + 1) * UNIT])
+        ag[r, :] = v
+        return carry
+
+    lax.fori_loop(0, tiles, act_back, 0)
+    for t in range(13, last_step):
+        zstep(t)
+
+    pipeline(early, early, p_units, stage0_branch)
+
+    def act_last(t, carry):
+        r = block(t, TILE)
+        v = ag[r, :]
+        for j in range(planes):
+            i = per - 1
+            c0 = j * fan + i * UNIT
+            v = v + dot_nt(cot[r, c0 : c0 + UNIT], wo[j, :, i * UNIT : (i + 1) * UNIT])
+        pgrad[r, :] = (v * pre[r, :]).astype(BF16)
+        return carry
+
+    lax.fori_loop(0, tiles, act_last, 0)
+
+    up_part = dot_nt(iup_ref[...], pgrad[...])
+    q_part = dot_nt(qup_ref[:, :mine], pg[0])
+    for c in range(1, 3):
+        q_part = q_part + dot_nt(qup_ref[:, c * mine : (c + 1) * mine], pg[c])
+    ar_send[1, :RANK, :] = ADAPTER_SCALE * q_part
+    ar_send[1, RANK : 2 * RANK, :] = ADAPTER_SCALE * up_part
+    reduce_round(1, 0)
+
+    def rounds(n):
+        for i in range(1, 4):
+
+            @pl.when(n == p_units + 2 * i - 1)
+            def _(i=i):
+                reduce_round(1, i)
+
+    pipeline(early, p_units, total, stage0_back, rounds)
+    packed_ref[:, at_iup : at_iup + units] = ADAPTER_SCALE * dot(
+        coeff_t[RANK : 2 * RANK, :], pgrad[...]
+    )
+    late = ar_send[1].astype(BF16)
+    g = dot(late, normed[:, block(s, share)])
+    packed_ref[:, :share] = g[:RANK]
+    packed_ref[:, at_idown : at_idown + share] = g[RANK:]
+    pipeline(early, total, total + 3, None)
+
+    first_t = ar_send[0, :, block(s, rows)].astype(BF16)
+    late_t = ar_send[1, :, block(s, rows)].astype(BF16)
+    out = tok_ref[...].astype(F32) + res[0] + ADAPTER_SCALE * dot_tn(first_t, ups_ref[...])
+    out_ref[...] = (out + db_ref[...].astype(F32) + ob_ref[...].astype(F32)).astype(BF16)
+    x = tok_ref[...].astype(F32)
+    mean = jnp.mean(x, axis=-1, keepdims=True)
+    centred = x - mean
+    inv = lax.rsqrt(jnp.mean(centred * centred, axis=-1, keepdims=True) + EPSILON)
+    xhat = centred * inv
+    e = (res[1] + dot_tn(late_t, downs_ref[...])) * gain_ref[...].astype(F32)
+    igrad_ref[...] = cotown_ref[...].astype(F32) + inv * (
+        e
+        - jnp.mean(e, axis=-1, keepdims=True)
+        - xhat * jnp.mean(e * xhat, axis=-1, keepdims=True)
+    )
+
+    for sends, _ in ((c_sends, None), (n_sends, None)):
+        for copy in sends:
+            copy.wait_send()
+    for c in range(n_chunks):
+        for k in range(planes - 1):
+            for direction in (0, 1):
+
+                @pl.when(zhas(direction, k))
+                def _(c=c, k=k, direction=direction):
+                    zcopy(c, direction, k).wait_send()
+
+
+def run_layer(planes, args, shapes):
+    rows, width, length, units, mine = shapes
+    fan = width // planes
+    vm = pl.BlockSpec(memory_space=pltpu.VMEM)
+    hbm = pl.BlockSpec(memory_space=pl.ANY)
+    n_chunks = 8 + 2 * (fan // UNIT)
+    total = 2 * width // UNIT
+    dma = pltpu.SemaphoreType.DMA
+    cols = width // 8 * 4 + 4 * mine + 2 * units
+    return pl.pallas_call(
+        functools.partial(layer_kernel, planes),
+        out_shape=(
+            jax.ShapeDtypeStruct((rows, width), BF16),
+            jax.ShapeDtypeStruct((rows, width), F32),
+            jax.ShapeDtypeStruct((RANK, cols), F32),
+        ),
+        in_specs=[vm, vm, hbm, hbm, hbm, hbm] + [vm] * 14,
+        out_specs=(vm, vm, vm),
+        scratch_shapes=[
+            pltpu.VMEM((length, width), BF16),
+            pltpu.VMEM((length, width), BF16),
+            pltpu.VMEM((planes, 3, fan, mine), BF16),
+            pltpu.VMEM((planes, mine, fan), BF16),
+            pltpu.VMEM((planes, fan, units), BF16),
+            pltpu.VMEM((planes, units, fan), BF16),
+            pltpu.VMEM((3, length, mine), BF16),
+            pltpu.VMEM((length, mine), BF16),
+            pltpu.VMEM((length, mine), BF16),
+            pltpu.VMEM((length, mine), F32),
+            pltpu.VMEM((length, mine), F32),
+            pltpu.VMEM((3, length, mine), BF16),
+            pltpu.VMEM((BLOCK, mine), F32),
+            pltpu.VMEM((BLOCK, mine), F32),
+            pltpu.VMEM((length, units), F32),
+            pltpu.VMEM((length, units), BF16),
+            pltpu.VMEM((length, units), F32),
+            pltpu.VMEM((length, units), BF16),
+            pltpu.VMEM((length, 2 * RANK), BF16),
+            pltpu.VMEM((length, 2 * RANK), BF16),
+            pltpu.VMEM((2 * RANK, length), BF16),
+            pltpu.VMEM((2 * RANK, length), BF16),
+            pltpu.VMEM((2, rows, width), F32),
+            pltpu.VMEM((4, 4, rows, UNIT), F32),
+            pltpu.VMEM((2, 4, rows, UNIT), BF16),
+            pltpu.VMEM((total, 4, rows, UNIT), BF16),
+            pltpu.VMEM((2, 2, rows, UNIT // 2), BF16),
+            pltpu.VMEM((total, 2, rows, UNIT // 2), BF16),
+            pltpu.VMEM((2, 2, rows, UNIT), BF16),
+            pltpu.VMEM((total, 2, rows, UNIT), BF16),
+            pltpu.VMEM((2, 2 * RANK, length), F32),
+            pltpu.VMEM((2, 3, 2 * RANK, length), F32),
+            dma((n_chunks,)),
+            dma((n_chunks, 2, planes)),
+            dma((n_chunks, planes)),
+            dma((2, 8)),
+            dma((2, 8)),
+            dma((2,)),
+            dma((total,)),
+            dma((2, 2)),
+            dma((total, 2)),
+            dma((2, 2)),
+            dma((total, 2)),
+            dma((2, 3)),
+            dma((2, 3)),
+        ],
+        compiler_params=pltpu.CompilerParams(
+            collective_id=0, has_side_effects=True, vmem_limit_bytes=63 * 1024 * 1024
+        ),
+    )(*args)
+
+
+def fits(planes, groups, shapes):
+    rows, width, length, units, mine = shapes
+    return (
+        groups == 8
+        and planes > 1
+        and rows * 2 == TILE
+        and length <= 1024
+        and width % (planes * UNIT) == 0
+        and mine % 128 == 0
+        and units % 256 == 0
+    )
+
+
+def deliver(packed, sizes, counts, pick, planes, groups):
+    s = lax.axis_index("seq")
+    everyone = lax.all_gather(packed, "seq", axis=0, tiled=False)
+    owned = []
+    at = 0
+    for i, (n, w) in enumerate(zip(counts, sizes)):
+        part = everyone[:, :, at : at + w]
+        at += w
+        blocks = 3 if i == 1 else 1
+        part = part.reshape(groups, RANK, blocks, w // blocks).transpose(1, 2, 0, 3)
+        part = part.reshape(RANK, planes, groups, n)
+        owned.append(lax.dynamic_index_in_dim(part, s, 2, keepdims=False))
+    owned = jnp.concatenate(owned, axis=2).transpose(1, 0, 2)
+    arrived = lax.all_to_all(owned, "fsdp", split_axis=0, concat_axis=0, tiled=True)
+    place = pick.astype(F32).reshape(planes * RANK, ADAPT * RANK)
+    spread = lax.dot_general(
+        arrived.reshape(planes * RANK, -1),
+        place,
+        (((0,), (0,)), ((), ())),
+        precision=lax.Precision.HIGHEST,
+        preferred_element_type=F32,
+    )
+    outs = []
+    at = 0
+    for n in counts:
+        outs.append(spread[at : at + n])
+        at += n
+    return outs
 
 
 def on_device(
@@ -100,6 +874,40 @@
     inner_up = own(inner_up, units)
     outer_down = own(outer_down, units)
 
+    shapes = (rows, width, length, units, mine)
+    if fits(planes, groups, shapes):
+        cos, sin = rope_constants(length)
+        layer_out, input_grad, packed = run_layer(
+            planes,
+            (
+                tokens,
+                cotangent,
+                qkv_weight,
+                dense_weight,
+                inner_weight,
+                outer_weight,
+                qkv_bias.reshape(3, width),
+                dense_bias[None],
+                inner_bias[None],
+                outer_bias[None],
+                norm_gain[None],
+                norm_bias[None],
+                jnp.concatenate([qkv_down, inner_down], axis=0),
+                jnp.concatenate([dense_up, outer_up], axis=0),
+                qkv_up,
+                dense_down,
+                inner_up,
+                outer_down,
+                cos,
+                sin,
+            ),
+            shapes,
+        )
+        sizes = [width // groups, 3 * mine, mine, width // groups, width // groups]
+        sizes += [units, units, width // groups]
+        outs = deliver(packed, sizes, counts, pick, planes, groups)
+        return (layer_out, input_grad, *outs)
+
     wqkv = lax.all_gather(qkv_weight, "fsdp", axis=1, tiled=True)
     wdense = lax.all_gather(dense_weight, "fsdp", axis=1, tiled=True)
     winner = lax.all_gather(inner_weight, "fsdp", axis=0, tiled=True)
@@ -246,32 +1054,8 @@
         ups[RANK:],
     ]
     packed = jnp.concatenate(mine_grads, axis=1)
-    everyone = lax.all_gather(packed, "seq", axis=0, tiled=False)
-    owned = []
-    at = 0
-    for i, (n, g) in enumerate(zip(counts, mine_grads)):
-        w = g.shape[1]
-        part = everyone[:, :, at : at + w]
-        at += w
-        blocks = 3 if i == 1 else 1
-        part = part.reshape(groups, RANK, blocks, w // blocks).transpose(1, 2, 0, 3)
-        part = part.reshape(RANK, planes, groups, n)
-        owned.append(lax.dynamic_index_in_dim(part, s, 2, keepdims=False))
-    owned = jnp.concatenate(owned, axis=2).transpose(1, 0, 2)
-    arrived = lax.all_to_all(owned, "fsdp", split_axis=0, concat_axis=0, tiled=True)
-    place = pick.astype(F32).reshape(planes * RANK, ADAPT * RANK)
-    spread = lax.dot_general(
-        arrived.reshape(planes * RANK, -1),
-        place,
-        (((0,), (0,)), ((), ())),
-        precision=lax.Precision.HIGHEST,
-        preferred_element_type=F32,
-    )
-    outs = []
-    at = 0
-    for n in counts:
-        outs.append(spread[at : at + n])
-        at += n
+    sizes = [g.shape[1] for g in mine_grads]
+    outs = deliver(packed, sizes, counts, pick, planes, groups)
     return (layer_out, input_grad, *outs)
 
 

time: 689 us -> 393 us (0.57); the launches traced: 678 us -> 392 us
  waiting for transfers between devices: 434 us -> 51.2 us
  Pallas kernels: 0 us -> 277 us
  matrix products: 142 us -> 0.86 us
  other arithmetic: 23.7 us -> 2.05 us
  blocking collectives: 21.3 us -> 12.3 us
    pallas_call x0 -> x1, Pallas kernels: none -> 277 us  [run_layer(): pl.pallas_call(functools.partial(layer_kernel, planes), out_shape=(jax.Sh...]
    all_gather x7 -> x1, waiting for transfers between devices: 233 us -> 27 us  [deliver(): everyone = lax.all_gather(packed, 'seq', axis=0, tiled=False)]
    reduce_scatter x4 -> x0, waiting for transfers between devices: 178 us -> none  [scatter(): return lax.psum_scatter(x, 'seq', scatter_dimension=0, tiled=True)]
    dot_general x31 -> x1, matrix products: 91.8 us -> 0.24 us  [dot(): return lax.dot_general(a, b, (dims, ((), ())), preferred_element_type=F32)]
    dot_general x22 -> x1, matrix products: 43 us -> 0.62 us  [deliver(): lax.dot_general(arrived.reshape(planes * RANK, -1), place, (((0,), (0,)),...]
    convert_element_type x15 -> x0, other arithmetic: 12.5 us -> none  [the longest x4 8.47 us: on_device(): score_grad = (prob * (prob_grad - row_dot)).astype(BF16)]
    all_gather x1 -> x0, blocking collectives: 9.02 us -> none  [on_device(): late = lax.all_gather(late_own, 'seq', axis=0, tiled=True)]
    unnamed x168 -> x25, local copies, waits for them, and re-layouts: 16.2 us -> 8.17 us
  transfers between devices with their start and end apart: 13 -> 3, of which waited for: 12 -> 3; matrix products, arithmetic and copies ran while one was open for 23% -> 2% of each run, Pallas kernels for 0% -> 0%
where the time goes in v2:
time: 393 us; the launch traced here: 392 us
  Pallas kernels  277 us (70%)
  waiting for transfers between devices  51.2 us (13%)
  local copies, waits for them, and re-layouts  29.4 us (7%)
  between operations  14.5 us (4%)
  blocking collectives  12.3 us (3%)
  starting transfers between devices  4.68 us (1%)
    pallas_call x1, Pallas kernels, run_layer(): pl.pallas_call(functools.partial(layer_kernel, planes), out_shape=(jax.Sh...  277 us
    all_gather x1, waiting for transfers between devices, deliver(): everyone = lax.all_gather(packed, 'seq', axis=0, tiled=False)  27 us
    all_gather x1, waiting for transfers between devices, on_device(): chosen = lax.all_gather(chosen, 'seq', axis=1, tiled=False)  14.9 us
    all_to_all x1, blocking collectives, on_device(): lax.all_to_all(chosen, 'fsdp', split_axis=0, concat_axis=0, tiled=True)  12.3 us
    all_to_all x1, waiting for transfers between devices, deliver(): lax.all_to_all(owned, 'fsdp', split_axis=0, concat_axis=0, tiled=True)  9.32 us
    unnamed x25, local copies, waits for them, and re-layouts  8.17 us
  transfers between devices with their start and end apart: 3, of which 3 were waited for; matrix products, arithmetic and copies ran while one was open for 2% of the time, Pallas kernels for 0%

profile of v2, /device:TPU:0, one launch (start us, length us, event | category | flops | bytes accessed | tf_op | source)
XLA Modules:
  0.0 392.1 jit_solution(4154042422314916512)
XLA Ops:
  7.2 0.7 constant_dynamic-update-slice_fusion.7
  7.9 0.7 broadcast_multiply_fusion
  8.8 0.8 constant_dynamic-update-slice_fusion.6
  9.6 0.7 constant_dynamic-update-slice_fusion.5
  10.3 0.7 constant_dynamic-update-slice_fusion.4
  11.0 0.7 constant_dynamic-update-slice_fusion.3
  11.7 0.9 constant_dynamic-update-slice_fusion.2
  12.6 0.9 constant_dynamic-update-slice_fusion.1
  13.4 0.7 constant_dynamic-update-slice_fusion
  14.2 0.2 convolution_convert_fusion
  14.4 12.3 %all_to_all.10 = bf16[4,16,1024]{2,1,0:T(8,128)(2,1)} all-to-all(bf16[4,16,1024]{2,1,0:T(8,128)(2,1)S(1)} %bitcast.148), channel_id=1, replica_groups=mesh['fsdp'=4,'seq'=8] {'fsdp'}, dimensions={0} | all-to-all | bytes 262144 | tf_op jit(solution)/shard_map/all_to_all | solution.py:857
  26.8 1.3 reshape.117.qb_ref
  28.1 1.3 broadcast_in_dim.18.db_ref
  29.4 1.3 broadcast_in_dim.19.ib_ref
  30.8 1.3 broadcast_in_dim.20.ob_ref
  32.1 1.3 broadcast_in_dim.21.gain_ref
  33.3 1.3 broadcast_in_dim.22.shift_ref
  34.6 14.9 %all-gather.5.cloned.1.call-done = bf16[4,128,1024]{2,1,0:T(8,128)(2,1)} async-done(((bf16[4,16,1024]{2,1,0:T(8,128)(2,1)}), bf16[4,128,1024]{2,1,0:T(8,128)(2,1)}) %all-gather.5.cloned.1.call-update) | async-done | bytes 1048592 | tf_op jit(solution)/shard_map/all_gather | solution.py:858
  49.5 1.4 slice_bitcast_fusion.4
  50.9 1.1 slice_bitcast_fusion.2
  52.1 0.2 slice_bitcast_fusion
  52.3 0.2 reshape.120
  52.6 0.2 reshape.119
  52.8 0.2 reshape.122
  53.0 0.2 reshape.121
  53.3 0.2 reshape.123
  53.9 0.6 constant_dynamic-slice_fusion.10
  54.5 0.6 pad_maximum_fusion.2.qup_ref
  55.1 0.6 constant_dynamic-slice_fusion.8
  55.7 0.7 pad_maximum_fusion
  56.4 277.0 %shard_map.294 = (bf16[128,2048]{1,0:T(8,128)(2,1)}, f32[128,2048]{1,0:T(8,128)}, f32[16,4096]{1,0:T(8,128)}) custom-call(bf16[128,2048]{1,0:T(8,128)(2,1)} %tok_ref.1, bf16[128,2048]{1,0:T(8,128)(2,1)} %cotown_ref.1, bf16[3,512,256]{2,1,0:T(8,128)(2,1)} %wq_in.1, bf16[256,512]{1,0:T(8,128)(2,1)} %wd_in.1, bf16[512,1024]{1,0:T(8,128)(2,1)} %wi_in.1, ...), custom_call_target="tpu_custom_call" | custom-call | tf_op jit(solution)/shard_map/pallas_call | solution.py:722
  333.5 27.0 %all-gather.7.cloned.1.call-done = f32[128,4096]{1,0:T(8,128)} async-done(((f32[16,4096]{1,0:T(8,128)}), f32[128,4096]{1,0:T(8,128)}) %all-gather.7.cloned.1.call-update) | async-done | bytes 2097168 | tf_op jit(solution)/shard_map/all_gather | solution.py:799
  360.5 1.4 fusion.3
  361.9 1.0 slice.120
  363.2 0.2 reshape.129
  363.4 0.2 copy.59
  363.7 0.2 reshape.130
  364.7 0.3 copy.98
  365.2 0.3 copy.97
  366.0 0.8 concatenate.19
  366.9 4.6 %all-to-all-start.1 = ((f32[4,16,1024]{2,1,0:T(8,128)}), f32[4,16,1024]{2,1,0:T(8,128)S(1)}, u32[]{:S(2)}, u32[]{:S(2)}) async-start(f32[4,16,1024]{2,1,0:T(8,128)} %bitcast.34), calls=%async_computation.1 | async-start | bytes 524288 | tf_op jit(solution)/shard_map/all_to_all | solution.py:810
  371.5 9.3 %all-to-all-done.1 = f32[4,16,1024]{2,1,0:T(8,128)S(1)} async-done(((f32[4,16,1024]{2,1,0:T(8,128)}), f32[4,16,1024]{2,1,0:T(8,128)S(1)}, u32[]{:S(2)}, u32[]{:S(2)}) %all-to-all-start.1) | async-done | bytes 262176 | tf_op jit(solution)/shard_map/all_to_all | solution.py:810
  380.8 0.6 fusion
  381.4 0.7 fusion.5
  382.1 0.6 slice.128
  382.7 0.7 fusion.6
  383.5 0.8 copy.120
  384.3 1.0 copy.121
  (54 shorter events, 2.4 us)
Async XLA Ops:
  7.2 42.3 %all-gather.5.cloned.1.call-start = ((), (), s32[]{:S(2)}) async-start(), calls=%async_computation.2 | async-start | bytes 1179648 | tf_op jit(solution)/shard_map/all_gather | solution.py:858
  26.7 333.8 %all-gather.7.cloned.1.call-start = ((), (), s32[]{:S(2)}) async-start(), calls=%async_computation.3 | async-start | bytes 2359296 | tf_op jit(solution)/shard_map/all_gather | solution.py:799
  49.5 2.6 copy-start.1
  360.5 2.4 copy-start
  365.7 17.8 %copy-start.3 = (bf16[128,2048]{1,0:T(8,128)(2,1)S(1)}, bf16[128,2048]{1,0:T(8,128)(2,1)}, u32[]{:S(2)}) copy-start(bf16[128,2048]{1,0:T(8,128)(2,1)} %get-tuple-element.58) | copy-start | bytes 1572868
  366.0 18.3 %copy-start.2 = (f32[128,2048]{1,0:T(8,128)S(1)}, f32[128,2048]{1,0:T(8,128)}, u32[]{:S(2)}) copy-start(f32[128,2048]{1,0:T(8,128)} %get-tuple-element.59) | copy-start | bytes 3145732
  366.9 13.9 %all-to-all-start.1 = ((f32[4,16,1024]{2,1,0:T(8,128)}), f32[4,16,1024]{2,1,0:T(8,128)S(1)}, u32[]{:S(2)}, u32[]{:S(2)}) async-start(f32[4,16,1024]{2,1,0:T(8,128)} %bitcast.34), calls=%async_computation.1 | async-start | bytes 524288 | tf_op jit(solution)/shard_map/all_to_all | solution.py:810
Sparse Core Ops, SparseCore 0:
  26.9 22.5 all-gather.4
  333.6 26.8 all-gather.6

commit v3 on v2

--- a/solution.py
+++ b/solution.py
@@ -107,17 +107,31 @@
     ob_ref,
     gain_ref,
     shift_ref,
-    downs_ref,
-    ups_ref,
-    qup_ref,
-    ddown_ref,
-    iup_ref,
-    odown_ref,
+    index_ref,
+    map_refs,
     cos_ref,
     sin_ref,
     out_ref,
     igrad_ref,
-    packed_ref,
+    grad_refs,
+    stack,
+    sel,
+    adm,
+    downs_ref,
+    ups_ref,
+    ddown_all,
+    qup_all,
+    iup_ref,
+    odown_ref,
+    qgrad,
+    a_msg,
+    a_h1,
+    a_h2,
+    b_msg,
+    b_h1,
+    b_h2,
+    q_h1,
+    q_h2,
     normed,
     cot,
     wq,
@@ -127,8 +141,6 @@
     qkv,
     hg,
     att,
-    dk,
-    dv,
     pg,
     acc_a,
     acc_b,
@@ -163,6 +175,16 @@
     c_rsem,
     ar_ssem,
     ar_rsem,
+    adz_ssem,
+    adz_rsem,
+    h1_ssem,
+    h1_rsem,
+    h2_ssem,
+    h2_rsem,
+    q1_ssem,
+    q1_rsem,
+    q2_ssem,
+    q2_rsem,
 ):
     z = lax.axis_index("fsdp")
     s = lax.axis_index("seq")
@@ -191,19 +213,11 @@
         return pl.ds(pl.multiple_of(i * n, n), n)
 
     bar = pltpu.get_barrier_semaphore()
-    for where in (to_core, to_x, to_y):
-        pl.semaphore_signal(bar, inc=1, device_id=where, device_id_type=MESH)
-
-    @pl.when(z > 0)
-    def _():
-        pl.semaphore_signal(bar, inc=1, device_id=(z - 1, s), device_id_type=MESH)
-
-    @pl.when(z < planes - 1)
-    def _():
-        pl.semaphore_signal(bar, inc=1, device_id=(z + 1, s), device_id_type=MESH)
-
-    above = jnp.where(z < planes - 1, 1, 0)
-    pl.semaphore_wait(bar, 3 + above + jnp.where(z > 0, 1, 0))
+    for k in range(1, 8):
+        pl.semaphore_signal(bar, inc=1, device_id=(z, (s + k) % 8), device_id_type=MESH)
+    for k in range(1, planes):
+        pl.semaphore_signal(bar, inc=1, device_id=((z + k) % planes, s), device_id_type=MESH)
+    pl.semaphore_wait(bar, 7 + planes - 1)
 
     chunks = []
     for c in range(3):
@@ -288,18 +302,28 @@
 
     half = width // 2
 
-    def gather_copies(p, buf):
-        me = buf.at[block(s, rows), :]
+    def row_view(buf, b, part):
+        if part is None:
+            return buf.at[block(b, rows), :]
+        return buf.at[block(b, rows), pl.ds(part * half, half)]
+
+    def lead_view(buf, b, part):
+        if part is None:
+            return buf.at[b]
+        return buf.at[b, pl.ds(part * (planes // 2), planes // 2)]
+
+    def gather_copies(p, buf, view):
         bx = chip_x * 2 + core
         by = chip_y * 2 + core
         bd = chip_d * 2 + core
-        blk_x = buf.at[block(bx, rows), :]
-        blk_y = buf.at[block(by, rows), :]
-        blk_d = buf.at[block(bd, rows), :]
-        x0 = buf.at[block(bx, rows), pl.ds(0, half)]
-        y1 = buf.at[block(by, rows), pl.ds(half, half)]
-        d0 = buf.at[block(bd, rows), pl.ds(0, half)]
-        d1 = buf.at[block(bd, rows), pl.ds(half, half)]
+        me = view(buf, s, None)
+        blk_x = view(buf, bx, None)
+        blk_y = view(buf, by, None)
+        blk_d = view(buf, bd, None)
+        x0 = view(buf, bx, 0)
+        y1 = view(buf, by, 1)
+        d0 = view(buf, bd, 0)
+        d1 = view(buf, bd, 1)
         ss, rs = ag_ssem.at[p], ag_rsem.at[p]
 
         def same(ref, i, where):
@@ -319,12 +343,12 @@
         into = [
             blk_x,
             blk_y,
-            buf.at[block(chip * 2 + other, rows), :],
+            view(buf, chip * 2 + other, None),
             d0,
-            buf.at[block(chip_x * 2 + other, rows), :],
+            view(buf, chip_x * 2 + other, None),
             d1,
-            buf.at[block(chip_y * 2 + other, rows), :],
-            buf.at[block(chip_d * 2 + other, rows), :],
+            view(buf, chip_y * 2 + other, None),
+            view(buf, chip_d * 2 + other, None),
         ]
 
         def arrived(i):
@@ -333,9 +357,32 @@
         return sends, arrived
 
     cot[block(s, rows), :] = cotown_ref[...]
-    c_sends, c_arrived = gather_copies(0, cot)
+    c_sends, c_arrived = gather_copies(0, cot, row_view)
     for i in range(3):
         c_sends[i].start()
+
+    counts = [m.shape[0] for m in map_refs]
+    spans = [2 * n if n % 128 else n for n in counts]
+    bases = [sum(spans[:i]) for i in range(8)]
+    stack[...] = jnp.zeros_like(stack)
+    odd = s % 2
+    for m, n, span, base in zip(map_refs, counts, spans, bases):
+        at = base + (odd * n if span != n else 0)
+        stack[pl.ds(pl.multiple_of(at, 64), n), :] = m[...]
+    lane = lax.broadcasted_iota(jnp.int32, (RANK, ADAPT * RANK), 1)
+    column = lax.broadcasted_iota(jnp.int32, (RANK, ADAPT * RANK), 0)
+    picks = []
+    for g in range(planes):
+        picks.append((lane == column + index_ref[g] * RANK).astype(F32))
+        sel[g] = dot_nt(picks[g].astype(BF16), stack[...]).astype(BF16)
+
+    def adapter_copy(k):
+        g = (z + k) % planes
+        return remote(sel.at[g], adm.at[s, z], adz_ssem.at[k - 1], adz_rsem.at[z], (g, s))
+
+    for k in range(1, planes):
+        adapter_copy(k).start()
+    adm[s, z] = sel[z]
 
     x = tok_ref[...].astype(F32)
     mean = jnp.mean(x, axis=-1, keepdims=True)
@@ -344,10 +391,17 @@
     normed[block(s, rows), :] = (
         centred * inv * gain_ref[...].astype(F32) + shift_ref[...].astype(F32)
     ).astype(BF16)
-    n_sends, n_arrived = gather_copies(1, normed)
+    n_sends, n_arrived = gather_copies(1, normed, row_view)
     for i in range(3):
         n_sends[i].start()
-    for sends, arrived in ((c_sends, c_arrived), (n_sends, n_arrived)):
+    for k in range(1, planes):
+        g = (z + k) % planes
+        pltpu.make_async_copy(adm.at[s, g], adm.at[s, g], adz_rsem.at[g]).wait()
+    m_sends, m_arrived = gather_copies(2, adm, lead_view)
+    for i in range(3):
+        m_sends[i].start()
+    gathers = ((c_sends, c_arrived), (n_sends, n_arrived), (m_sends, m_arrived))
+    for sends, arrived in gathers:
         arrived(0)
         sends[3].start()
         sends[4].start()
@@ -355,14 +409,43 @@
         sends[5].start()
         sends[6].start()
     zstep(1)
-    for sends, arrived in ((c_sends, c_arrived), (n_sends, n_arrived)):
+    for sends, arrived in gathers:
         arrived(3)
         arrived(5)
         sends[7].start()
-    for sends, arrived in ((c_sends, c_arrived), (n_sends, n_arrived)):
+    for sends, arrived in gathers:
         for i in (2, 4, 6, 7):
             arrived(i)
     zstep(2)
+
+    def order(f, carry):
+        for pair in range(4):
+
+            def both(i):
+                cols = slice(bases[i], bases[i] + spans[i])
+                return adm[2 * pair, f, :, cols] + adm[2 * pair + 1, f, :, cols]
+
+            where = block(f * 4 + pair, 128)
+            downs_ref[:RANK, where] = both(0)
+            downs_ref[RANK:, where] = both(4)
+            ups_ref[:RANK, where] = both(3)
+            ups_ref[RANK:, where] = both(7)
+            ddown_all[:, where] = both(2)
+            qup_all[:, block(f * 4 + pair, spans[1])] = both(1)
+        return carry
+
+    lax.fori_loop(0, planes, order, 0)
+    for j in range(4):
+        q = s * 4 + j
+        n = counts[5]
+        iup_ref[:, j * n : (j + 1) * n] = adm[q % 8, q // 8, :, bases[5] : bases[5] + n]
+        odown_ref[:, j * n : (j + 1) * n] = adm[q % 8, q // 8, :, bases[6] : bases[6] + n]
+
+    def qup(c):
+        return qup_all[:, pl.ds(pl.multiple_of(c * width + s * mine, mine), mine)]
+
+    def ddown():
+        return ddown_all[:, block(s, mine)]
 
     def low(t, carry):
         r = block(t, TILE)
@@ -385,7 +468,7 @@
         cos = cos_ref[r, :]
         sin = sin_ref[r, :]
         for c in range(3):
-            v = ADAPTER_SCALE * dot(coeff[r, :RANK], qup_ref[:, c * mine : (c + 1) * mine])
+            v = ADAPTER_SCALE * dot(coeff[r, :RANK], qup(c))
             v = v + qb_ref[c : c + 1, block(s, mine)].astype(F32)
             for j in range(planes):
                 v = v + dot(normed[r, j * fan : (j + 1) * fan], wq[j, c])
@@ -395,7 +478,7 @@
             if c == 0:
                 v = v * jnp.asarray(HD**-0.5, BF16)
             qkv[c, r, :] = v
-        g = dot(cgs[r, :RANK], ddown_ref[...])
+        g = dot(cgs[r, :RANK], ddown())
         for j in range(planes):
             g = g + dot_nt(cot[r, j * fan : (j + 1) * fan], wd[j])
         hg[r, :] = g.astype(BF16)
@@ -404,8 +487,9 @@
     lax.fori_loop(0, tiles, project, 0)
     zstep(7)
 
-    dk[...] = jnp.zeros_like(dk)
-    dv[...] = jnp.zeros_like(dv)
+    dk = ag.at[:, pl.ds(0, mine)]
+    dv = ag.at[:, pl.ds(mine, mine)]
+    ag[:, : 2 * mine] = jnp.zeros((length, 2 * mine), F32)
     heads = mine // HD
 
     for b in range(length // BLOCK):
@@ -453,18 +537,126 @@
     cgs_t[...] = (ADAPTER_SCALE * dot_nt(ups_ref[...], cot[...])).astype(BF16)
 
     share = width // 8
-    at_qup = share
-    at_ddown = at_qup + 3 * mine
-    at_dup = at_ddown + mine
-    at_idown = at_dup + share
-    at_iup = at_idown + share
-    at_odown = at_iup + units
-    at_oup = at_odown + units
+
+    def wait_on(ref, sem):
+        pltpu.make_async_copy(ref, ref, sem).wait()
+
+    def hop1(w, msg, h1, start):
+        for j in range(4):
+            to = 4 * (s % 2) + j
+            there = (z, to)
+
+            @pl.when(to != s)
+            def _(j=j, there=there):
+                copy = remote(
+                    msg.at[j], h1.at[s // 2], h1_ssem.at[w, j], h1_rsem.at[w, s // 2], there
+                )
+                if start:
+                    copy.start()
+                else:
+                    copy.wait_send()
+
+            if start:
+
+                @pl.when(to == s)
+                def _(j=j):
+                    pltpu.make_async_copy(
+                        msg.at[j], h1.at[s // 2], h1_rsem.at[w, s // 2]
+                    ).start()
+
+    def hop2_copy(w, h1, h2, k):
+        g = (z + k) % planes
+        return remote(h1.at[g], h2.at[z], h2_ssem.at[w, k - 1], h2_rsem.at[w, z], (g, s))
+
+    def hop2(w, h1, h2):
+        for g in range(planes):
+            wait_on(h1.at[g], h1_rsem.at[w, g])
+        for k in range(1, planes):
+            hop2_copy(w, h1, h2, k).start()
+        h2[z] = h1[z]
+
+    def landed(w, h1, h2):
+        for k in range(1, planes):
+            g = (z + k) % planes
+            wait_on(h2.at[g], h2_rsem.at[w, g])
+        for k in range(1, planes):
+            hop2_copy(w, h1, h2, k).wait_send()
+
+    def place(parts, i, rows_of):
+        full = None
+        for g in range(planes):
+            v = lax.dot_general(
+                parts[g], picks[g], (((0,), (0,)), ((), ())),
+                precision=lax.Precision.HIGHEST, preferred_element_type=F32,
+            )
+            full = v if full is None else full + v
+        grad_refs[i][...] = rows_of(full)
+
+    def half_rows(v):
+        return jnp.where(s % 2 == 0, v[:64], v[64:])
+
+    def all_rows(v):
+        return v
+
     for c in range(3):
-        packed_ref[:, at_qup + c * mine : at_qup + (c + 1) * mine] = ADAPTER_SCALE * dot(
-            coeff_t[:RANK, :], pg[c]
-        )
-    packed_ref[:, at_ddown : at_ddown + mine] = dot(cgs_t[:RANK, :], att[...])
+        g = ADAPTER_SCALE * dot(coeff_t[:RANK, :], pg[c])
+        for i in range(2):
+            qgrad[2 * c + i] = g[:, i * 128 : (i + 1) * 128]
+
+    def qkv_hop1(start):
+        for c in range(3):
+            for i in range(2):
+                t = 16 * c + 2 * s + i
+                for o in range(2):
+                    owner = 2 * (t // 3) + o
+                    slot = t % 3 - o
+                    ok = jnp.logical_and(slot >= 0, slot <= 1)
+                    to = owner % 8
+                    src = qgrad.at[2 * c + i]
+                    n = 4 * c + 2 * i + o
+
+                    @pl.when(jnp.logical_and(ok, to != s))
+                    def _(src=src, owner=owner, slot=slot, to=to, n=n):
+                        copy = remote(
+                            src, q_h1.at[owner // 8, slot], q1_ssem.at[n],
+                            q1_rsem.at[owner // 8, slot], (z, to),
+                        )
+                        if start:
+                            copy.start()
+                        else:
+                            copy.wait_send()
+
+                    if start:
+
+                        @pl.when(jnp.logical_and(ok, to == s))
+                        def _(src=src, owner=owner, slot=slot):
+                            pltpu.make_async_copy(
+                                src, q_h1.at[owner // 8, slot], q1_rsem.at[owner // 8, slot]
+                            ).start()
+
+    def qkv_hop2_copy(k):
+        g = (z + k) % planes
+        return remote(q_h1.at[g], q_h2.at[z], q2_ssem.at[k - 1], q2_rsem.at[z], (g, s))
+
+    def qkv_hop2():
+        for g in range(planes):
+            for slot in range(2):
+                wait_on(q_h1.at[g, slot], q1_rsem.at[g, slot])
+        for k in range(1, planes):
+            qkv_hop2_copy(k).start()
+        q_h2[z] = q_h1[z]
+
+    def qkv_landed():
+        for k in range(1, planes):
+            g = (z + k) % planes
+            wait_on(q_h2.at[g], q2_rsem.at[g])
+        for k in range(1, planes):
+            qkv_hop2_copy(k).wait_send()
+
+    qkv_hop1(True)
+    g = dot(cgs_t[:RANK, :], att[...])
+    for j in range(4):
+        a_msg[j, :, 256:384] = g[:, (j // 2) * 128 : (j // 2 + 1) * 128]
     zstep(10)
 
     k0 = 0.7978845608028654
@@ -483,7 +675,10 @@
         return carry
 
     lax.fori_loop(0, tiles, inner, 0)
-    packed_ref[:, at_odown : at_odown + units] = dot(cgs_t[RANK : 2 * RANK, :], act[...])
+    g = dot(cgs_t[RANK : 2 * RANK, :], act[...])
+    for j in range(4):
+        a_msg[j, :, :256] = g[:, j * 256 : (j + 1) * 256]
+    qkv_hop2()
     zstep(11)
 
     partners = (to_core, to_x, to_y)
@@ -500,7 +695,7 @@
         if i < 3:
             reduce_copy(w, i).start()
 
-    ar_send[0, :RANK, :] = dot_nt(ddown_ref[...], att[...])
+    ar_send[0, :RANK, :] = dot_nt(ddown(), att[...])
     ar_send[0, RANK : 2 * RANK, :] = dot_nt(odown_ref[...], act[...])
     for i in range(4):
         reduce_round(0, i)
@@ -509,8 +704,10 @@
         g = ADAPTER_SCALE * dot(
             coeff_dense[i * RANK : (i + 1) * RANK, :], cot[:, block(s, share)]
         )
-        at = (at_dup, at_oup)[i]
-        packed_ref[:, at : at + share] = g
+        for j in range(4):
+            at = 384 + i * 128
+            a_msg[j, :, at : at + 128] = g[:, (j // 2) * 128 : (j // 2 + 1) * 128]
+    hop1(0, a_msg, a_h1, True)
 
     p_units = width // UNIT
     per = fan // UNIT
@@ -603,7 +800,15 @@
             c_copy(n, i).wait()
         j, i = place_of(n)
         v = keep[q, chip] + c_recv[n, 0].astype(F32) + c_recv[n, 1].astype(F32)
-        res[n // p_units, :, block(j * per + i, UNIT)] = v
+        cols = block(j * per + i, UNIT)
+
+        @pl.when(n < p_units)
+        def _():
+            res[:, cols] = v
+
+        @pl.when(n >= p_units)
+        def _():
+            igrad_ref[:, cols] = v
 
     def pipeline(first, lo, hi, stage0, extra=None):
         def body(n, carry):
@@ -639,7 +844,21 @@
         ag[r, :] = v
         return carry
 
+    hop2(0, a_h1, a_h2)
     lax.fori_loop(0, tiles, act_back, 0)
+    qkv_landed()
+    landed(0, a_h1, a_h2)
+    place([a_h2[g, :, :256] for g in range(planes)], 6, all_rows)
+    place([a_h2[g, :, 256:384] for g in range(planes)], 2, half_rows)
+    place([a_h2[g, :, 384:512] for g in range(planes)], 3, half_rows)
+    place([a_h2[g, :, 512:640] for g in range(planes)], 7, half_rows)
+
+    def qkv_rows(v):
+        return jnp.where(s % 2 == 0, v[:192], v[64:])
+
+    place(
+        [jnp.concatenate([q_h2[g, 0], q_h2[g, 1]], axis=1) for g in range(planes)], 1, qkv_rows
+    )
     for t in range(13, last_step):
         zstep(t)
 
@@ -658,9 +877,9 @@
     lax.fori_loop(0, tiles, act_last, 0)
 
     up_part = dot_nt(iup_ref[...], pgrad[...])
-    q_part = dot_nt(qup_ref[:, :mine], pg[0])
+    q_part = dot_nt(qup(0), pg[0])
     for c in range(1, 3):
-        q_part = q_part + dot_nt(qup_ref[:, c * mine : (c + 1) * mine], pg[c])
+        q_part = q_part + dot_nt(qup(c), pg[c])
     ar_send[1, :RANK, :] = ADAPTER_SCALE * q_part
     ar_send[1, RANK : 2 * RANK, :] = ADAPTER_SCALE * up_part
     reduce_round(1, 0)
@@ -671,34 +890,50 @@
             @pl.when(n == p_units + 2 * i - 1)
             def _(i=i):
                 reduce_round(1, i)
+                if i == 2:
+                    g = ADAPTER_SCALE * dot(coeff_t[RANK : 2 * RANK, :], pgrad[...])
+                    for j in range(4):
+                        b_msg[j, :, :256] = g[:, j * 256 : (j + 1) * 256]
+                if i == 3:
+                    g = dot(ar_send[1].astype(BF16), normed[:, block(s, share)])
+                    for m in range(2):
+                        for j in range(4):
+                            b_msg[j, :, 256 + m * 128 : 384 + m * 128] = g[
+                                m * RANK : (m + 1) * RANK, (j // 2) * 128 : (j // 2 + 1) * 128
+                            ]
+                    hop1(1, b_msg, b_h1, True)
 
     pipeline(early, p_units, total, stage0_back, rounds)
-    packed_ref[:, at_iup : at_iup + units] = ADAPTER_SCALE * dot(
-        coeff_t[RANK : 2 * RANK, :], pgrad[...]
-    )
-    late = ar_send[1].astype(BF16)
-    g = dot(late, normed[:, block(s, share)])
-    packed_ref[:, :share] = g[:RANK]
-    packed_ref[:, at_idown : at_idown + share] = g[RANK:]
+    hop2(1, b_h1, b_h2)
     pipeline(early, total, total + 3, None)
 
     first_t = ar_send[0, :, block(s, rows)].astype(BF16)
     late_t = ar_send[1, :, block(s, rows)].astype(BF16)
-    out = tok_ref[...].astype(F32) + res[0] + ADAPTER_SCALE * dot_tn(first_t, ups_ref[...])
+    out = tok_ref[...].astype(F32) + res[...] + ADAPTER_SCALE * dot_tn(first_t, ups_ref[...])
     out_ref[...] = (out + db_ref[...].astype(F32) + ob_ref[...].astype(F32)).astype(BF16)
     x = tok_ref[...].astype(F32)
     mean = jnp.mean(x, axis=-1, keepdims=True)
     centred = x - mean
     inv = lax.rsqrt(jnp.mean(centred * centred, axis=-1, keepdims=True) + EPSILON)
     xhat = centred * inv
-    e = (res[1] + dot_tn(late_t, downs_ref[...])) * gain_ref[...].astype(F32)
+    e = (igrad_ref[...] + dot_tn(late_t, downs_ref[...])) * gain_ref[...].astype(F32)
     igrad_ref[...] = cotown_ref[...].astype(F32) + inv * (
         e
         - jnp.mean(e, axis=-1, keepdims=True)
         - xhat * jnp.mean(e * xhat, axis=-1, keepdims=True)
     )
 
-    for sends, _ in ((c_sends, None), (n_sends, None)):
+    landed(1, b_h1, b_h2)
+    place([b_h2[g, :, :256] for g in range(planes)], 5, all_rows)
+    place([b_h2[g, :, 256:384] for g in range(planes)], 0, half_rows)
+    place([b_h2[g, :, 384:512] for g in range(planes)], 4, half_rows)
+
+    hop1(0, a_msg, a_h1, False)
+    hop1(1, b_msg, b_h1, False)
+    qkv_hop1(False)
+    for k in range(1, planes):
+        adapter_copy(k).wait_send()
+    for sends, _ in gathers:
         for copy in sends:
             copy.wait_send()
     for c in range(n_chunks):
@@ -718,17 +953,43 @@
     n_chunks = 8 + 2 * (fan // UNIT)
     total = 2 * width // UNIT
     dma = pltpu.SemaphoreType.DMA
-    cols = width // 8 * 4 + 4 * mine + 2 * units
+    maps = args[13:21]
+    lanes = sum(2 * m.shape[0] if m.shape[0] % 128 else m.shape[0] for m in maps)
+
+    def entry(*refs):
+        layer_kernel(planes, *refs[:13], refs[13:21], *refs[21:25], refs[25:33], *refs[33:])
+
     return pl.pallas_call(
-        functools.partial(layer_kernel, planes),
+        entry,
         out_shape=(
             jax.ShapeDtypeStruct((rows, width), BF16),
             jax.ShapeDtypeStruct((rows, width), F32),
-            jax.ShapeDtypeStruct((RANK, cols), F32),
+            *(jax.ShapeDtypeStruct(m.shape, F32) for m in maps),
         ),
-        in_specs=[vm, vm, hbm, hbm, hbm, hbm] + [vm] * 14,
-        out_specs=(vm, vm, vm),
+        in_specs=[vm, vm, hbm, hbm, hbm, hbm]
+        + [vm] * 6
+        + [pl.BlockSpec(memory_space=pltpu.SMEM)]
+        + [vm] * 10,
+        out_specs=(vm,) * 10,
         scratch_shapes=[
+            pltpu.VMEM((lanes, ADAPT * RANK), BF16),
+            pltpu.VMEM((planes, RANK, lanes), BF16),
+            pltpu.VMEM((8, planes, RANK, lanes), BF16),
+            pltpu.VMEM((2 * RANK, width), BF16),
+            pltpu.VMEM((2 * RANK, width), BF16),
+            pltpu.VMEM((RANK, width), BF16),
+            pltpu.VMEM((RANK, 3 * width), BF16),
+            pltpu.VMEM((RANK, units), BF16),
+            pltpu.VMEM((RANK, units), BF16),
+            pltpu.VMEM((6, RANK, 128), F32),
+            pltpu.VMEM((4, RANK, 640), F32),
+            pltpu.VMEM((planes, RANK, 640), F32),
+            pltpu.VMEM((planes, RANK, 640), F32),
+            pltpu.VMEM((4, RANK, 512), F32),
+            pltpu.VMEM((planes, RANK, 512), F32),
+            pltpu.VMEM((planes, RANK, 512), F32),
+            pltpu.VMEM((planes, 2, RANK, 128), F32),
+            pltpu.VMEM((planes, 2, RANK, 128), F32),
             pltpu.VMEM((length, width), BF16),
             pltpu.VMEM((length, width), BF16),
             pltpu.VMEM((planes, 3, fan, mine), BF16),
@@ -738,8 +999,6 @@
             pltpu.VMEM((3, length, mine), BF16),
             pltpu.VMEM((length, mine), BF16),
             pltpu.VMEM((length, mine), BF16),
-            pltpu.VMEM((length, mine), F32),
-            pltpu.VMEM((length, mine), F32),
             pltpu.VMEM((3, length, mine), BF16),
             pltpu.VMEM((BLOCK, mine), F32),
             pltpu.VMEM((BLOCK, mine), F32),
@@ -751,7 +1010,7 @@
             pltpu.VMEM((length, 2 * RANK), BF16),
             pltpu.VMEM((2 * RANK, length), BF16),
             pltpu.VMEM((2 * RANK, length), BF16),
-            pltpu.VMEM((2, rows, width), F32),
+            pltpu.VMEM((rows, width), F32),
             pltpu.VMEM((4, 4, rows, UNIT), F32),
             pltpu.VMEM((2, 4, rows, UNIT), BF16),
             pltpu.VMEM((total, 4, rows, UNIT), BF16),
@@ -764,8 +1023,8 @@
             dma((n_chunks,)),
             dma((n_chunks, 2, planes)),
             dma((n_chunks, planes)),
-            dma((2, 8)),
-            dma((2, 8)),
+            dma((3, 8)),
+            dma((3, 8)),
             dma((2,)),
             dma((total,)),
             dma((2, 2)),
@@ -774,6 +1033,16 @@
             dma((total, 2)),
             dma((2, 3)),
             dma((2, 3)),
+            dma((planes,)),
+            dma((planes,)),
+            dma((2, 4)),
+            dma((2, planes)),
+            dma((2, planes)),
+            dma((2, planes)),
+            dma((12,)),
+            dma((planes, 2)),
+            dma((planes,)),
+            dma((planes,)),
         ],
         compiler_params=pltpu.CompilerParams(
             collective_id=0, has_side_effects=True, vmem_limit_bytes=63 * 1024 * 1024
@@ -785,12 +1054,12 @@
     rows, width, length, units, mine = shapes
     return (
         groups == 8
-        and planes > 1
+        and planes == 4
         and rows * 2 == TILE
         and length <= 1024
-        and width % (planes * UNIT) == 0
-        and mine % 128 == 0
-        and units % 256 == 0
+        and width == 2048
+        and mine == 256
+        and units == 1024
     )
 
 
@@ -849,6 +1118,30 @@
     units = inner_weight.shape[1]
     s = lax.axis_index("seq")
 
+    shapes = (rows, width, length, units, mine)
+    if fits(planes, groups, shapes):
+        return run_layer(
+            planes,
+            (
+                tokens,
+                cotangent,
+                qkv_weight,
+                dense_weight,
+                inner_weight,
+                outer_weight,
+                qkv_bias.reshape(3, width),
+                dense_bias[None],
+                inner_bias[None],
+                outer_bias[None],
+                norm_gain[None],
+                norm_bias[None],
+                adapter_index,
+                *maps,
+                *rope_constants(length),
+            ),
+            shapes,
+        )
+
     counts = [m.shape[0] for m in maps]
     stacked = jnp.concatenate(maps, axis=0)
     wanted = (adapter_index[:, None] * RANK + jnp.arange(RANK)[None, :]).reshape(-1)
@@ -873,40 +1166,6 @@
     dense_down = own(dense_down, mine)
     inner_up = own(inner_up, units)
     outer_down = own(outer_down, units)
-
-    shapes = (rows, width, length, units, mine)
-    if fits(planes, groups, shapes):
-        cos, sin = rope_constants(length)
-        layer_out, input_grad, packed = run_layer(
-            planes,
-            (
-                tokens,
-                cotangent,
-                qkv_weight,
-                dense_weight,
-                inner_weight,
-                outer_weight,
-                qkv_bias.reshape(3, width),
-                dense_bias[None],
-                inner_bias[None],
-                outer_bias[None],
-                norm_gain[None],
-                norm_bias[None],
-                jnp.concatenate([qkv_down, inner_down], axis=0),
-                jnp.concatenate([dense_up, outer_up], axis=0),
-                qkv_up,
-                dense_down,
-                inner_up,
-                outer_down,
-                cos,
-                sin,
-            ),
-            shapes,
-        )
-        sizes = [width // groups, 3 * mine, mine, width // groups, width // groups]
-        sizes += [units, units, width // groups]
-        outs = deliver(packed, sizes, counts, pick, planes, groups)
-        return (layer_out, input_grad, *outs)
 
     wqkv = lax.all_gather(qkv_weight, "fsdp", axis=1, tiled=True)
     wdense = lax.all_gather(dense_weight, "fsdp", axis=1, tiled=True)

time: 393 us -> 312 us (0.79)
  waiting for transfers between devices: 51.2 us -> 0 us
  Pallas kernels: 277 us -> 298 us
  local copies, waits for them, and re-layouts: 29.4 us -> 13 us
  between operations: 14.5 us -> 0.69 us
  blocking collectives: 12.3 us -> 0 us
  starting transfers between devices: 4.68 us -> 0 us
    all_gather x2 -> x0, waiting for transfers between devices: 41.9 us -> none  [the longest x1 27 us: deliver(): everyone = lax.all_gather(packed, 'seq', axis=0, tiled=False)]
    pallas_call x1, Pallas kernels: 277 us -> 298 us  [run_layer(): pl.pallas_call(entry, out_shape=(jax.ShapeDtypeStruct((rows, width), BF16...]
    all_to_all x1 -> x0, blocking collectives: 12.3 us -> none  [on_device(): lax.all_to_all(chosen, 'fsdp', split_axis=0, concat_axis=0, tiled=True)]
    all_to_all x1 -> x0, waiting for transfers between devices: 9.32 us -> none  [deliver(): lax.all_to_all(owned, 'fsdp', split_axis=0, concat_axis=0, tiled=True)]
    all_to_all x1 -> x0, starting transfers between devices: 4.6 us -> none  [deliver(): lax.all_to_all(owned, 'fsdp', split_axis=0, concat_axis=0, tiled=True)]
    slice x7 -> x0, local copies, waits for them, and re-layouts: 4.49 us -> none  [the longest x3 2.45 us: deliver(): part = everyone[:, :, at:at + w]]
    unnamed x25 -> x38, local copies, waits for them, and re-layouts: 8.17 us -> 8.69 us
  transfers between devices with their start and end apart: 3 -> 0, of which waited for: 3 -> 0; matrix products, arithmetic and copies ran while one was open for 2% -> 0% of each run, Pallas kernels for 0% -> 0%
where the time goes in v3:
time: 312 us; the launch traced here: 311 us
  Pallas kernels  298 us (96%)
  local copies, waits for them, and re-layouts  13 us (4%)
    pallas_call x1, Pallas kernels, run_layer(): pl.pallas_call(entry, out_shape=(jax.ShapeDtypeStruct((rows, width), BF16...  298 us
    unnamed x38, local copies, waits for them, and re-layouts  8.69 us

profile of v3, /device:TPU:0, one launch (start us, length us, event | category | flops | bytes accessed | tf_op | source)
XLA Modules:
  0.0 311.3 jit_solution(5058943460278937596)
XLA Ops:
  0.6 0.0 copy-start.11
  0.7 1.3 broadcast_in_dim.15.refs_7_
  1.9 0.0 copy-done.11
  2.0 0.0 copy-start.12
  2.0 0.0 copy-start.13
  2.0 0.6 broadcast_in_dim.17.refs_9_
  2.6 0.1 copy-done.12
  2.6 0.0 copy-start.10
  2.6 0.6 broadcast_in_dim.18.refs_10_
  3.3 0.0 copy-done.13
  3.3 0.6 broadcast_in_dim.19.refs_11_
  3.9 0.0 copy-done.10
  3.9 0.0 copy-start.9
  3.9 0.6 reshape.23.refs_6_
  4.5 0.1 copy-done.9
  4.6 0.6 broadcast_in_dim.16.refs_8_
  5.2 297.6 %shard_map.294 = (bf16[128,2048]{1,0:T(8,128)(2,1)}, f32[128,2048]{1,0:T(8,128)}, f32[64,128]{1,0:T(8,128)}, f32[192,128]{1,0:T(8,128)}, f32[64,128]{1,0:T(8,128...) custom-call(bf16[128,2048]{1,0:T(8,128)(2,1)} %refs_0_.1, ...), custom_call_target="tpu_custom_call" | custom-call | tf_op jit(solution)/shard_map/pallas_call | solution.py:962
  302.8 0.0 copy-start
  302.8 2.0 copy.43
  304.8 0.0 copy-done
  304.8 0.0 copy-start.8
  304.8 0.0 copy-start.3
  304.8 1.0 copy.44
  305.8 0.0 copy-done.8
  305.8 0.6 copy.45
  306.4 0.0 copy-done.3
  306.4 0.0 copy-start.7
  306.4 0.0 copy-start.6
  306.4 0.0 copy-start.5
  306.4 0.6 copy.46
  307.0 0.1 copy-done.7
  307.2 0.0 copy-start.2
  307.2 0.6 copy.47
  307.8 0.0 copy-done.6
  307.8 0.6 copy.48
  308.4 0.0 copy-done.5
  308.4 0.6 copy.49
  309.0 0.0 copy-done.2
  309.0 0.0 copy-start.1
  309.0 0.7 copy.50
  309.7 0.3 copy-done.1
  310.0 0.0 copy-start.4
  310.0 0.7 copy.51
  310.6 0.1 copy-done.4
  310.7 0.6 copy.52
Async XLA Ops:
  0.6 1.3 copy-start.11
  2.0 0.7 copy-start.12
  2.0 1.3 copy-start.13
  2.6 1.2 copy-start.10
  3.9 0.7 copy-start.9
  302.8 2.0 copy-start
  304.8 1.0 copy-start.8
  304.8 1.6 copy-start.3
  306.4 0.8 copy-start.7
  306.4 1.4 copy-start.6
  306.4 2.0 copy-start.5
  307.2 1.9 copy-start.2
  309.0 1.0 copy-start.1
  310.0 0.8 copy-start.4

commit v4 on v3

--- a/solution.py
+++ b/solution.py
@@ -58,6 +58,8 @@
 MESH = pl.DeviceIdType.MESH
 TILE = 256
 UNIT = 256
+PART = 128
+ALL = slice(None)
 
 
 def rope_constants(length):
@@ -209,6 +211,9 @@
             device_id_type=MESH,
         )
 
+    def line(ref, cols):
+        return ref[cols].astype(F32)[None, :]
+
     def block(i, n):
         return pl.ds(pl.multiple_of(i * n, n), n)
 
@@ -231,18 +236,15 @@
                 lambda j, i=i: wi.at[j, pl.ds(i * part, part), :],
             )
         )
-    deep = units // 2
-    for j2 in range(fan // UNIT):
-        for i in range(2):
-            chunks.append(
-                (
-                    wo_in.at[pl.ds(i * deep, deep), pl.ds(j2 * UNIT, UNIT)],
-                    lambda j, i=i, j2=j2: wo.at[
-                        j, pl.ds(i * deep, deep), pl.ds(j2 * UNIT, UNIT)
-                    ],
-                )
+    for i in range(fan // PART):
+        chunks.append(
+            (
+                wo_in.at[:, pl.ds(i * PART, PART)],
+                lambda j, i=i: wo.at[j, :, pl.ds(i * PART, PART)],
             )
+        )
     n_chunks = len(chunks)
+    ahead = 2
     last_step = n_chunks + planes - 1
 
     def zcopy(c, direction, k):
@@ -268,28 +270,38 @@
             def _(direction=direction):
                 zcopy(c, direction, k).start()
 
-    def zwait(c, k):
+    def zarrived(c, j):
+        place = chunks[c][1](j)
+        pltpu.make_async_copy(place, place, zr_sem.at[c, j]).wait()
+
+    def zrelay(c, k):
         for direction in (0, 1):
-            j = z - k if direction == 0 else z + k
-            there = z - k >= 0 if direction == 0 else z + k < planes
-
-            @pl.when(there)
-            def _(j=j, direction=direction):
-                place = chunks[c][1](j)
-                pltpu.make_async_copy(place, place, zr_sem.at[c, j]).wait()
+
+            @pl.when(zhas(direction, k))
+            def _(direction=direction):
+                zarrived(c, z - k if direction == 0 else z + k)
+                zcopy(c, direction, k).start()
+
+    def zfinish(first, last):
+        for c in range(first, last):
+            for direction in (0, 1):
+                for k in range(1, planes):
+                    j = z - k if direction == 0 else z + k
+                    here = z == planes - 1 if direction == 0 else z == 0
+
+                    @pl.when(here)
+                    def _(c=c, j=j):
+                        zarrived(c, j)
 
     def zstep(t):
         if t == 0:
-            zsend(0, 0)
-            zsend(1, 0)
-        elif t + 1 < n_chunks:
-            zsend(t + 1, 0)
-        for k in range(1, planes):
-            c = t - k
-            if 0 <= c < n_chunks:
-                zwait(c, k)
-                if k < planes - 1:
-                    zsend(c, k)
+            for c in range(min(ahead, n_chunks - 1) + 1):
+                zsend(c, 0)
+        elif t + ahead < n_chunks:
+            zsend(t + ahead, 0)
+        for k in range(1, planes - 1):
+            if 0 <= t - k < n_chunks:
+                zrelay(t - k, k)
 
     own = []
     for c in range(n_chunks):
@@ -389,7 +401,7 @@
     centred = x - mean
     inv = lax.rsqrt(jnp.mean(centred * centred, axis=-1, keepdims=True) + EPSILON)
     normed[block(s, rows), :] = (
-        centred * inv * gain_ref[...].astype(F32) + shift_ref[...].astype(F32)
+        centred * inv * line(gain_ref, ALL) + line(shift_ref, ALL)
     ).astype(BF16)
     n_sends, n_arrived = gather_copies(1, normed, row_view)
     for i in range(3):
@@ -401,22 +413,28 @@
     for i in range(3):
         m_sends[i].start()
     gathers = ((c_sends, c_arrived), (n_sends, n_arrived), (m_sends, m_arrived))
-    for sends, arrived in gathers:
+    zstep(1)
+    for m, (sends, arrived) in enumerate(gathers):
         arrived(0)
         sends[3].start()
         sends[4].start()
         arrived(1)
         sends[5].start()
         sends[6].start()
-    zstep(1)
-    for sends, arrived in gathers:
+        if m == 0:
+            zstep(2)
+        if m == 2:
+            zstep(3)
+    for m, (sends, arrived) in enumerate(gathers):
         arrived(3)
         arrived(5)
         sends[7].start()
+        if m == 0:
+            zstep(4)
     for sends, arrived in gathers:
         for i in (2, 4, 6, 7):
             arrived(i)
-    zstep(2)
+    zstep(5)
 
     def order(f, carry):
         for pair in range(4):
@@ -458,10 +476,8 @@
     lax.fori_loop(0, tiles, low, 0)
     for copy in own:
         copy.wait()
-    zstep(3)
-    zstep(4)
-    zstep(5)
     zstep(6)
+    zfinish(0, 4)
 
     def project(t, carry):
         r = block(t, TILE)
@@ -469,7 +485,7 @@
         sin = sin_ref[r, :]
         for c in range(3):
             v = ADAPTER_SCALE * dot(coeff[r, :RANK], qup(c))
-            v = v + qb_ref[c : c + 1, block(s, mine)].astype(F32)
+            v = v + line(qb_ref, pl.ds(pl.multiple_of(c * width + s * mine, mine), mine))
             for j in range(planes):
                 v = v + dot(normed[r, j * fan : (j + 1) * fan], wq[j, c])
             if c < 2:
@@ -521,8 +537,12 @@
         att[lo:hi, :] = acc_a[...].astype(BF16)
         back = (acc_b[...] * (HD**-0.5)).astype(BF16).astype(F32)
         pg[0, lo:hi, :] = turn_all(back, cos_ref[lo:hi, :], sin_ref[lo:hi, :], -1.0).astype(BF16)
-        if b % 2 == 1:
-            zstep(8 + b // 2)
+        if b == 1:
+            zstep(8)
+        if b == 2:
+            zstep(9)
+        if b == 3:
+            zstep(10)
 
     def finish(t, carry):
         r = block(t, TILE)
@@ -657,7 +677,9 @@
     g = dot(cgs_t[:RANK, :], att[...])
     for j in range(4):
         a_msg[j, :, 256:384] = g[:, (j // 2) * 128 : (j // 2 + 1) * 128]
-    zstep(10)
+    pass
+    zfinish(4, 8)
+    zstep(11)
 
     k0 = 0.7978845608028654
     k1 = 0.044715
@@ -665,7 +687,7 @@
     def inner(t, carry):
         r = block(t, TILE)
         v = ADAPTER_SCALE * dot(coeff[r, RANK : 2 * RANK], iup_ref[...])
-        v = v + ib_ref[:, block(s, units)].astype(F32)
+        v = v + line(ib_ref, block(s, units))
         for j in range(planes):
             v = v + dot(normed[r, j * fan : (j + 1) * fan], wi[j])
         sq = v * v
@@ -679,7 +701,7 @@
     for j in range(4):
         a_msg[j, :, :256] = g[:, j * 256 : (j + 1) * 256]
     qkv_hop2()
-    zstep(11)
+    zstep(12)
 
     partners = (to_core, to_x, to_y)
 
@@ -699,6 +721,7 @@
     ar_send[0, RANK : 2 * RANK, :] = dot_nt(odown_ref[...], act[...])
     for i in range(4):
         reduce_round(0, i)
+        pass
     coeff_dense = ar_send[0].astype(BF16)
     for i in range(2):
         g = ADAPTER_SCALE * dot(
@@ -711,21 +734,21 @@
 
     p_units = width // UNIT
     per = fan // UNIT
-    early = p_units - planes
+    early = p_units - planes // 2
     total = 2 * p_units
 
-    def place_of(n):
-        first = n < p_units
-        j = jnp.where(first, n % planes, (n - p_units) // per)
-        i = jnp.where(first, n // planes, (n - p_units) % per)
-        return j, i
+    def branch_place(n):
+        return (n % (planes // 2)) * 2, n // (planes // 2)
+
+    def back_place(n):
+        return (n - p_units) // per, (n - p_units) % per
 
     def keep_split(n, k, r):
         slot = n % 2
         a = r[:rows, :]
         b = r[rows:, :]
         first = core == 0
-        keep[n % 4, k] = jnp.where(first, a, b)
+        keep[n % 6, k] = jnp.where(first, a, b)
         s1_send[slot, k] = jnp.where(first, b, a).astype(BF16)
 
     def s1_copy(n):
@@ -733,32 +756,34 @@
 
     def a_copy(n, i):
         return remote(
-            a_send.at[n % 2, i], a_recv.at[n, i], a_ssem.at[n % 2, i], a_rsem.at[n, i],
+            a_send.at[n % 3, i], a_recv.at[n, i], a_ssem.at[n % 3, i], a_rsem.at[n, i],
             (to_x, to_y)[i],
         )
 
     def c_copy(n, i):
         return remote(
-            c_send.at[n % 2, i], c_recv.at[n, i], c_ssem.at[n % 2, i], c_rsem.at[n, i],
+            c_send.at[n % 3, i], c_recv.at[n, i], c_ssem.at[n % 3, i], c_rsem.at[n, i],
             (to_x, to_y)[i],
         )
 
     hu = UNIT // 2
 
     def stage0_branch(n):
-        j, i = place_of(n)
+        j, i = branch_place(n)
 
         def tile(k, carry):
             r = block(k, TILE)
-            cols = block(i, UNIT)
-            keep_split(n, k, dot(act[r, :], wo[j, :, cols]) + dot(att[r, :], wd[j, :, cols]))
+            cols = block(i, PART)
+            w_o = jnp.concatenate([wo[j, :, cols], wo[j + 1, :, cols]], axis=1)
+            w_d = jnp.concatenate([wd[j, :, cols], wd[j + 1, :, cols]], axis=1)
+            keep_split(n, k, dot(act[r, :], w_o) + dot(att[r, :], w_d))
             return carry
 
         lax.fori_loop(0, tiles, tile, 0)
         s1_copy(n).start()
 
     def stage0_back(n):
-        j, i = place_of(n)
+        j, i = back_place(n)
 
         def tile(k, carry):
             r = block(k, TILE)
@@ -774,51 +799,53 @@
 
     def stage1(n):
         s1_copy(n).wait()
-        q = n % 4
+        q = n % 6
         for k in range(4):
             keep[q, k] += s1_recv[n, k].astype(F32)
         far = keep[q, chip_d]
-        a_send[n % 2, 0] = far[:, :hu].astype(BF16)
-        a_send[n % 2, 1] = far[:, hu:].astype(BF16)
+        a_send[n % 3, 0] = far[:, :hu].astype(BF16)
+        a_send[n % 3, 1] = far[:, hu:].astype(BF16)
         for i in range(2):
             a_copy(n, i).start()
 
     def stage2(n):
-        q = n % 4
+        q = n % 6
         for i in range(2):
             a_copy(n, i).wait()
         keep[q, chip_y, :, :hu] += a_recv[n, 0].astype(F32)
         keep[q, chip_x, :, hu:] += a_recv[n, 1].astype(F32)
-        c_send[n % 2, 0] = keep[q, chip_x].astype(BF16)
-        c_send[n % 2, 1] = keep[q, chip_y].astype(BF16)
+        c_send[n % 3, 0] = keep[q, chip_x].astype(BF16)
+        c_send[n % 3, 1] = keep[q, chip_y].astype(BF16)
         for i in range(2):
             c_copy(n, i).start()
 
     def stage3(n):
-        q = n % 4
+        q = n % 6
         for i in range(2):
             c_copy(n, i).wait()
-        j, i = place_of(n)
         v = keep[q, chip] + c_recv[n, 0].astype(F32) + c_recv[n, 1].astype(F32)
-        cols = block(j * per + i, UNIT)
 
         @pl.when(n < p_units)
         def _():
-            res[:, cols] = v
+            j, i = branch_place(n)
+            for m in range(2):
+                res[:, pl.ds(pl.multiple_of((j + m) * fan + i * PART, PART), PART)] = v[
+                    :, m * PART : (m + 1) * PART
+                ]
 
         @pl.when(n >= p_units)
         def _():
-            igrad_ref[:, cols] = v
+            igrad_ref[:, block(n - p_units, UNIT)] = v
 
     def pipeline(first, lo, hi, stage0, extra=None):
         def body(n, carry):
             if stage0 is not None:
                 stage0(n)
-            for back, stage in ((1, stage1), (2, stage2), (3, stage3)):
+            for back, stage in ((1, stage1), (3, stage2), (5, stage3)):
                 m = n - back
                 ok = m >= first
                 if stage0 is None:
-                    ok = jnp.logical_and(ok, m < hi - 3)
+                    ok = jnp.logical_and(ok, m < hi - 5)
 
                 @pl.when(ok)
                 def _(m=m, stage=stage):
@@ -830,17 +857,23 @@
 
         lax.fori_loop(lo, hi, body, 0)
 
-    zstep(12)
-    pipeline(0, 0, early, stage0_branch)
-    pipeline(0, early, early + 3, None)
+    zstep(13)
+    zfinish(8, 10)
+    pass
+    per_part = planes // 2
+    pipeline(0, 0, 2 * per_part, stage0_branch)
+
+    def act_part(r, i):
+        cols = [slice(j * fan + i * PART, j * fan + (i + 1) * PART) for j in range(planes)]
+        g = jnp.concatenate([cot[r, c] for c in cols], axis=1)
+        w = [wo[j, :, i * PART : (i + 1) * PART] for j in range(planes)]
+        return dot_nt(g, jnp.concatenate(w, axis=1))
 
     def act_back(t, carry):
         r = block(t, TILE)
         v = dot(cgs[r, RANK : 2 * RANK], odown_ref[...])
-        for j in range(planes):
-            for i in range(per - 1):
-                c0 = j * fan + i * UNIT
-                v = v + dot_nt(cot[r, c0 : c0 + UNIT], wo[j, :, i * UNIT : (i + 1) * UNIT])
+        for i in range(2):
+            v = v + act_part(r, i)
         ag[r, :] = v
         return carry
 
@@ -859,18 +892,23 @@
     place(
         [jnp.concatenate([q_h2[g, 0], q_h2[g, 1]], axis=1) for g in range(planes)], 1, qkv_rows
     )
-    for t in range(13, last_step):
-        zstep(t)
-
-    pipeline(early, early, p_units, stage0_branch)
+    pass
+    zfinish(10, 11)
+    pipeline(0, 2 * per_part, early, stage0_branch)
+
+    def act_more(t, carry):
+        r = block(t, TILE)
+        ag[r, :] += act_part(r, 2)
+        return carry
+
+    lax.fori_loop(0, tiles, act_more, 0)
+    zfinish(11, 12)
+
+    pipeline(0, early, p_units, stage0_branch)
 
     def act_last(t, carry):
         r = block(t, TILE)
-        v = ag[r, :]
-        for j in range(planes):
-            i = per - 1
-            c0 = j * fan + i * UNIT
-            v = v + dot_nt(cot[r, c0 : c0 + UNIT], wo[j, :, i * UNIT : (i + 1) * UNIT])
+        v = ag[r, :] + act_part(r, fan // PART - 1)
         pgrad[r, :] = (v * pre[r, :]).astype(BF16)
         return carry
 
@@ -903,20 +941,20 @@
                             ]
                     hop1(1, b_msg, b_h1, True)
 
-    pipeline(early, p_units, total, stage0_back, rounds)
+    pipeline(0, p_units, total, stage0_back, rounds)
     hop2(1, b_h1, b_h2)
-    pipeline(early, total, total + 3, None)
+    pipeline(0, total, total + 5, None)
 
     first_t = ar_send[0, :, block(s, rows)].astype(BF16)
     late_t = ar_send[1, :, block(s, rows)].astype(BF16)
     out = tok_ref[...].astype(F32) + res[...] + ADAPTER_SCALE * dot_tn(first_t, ups_ref[...])
-    out_ref[...] = (out + db_ref[...].astype(F32) + ob_ref[...].astype(F32)).astype(BF16)
+    out_ref[...] = (out + line(db_ref, ALL) + line(ob_ref, ALL)).astype(BF16)
     x = tok_ref[...].astype(F32)
     mean = jnp.mean(x, axis=-1, keepdims=True)
     centred = x - mean
     inv = lax.rsqrt(jnp.mean(centred * centred, axis=-1, keepdims=True) + EPSILON)
     xhat = centred * inv
-    e = (igrad_ref[...] + dot_tn(late_t, downs_ref[...])) * gain_ref[...].astype(F32)
+    e = (igrad_ref[...] + dot_tn(late_t, downs_ref[...])) * line(gain_ref, ALL)
     igrad_ref[...] = cotown_ref[...].astype(F32) + inv * (
         e
         - jnp.mean(e, axis=-1, keepdims=True)
@@ -950,7 +988,7 @@
     fan = width // planes
     vm = pl.BlockSpec(memory_space=pltpu.VMEM)
     hbm = pl.BlockSpec(memory_space=pl.ANY)
-    n_chunks = 8 + 2 * (fan // UNIT)
+    n_chunks = 8 + fan // PART
     total = 2 * width // UNIT
     dma = pltpu.SemaphoreType.DMA
     maps = args[13:21]
@@ -1011,12 +1049,12 @@
             pltpu.VMEM((2 * RANK, length), BF16),
             pltpu.VMEM((2 * RANK, length), BF16),
             pltpu.VMEM((rows, width), F32),
-            pltpu.VMEM((4, 4, rows, UNIT), F32),
+            pltpu.VMEM((6, 4, rows, UNIT), F32),
             pltpu.VMEM((2, 4, rows, UNIT), BF16),
             pltpu.VMEM((total, 4, rows, UNIT), BF16),
-            pltpu.VMEM((2, 2, rows, UNIT // 2), BF16),
+            pltpu.VMEM((3, 2, rows, UNIT // 2), BF16),
             pltpu.VMEM((total, 2, rows, UNIT // 2), BF16),
-            pltpu.VMEM((2, 2, rows, UNIT), BF16),
+            pltpu.VMEM((3, 2, rows, UNIT), BF16),
             pltpu.VMEM((total, 2, rows, UNIT), BF16),
             pltpu.VMEM((2, 2 * RANK, length), F32),
             pltpu.VMEM((2, 3, 2 * RANK, length), F32),
@@ -1027,9 +1065,9 @@
             dma((3, 8)),
             dma((2,)),
             dma((total,)),
-            dma((2, 2)),
+            dma((3, 2)),
             dma((total, 2)),
-            dma((2, 2)),
+            dma((3, 2)),
             dma((total, 2)),
             dma((2, 3)),
             dma((2, 3)),
@@ -1129,12 +1167,12 @@
                 dense_weight,
                 inner_weight,
                 outer_weight,
-                qkv_bias.reshape(3, width),
-                dense_bias[None],
-                inner_bias[None],
-                outer_bias[None],
-                norm_gain[None],
-                norm_bias[None],
+                qkv_bias,
+                dense_bias,
+                inner_bias,
+                outer_bias,
+                norm_gain,
+                norm_bias,
                 adapter_index,
                 *maps,
                 *rope_constants(length),

time: 312 us -> 280 us (0.90)
  Pallas kernels: 298 us -> 271 us
  local copies, waits for them, and re-layouts: 13 us -> 8.49 us
    pallas_call x1, Pallas kernels: 298 us -> 271 us  [run_layer(): pl.pallas_call(entry, out_shape=(jax.ShapeDtypeStruct((rows, width), BF16...]
    broadcast_in_dim x5 -> x0, local copies, waits for them, and re-layouts: 3.74 us -> none  [the longest x1 1.3 us: on_device(): dense_bias[None]]
    unnamed x38 -> x28, local copies, waits for them, and re-layouts: 8.69 us -> 8.49 us
where the time goes in v4:
time: 280 us
  Pallas kernels  271 us (97%)
  local copies, waits for them, and re-layouts  8.49 us (3%)
    pallas_call x1, Pallas kernels, run_layer(): pl.pallas_call(entry, out_shape=(jax.ShapeDtypeStruct((rows, width), BF16...  271 us
    unnamed x28, local copies, waits for them, and re-layouts  8.49 us

profile of v4, /device:TPU:0, one launch (start us, length us, event | category | flops | bytes accessed | tf_op | source)
XLA Modules:
  0.0 280.0 jit_solution(7291464340751824579)
XLA Ops:
  0.7 270.8 %shard_map.294 = (bf16[128,2048]{1,0:T(8,128)(2,1)}, f32[128,2048]{1,0:T(8,128)}, f32[64,128]{1,0:T(8,128)}, f32[192,128]{1,0:T(8,128)}, f32[64,128]{1,0:T(8,128...) custom-call(bf16[128,2048]{1,0:T(8,128)(2,1)} %refs_0_.1, ...), custom_call_target="tpu_custom_call" | custom-call | tf_op jit(solution)/shard_map/pallas_call | solution.py:1000
  271.5 0.0 copy-start
  271.5 2.0 copy.43
  273.5 0.0 copy-done
  273.5 0.0 copy-start.8
  273.5 0.0 copy-start.3
  273.5 1.0 copy.44
  274.4 0.0 copy-done.8
  274.4 0.6 copy.45
  275.1 0.0 copy-done.3
  275.1 0.0 copy-start.7
  275.1 0.0 copy-start.6
  275.1 0.0 copy-start.5
  275.1 0.6 copy.46
  275.7 0.1 copy-done.7
  275.8 0.0 copy-start.2
  275.8 0.6 copy.47
  276.4 0.0 copy-done.6
  276.4 0.6 copy.48
  277.1 0.0 copy-done.5
  277.1 0.6 copy.49
  277.7 0.0 copy-done.2
  277.7 0.0 copy-start.1
  277.7 0.7 copy.50
  278.3 0.3 copy-done.1
  278.6 0.0 copy-start.4
  278.6 0.7 copy.51
  279.3 0.1 copy-done.4
  279.4 0.6 copy.52
Async XLA Ops:
  271.5 2.0 copy-start
  273.5 1.0 copy-start.8
  273.5 1.6 copy-start.3
  275.1 0.8 copy-start.7
  275.1 1.4 copy-start.6
  275.1 2.0 copy-start.5
  275.8 1.9 copy-start.2
  277.7 1.0 copy-start.1
  278.6 0.8 copy-start.4

commit v5 on v4

--- a/solution.py
+++ b/solution.py
@@ -164,6 +164,8 @@
     c_recv,
     ar_send,
     ar_recv,
+    ar_low,
+    ar_recv_low,
     local_sem,
     zs_sem,
     zr_sem,
@@ -307,10 +309,9 @@
     for c in range(n_chunks):
         src, place = chunks[c]
         own.append(pltpu.make_async_copy(src, place(z), local_sem.at[c]))
+    zstep(0)
     for copy in own:
         copy.start()
-
-    zstep(0)
 
     half = width // 2
 
@@ -404,14 +405,10 @@
         centred * inv * line(gain_ref, ALL) + line(shift_ref, ALL)
     ).astype(BF16)
     n_sends, n_arrived = gather_copies(1, normed, row_view)
-    for i in range(3):
-        n_sends[i].start()
     for k in range(1, planes):
         g = (z + k) % planes
         pltpu.make_async_copy(adm.at[s, g], adm.at[s, g], adz_rsem.at[g]).wait()
     m_sends, m_arrived = gather_copies(2, adm, lead_view)
-    for i in range(3):
-        m_sends[i].start()
     gathers = ((c_sends, c_arrived), (n_sends, n_arrived), (m_sends, m_arrived))
     zstep(1)
     for m, (sends, arrived) in enumerate(gathers):
@@ -421,16 +418,15 @@
         arrived(1)
         sends[5].start()
         sends[6].start()
-        if m == 0:
-            zstep(2)
-        if m == 2:
-            zstep(3)
+        if m < 2:
+            for i in range(3):
+                gathers[m + 1][0][i].start()
+            zstep(m + 2)
+    zstep(4)
     for m, (sends, arrived) in enumerate(gathers):
         arrived(3)
         arrived(5)
         sends[7].start()
-        if m == 0:
-            zstep(4)
     for sends, arrived in gathers:
         for i in (2, 4, 6, 7):
             arrived(i)
@@ -602,21 +598,16 @@
         for k in range(1, planes):
             hop2_copy(w, h1, h2, k).wait_send()
 
-    def place(parts, i, rows_of):
-        full = None
-        for g in range(planes):
-            v = lax.dot_general(
-                parts[g], picks[g], (((0,), (0,)), ((), ())),
-                precision=lax.Precision.HIGHEST, preferred_element_type=F32,
-            )
-            full = v if full is None else full + v
-        grad_refs[i][...] = rows_of(full)
+    pick_all = jnp.concatenate(picks, axis=0)
+
+    def spread(h2):
+        return lax.dot_general(
+            h2.reshape(planes * RANK, h2.shape[-1]), pick_all, (((0,), (0,)), ((), ())),
+            precision=lax.Precision.HIGHEST, preferred_element_type=F32,
+        )
 
     def half_rows(v):
         return jnp.where(s % 2 == 0, v[:64], v[64:])
-
-    def all_rows(v):
-        return v
 
     for c in range(3):
         g = ADAPTER_SCALE * dot(coeff_t[:RANK, :], pg[c])
@@ -697,6 +688,17 @@
         return carry
 
     lax.fori_loop(0, tiles, inner, 0)
+    for k in range(1, planes):
+        adapter_copy(k).wait_send()
+    for sends, _ in gathers:
+        for copy in sends:
+            copy.wait_send()
+    spot = (8, planes, RANK, share)
+    for i in range(length // (8 * planes * RANK)):
+        span = 8 * planes * RANK
+        adm[:, :, :, i * share : (i + 1) * share] = normed[
+            i * span : (i + 1) * span, block(s, share)
+        ].reshape(spot)
     g = dot(cgs_t[RANK : 2 * RANK, :], act[...])
     for j in range(4):
         a_msg[j, :, :256] = g[:, j * 256 : (j + 1) * 256]
@@ -706,15 +708,18 @@
     partners = (to_core, to_x, to_y)
 
     def reduce_copy(w, i):
-        return remote(
-            ar_send.at[w], ar_recv.at[w, i], ar_ssem.at[w, i], ar_rsem.at[w, i], partners[i]
-        )
+        src = ar_send.at[0] if w == 0 else ar_low
+        dst = ar_recv.at[i] if w == 0 else ar_recv_low.at[i]
+        return remote(src, dst, ar_ssem.at[w, i], ar_rsem.at[w, i], partners[i])
 
     def reduce_round(w, i):
         if i > 0:
             reduce_copy(w, i - 1).wait()
-            ar_send[w] += ar_recv[w, i - 1]
+            got = ar_recv[i - 1] if w == 0 else ar_recv_low[i - 1].astype(F32)
+            ar_send[w] += got
         if i < 3:
+            if w == 1:
+                ar_low[...] = ar_send[1].astype(BF16)
             reduce_copy(w, i).start()
 
     ar_send[0, :RANK, :] = dot_nt(ddown(), att[...])
@@ -751,6 +756,10 @@
         keep[n % 6, k] = jnp.where(first, a, b)
         s1_send[slot, k] = jnp.where(first, b, a).astype(BF16)
 
+    def keep_pair(n, k, v):
+        keep_split(n, 2 * k, v[:TILE])
+        keep_split(n, 2 * k + 1, v[TILE:])
+
     def s1_copy(n):
         return remote(s1_send.at[n % 2], s1_recv.at[n], s1_ssem.at[n % 2], s1_rsem.at[n], to_core)
 
@@ -772,29 +781,28 @@
         j, i = branch_place(n)
 
         def tile(k, carry):
-            r = block(k, TILE)
+            r = block(k, 2 * TILE)
             cols = block(i, PART)
             w_o = jnp.concatenate([wo[j, :, cols], wo[j + 1, :, cols]], axis=1)
             w_d = jnp.concatenate([wd[j, :, cols], wd[j + 1, :, cols]], axis=1)
-            keep_split(n, k, dot(act[r, :], w_o) + dot(att[r, :], w_d))
+            keep_pair(n, k, dot(act[r, :], w_o) + dot(att[r, :], w_d))
             return carry
 
-        lax.fori_loop(0, tiles, tile, 0)
+        lax.fori_loop(0, tiles // 2, tile, 0)
         s1_copy(n).start()
 
     def stage0_back(n):
         j, i = back_place(n)
 
         def tile(k, carry):
-            r = block(k, TILE)
+            r = block(k, 2 * TILE)
             rws = block(i, UNIT)
             v = dot_nt(pgrad[r, :], wi[j, rws, :])
-            for c in range(3):
-                v = v + dot_nt(pg[c, r, :], wq[j, c, rws, :])
-            keep_split(n, k, v)
+            v = v + normed[r, block(n - p_units, UNIT)].astype(F32)
+            keep_pair(n, k, v)
             return carry
 
-        lax.fori_loop(0, tiles, tile, 0)
+        lax.fori_loop(0, tiles // 2, tile, 0)
         s1_copy(n).start()
 
     def stage1(n):
@@ -837,7 +845,7 @@
         def _():
             igrad_ref[:, block(n - p_units, UNIT)] = v
 
-    def pipeline(first, lo, hi, stage0, extra=None):
+    def pipeline(first, lo, hi, stage0, extra=None, units_end=None):
         def body(n, carry):
             if stage0 is not None:
                 stage0(n)
@@ -845,7 +853,7 @@
                 m = n - back
                 ok = m >= first
                 if stage0 is None:
-                    ok = jnp.logical_and(ok, m < hi - 5)
+                    ok = jnp.logical_and(ok, m < units_end)
 
                 @pl.when(ok)
                 def _(m=m, stage=stage):
@@ -858,53 +866,43 @@
         lax.fori_loop(lo, hi, body, 0)
 
     zstep(13)
-    zfinish(8, 10)
-    pass
-    per_part = planes // 2
-    pipeline(0, 0, 2 * per_part, stage0_branch)
-
     def act_part(r, i):
         cols = [slice(j * fan + i * PART, j * fan + (i + 1) * PART) for j in range(planes)]
         g = jnp.concatenate([cot[r, c] for c in cols], axis=1)
         w = [wo[j, :, i * PART : (i + 1) * PART] for j in range(planes)]
         return dot_nt(g, jnp.concatenate(w, axis=1))
 
-    def act_back(t, carry):
-        r = block(t, TILE)
-        v = dot(cgs[r, RANK : 2 * RANK], odown_ref[...])
-        for i in range(2):
-            v = v + act_part(r, i)
-        ag[r, :] = v
+    def attention_back(u, carry):
+        j = u // per
+        rws = block(u % per, UNIT)
+        for h in range(2):
+            r = slice(h * length // 2, (h + 1) * length // 2)
+            v = dot_nt(pg[0, r, :], wq[j, 0, rws, :])
+            for c in range(1, 3):
+                v = v + dot_nt(pg[c, r, :], wq[j, c, rws, :])
+            normed[r, block(u, UNIT)] = v.astype(BF16)
         return carry
 
-    hop2(0, a_h1, a_h2)
-    lax.fori_loop(0, tiles, act_back, 0)
-    qkv_landed()
-    landed(0, a_h1, a_h2)
-    place([a_h2[g, :, :256] for g in range(planes)], 6, all_rows)
-    place([a_h2[g, :, 256:384] for g in range(planes)], 2, half_rows)
-    place([a_h2[g, :, 384:512] for g in range(planes)], 3, half_rows)
-    place([a_h2[g, :, 512:640] for g in range(planes)], 7, half_rows)
-
-    def qkv_rows(v):
-        return jnp.where(s % 2 == 0, v[:192], v[64:])
-
-    place(
-        [jnp.concatenate([q_h2[g, 0], q_h2[g, 1]], axis=1) for g in range(planes)], 1, qkv_rows
-    )
-    pass
-    zfinish(10, 11)
-    pipeline(0, 2 * per_part, early, stage0_branch)
-
-    def act_more(t, carry):
-        r = block(t, TILE)
-        ag[r, :] += act_part(r, 2)
-        return carry
-
-    lax.fori_loop(0, tiles, act_more, 0)
+    lax.fori_loop(0, p_units, attention_back, 0)
+
+    per_part = planes // 2
+    for i in range(fan // PART - 1):
+        zfinish(8 + i, 9 + i)
+        pipeline(0, i * per_part, (i + 1) * per_part, stage0_branch)
+
+        def act_back(t, carry, i=i):
+            r = block(t, TILE)
+            first = dot(cgs[r, RANK : 2 * RANK], odown_ref[...]) if i == 0 else ag[r, :]
+            ag[r, :] = first + act_part(r, i)
+            return carry
+
+        lax.fori_loop(0, tiles, act_back, 0)
+        if i == 0:
+            hop2(0, a_h1, a_h2)
+    pipeline(0, early, early + 5, None, None, early)
     zfinish(11, 12)
 
-    pipeline(0, early, p_units, stage0_branch)
+    pipeline(early, early, p_units, stage0_branch)
 
     def act_last(t, carry):
         r = block(t, TILE)
@@ -914,18 +912,37 @@
 
     lax.fori_loop(0, tiles, act_last, 0)
 
-    up_part = dot_nt(iup_ref[...], pgrad[...])
-    q_part = dot_nt(qup(0), pg[0])
-    for c in range(1, 3):
-        q_part = q_part + dot_nt(qup(c), pg[c])
-    ar_send[1, :RANK, :] = ADAPTER_SCALE * q_part
-    ar_send[1, RANK : 2 * RANK, :] = ADAPTER_SCALE * up_part
-    reduce_round(1, 0)
-
     def rounds(n):
+        @pl.when(n == p_units)
+        def _():
+            up_part = dot_nt(iup_ref[...], pgrad[...])
+            q_part = dot_nt(qup(0), pg[0])
+            for c in range(1, 3):
+                q_part = q_part + dot_nt(qup(c), pg[c])
+            ar_send[1, :RANK, :] = ADAPTER_SCALE * q_part
+            ar_send[1, RANK : 2 * RANK, :] = ADAPTER_SCALE * up_part
+            reduce_round(1, 0)
+
+        @pl.when(n == p_units + 1)
+        def _():
+            qkv_landed()
+            full = [spread(q_h2[:, i]) for i in range(2)]
+            full = jnp.concatenate(full, axis=0)
+            grad_refs[1][...] = jnp.where(s % 2 == 0, full[:192], full[64:])
+
+        @pl.when(n == p_units + 3)
+        def _():
+            landed(0, a_h1, a_h2)
+            full = spread(a_h2[...])
+            grad_refs[6][...] = full[:256]
+            grad_refs[2][...] = half_rows(full[256:384])
+            grad_refs[3][...] = half_rows(full[384:512])
+            grad_refs[7][...] = half_rows(full[512:640])
+
+
         for i in range(1, 4):
 
-            @pl.when(n == p_units + 2 * i - 1)
+            @pl.when(n == p_units + (1, 3, 5)[i - 1])
             def _(i=i):
                 reduce_round(1, i)
                 if i == 2:
@@ -933,7 +950,14 @@
                     for j in range(4):
                         b_msg[j, :, :256] = g[:, j * 256 : (j + 1) * 256]
                 if i == 3:
-                    g = dot(ar_send[1].astype(BF16), normed[:, block(s, share)])
+                    g = None
+                    span = 8 * planes * RANK
+                    for m in range(length // span):
+                        part = dot(
+                            ar_send[1, :, m * span : (m + 1) * span].astype(BF16),
+                            adm[:, :, :, m * share : (m + 1) * share].reshape(span, share),
+                        )
+                        g = part if g is None else g + part
                     for m in range(2):
                         for j in range(4):
                             b_msg[j, :, 256 + m * 128 : 384 + m * 128] = g[
@@ -941,9 +965,10 @@
                             ]
                     hop1(1, b_msg, b_h1, True)
 
-    pipeline(0, p_units, total, stage0_back, rounds)
+    pipeline(early, p_units, total, stage0_back, rounds)
+    pipeline(early, total, total + 3, None, None, total)
     hop2(1, b_h1, b_h2)
-    pipeline(0, total, total + 5, None)
+    pipeline(early, total + 3, total + 5, None, None, total)
 
     first_t = ar_send[0, :, block(s, rows)].astype(BF16)
     late_t = ar_send[1, :, block(s, rows)].astype(BF16)
@@ -962,18 +987,14 @@
     )
 
     landed(1, b_h1, b_h2)
-    place([b_h2[g, :, :256] for g in range(planes)], 5, all_rows)
-    place([b_h2[g, :, 256:384] for g in range(planes)], 0, half_rows)
-    place([b_h2[g, :, 384:512] for g in range(planes)], 4, half_rows)
+    full = spread(b_h2[...])
+    grad_refs[5][...] = full[:256]
+    grad_refs[0][...] = half_rows(full[256:384])
+    grad_refs[4][...] = half_rows(full[384:512])
 
     hop1(0, a_msg, a_h1, False)
     hop1(1, b_msg, b_h1, False)
     qkv_hop1(False)
-    for k in range(1, planes):
-        adapter_copy(k).wait_send()
-    for sends, _ in gathers:
-        for copy in sends:
-            copy.wait_send()
     for c in range(n_chunks):
         for k in range(planes - 1):
             for direction in (0, 1):
@@ -997,7 +1018,7 @@
     def entry(*refs):
         layer_kernel(planes, *refs[:13], refs[13:21], *refs[21:25], refs[25:33], *refs[33:])
 
-    return pl.pallas_call(
+    outs = pl.pallas_call(
         entry,
         out_shape=(
             jax.ShapeDtypeStruct((rows, width), BF16),
@@ -1057,7 +1078,9 @@
             pltpu.VMEM((3, 2, rows, UNIT), BF16),
             pltpu.VMEM((total, 2, rows, UNIT), BF16),
             pltpu.VMEM((2, 2 * RANK, length), F32),
-            pltpu.VMEM((2, 3, 2 * RANK, length), F32),
+            pltpu.VMEM((3, 2 * RANK, length), F32),
+            pltpu.VMEM((2 * RANK, length), BF16),
+            pltpu.VMEM((3, 2 * RANK, length), BF16),
             dma((n_chunks,)),
             dma((n_chunks, 2, planes)),
             dma((n_chunks, planes)),
@@ -1086,6 +1109,17 @@
             collective_id=0, has_side_effects=True, vmem_limit_bytes=63 * 1024 * 1024
         ),
     )(*args)
+    return pl.pallas_call(
+        hand_over,
+        out_shape=tuple(jax.ShapeDtypeStruct(o.shape, o.dtype) for o in outs),
+        in_specs=[vm] * 10,
+        out_specs=(vm,) * 10,
+    )(*outs)
+
+
+def hand_over(*refs):
+    for i in range(10):
+        refs[10 + i][...] = refs[i][...]
 
 
 def fits(planes, groups, shapes):

time: 280 us -> 270 us (0.964)
  local copies, waits for them, and re-layouts: 8.49 us -> 0 us
    unnamed x28 -> x0, local copies, waits for them, and re-layouts: 8.49 us -> none
    pallas_call x1, Pallas kernels: 271 us -> 266 us  [run_layer(): pl.pallas_call(entry, out_shape=(jax.ShapeDtypeStruct((rows, width), BF16...]
    pallas_call x0 -> x1, Pallas kernels: none -> 2.88 us  [run_layer(): pl.pallas_call(hand_over, out_shape=tuple((jax.ShapeDtypeStruct(o.shape,...]
where the time goes in v5:
time: 270 us; the launch traced here: 269 us
  Pallas kernels  269 us (100%)
    pallas_call x1, Pallas kernels, run_layer(): pl.pallas_call(entry, out_shape=(jax.ShapeDtypeStruct((rows, width), BF16...  266 us

profile of v5, /device:TPU:0, one launch (start us, length us, event | category | flops | bytes accessed | tf_op | source)
XLA Modules:
  0.0 269.5 jit_solution(20811451491973638)
XLA Ops:
  0.7 265.8 %shard_map.294 = (bf16[128,2048]{1,0:T(8,128)(2,1)}, f32[128,2048]{1,0:T(8,128)}, f32[64,128]{1,0:T(8,128)}, f32[192,128]{1,0:T(8,128)}, f32[64,128]{1,0:T(8,128...) custom-call(bf16[128,2048]{1,0:T(8,128)(2,1)} %refs_0_.1, ...), custom_call_target="tpu_custom_call" | custom-call | tf_op jit(solution)/shard_map/pallas_call | solution.py:1021
  266.5 2.9 %shard_map.295 = (bf16[128,2048]{1,0:T(8,128)(2,1)}, f32[128,2048]{1,0:T(8,128)}, f32[64,128]{1,0:T(8,128)}, f32[192,128]{1,0:T(8,128)}, f32[64,128]{1,0:T(8,128...) custom-call(bf16[128,2048]{1,0:T(8,128)(2,1)} %get-tuple-element.20., ...), custom_call_target="tpu_custom_call" | custom-call | tf_op jit(solution)/shard_map/pallas_call | solution.py:1112

commit v6 on v5

--- a/solution.py
+++ b/solution.py
@@ -386,8 +386,8 @@
     column = lax.broadcasted_iota(jnp.int32, (RANK, ADAPT * RANK), 0)
     picks = []
     for g in range(planes):
-        picks.append((lane == column + index_ref[g] * RANK).astype(F32))
-        sel[g] = dot_nt(picks[g].astype(BF16), stack[...]).astype(BF16)
+        picks.append((lane == column + index_ref[g] * RANK).astype(F32).astype(BF16))
+        sel[g] = dot_nt(picks[g], stack[...]).astype(BF16)
 
     def adapter_copy(k):
         g = (z + k) % planes
@@ -601,10 +601,7 @@
     pick_all = jnp.concatenate(picks, axis=0)
 
     def spread(h2):
-        return lax.dot_general(
-            h2.reshape(planes * RANK, h2.shape[-1]), pick_all, (((0,), (0,)), ((), ())),
-            precision=lax.Precision.HIGHEST, preferred_element_type=F32,
-        )
+        return dot_tn(h2.reshape(planes * RANK, h2.shape[-1]), pick_all)
 
     def half_rows(v):
         return jnp.where(s % 2 == 0, v[:64], v[64:])
@@ -612,7 +609,7 @@
     for c in range(3):
         g = ADAPTER_SCALE * dot(coeff_t[:RANK, :], pg[c])
         for i in range(2):
-            qgrad[2 * c + i] = g[:, i * 128 : (i + 1) * 128]
+            qgrad[2 * c + i] = g[:, i * 128 : (i + 1) * 128].astype(BF16)
 
     def qkv_hop1(start):
         for c in range(3):
@@ -667,7 +664,7 @@
     qkv_hop1(True)
     g = dot(cgs_t[:RANK, :], att[...])
     for j in range(4):
-        a_msg[j, :, 256:384] = g[:, (j // 2) * 128 : (j // 2 + 1) * 128]
+        a_msg[j, :, 256:384] = g[:, (j // 2) * 128 : (j // 2 + 1) * 128].astype(BF16)
     pass
     zfinish(4, 8)
     zstep(11)
@@ -701,7 +698,7 @@
         ].reshape(spot)
     g = dot(cgs_t[RANK : 2 * RANK, :], act[...])
     for j in range(4):
-        a_msg[j, :, :256] = g[:, j * 256 : (j + 1) * 256]
+        a_msg[j, :, :256] = g[:, j * 256 : (j + 1) * 256].astype(BF16)
     qkv_hop2()
     zstep(12)
 
@@ -734,7 +731,7 @@
         )
         for j in range(4):
             at = 384 + i * 128
-            a_msg[j, :, at : at + 128] = g[:, (j // 2) * 128 : (j // 2 + 1) * 128]
+            a_msg[j, :, at : at + 128] = g[:, (j // 2) * 128 : (j // 2 + 1) * 128].astype(BF16)
     hop1(0, a_msg, a_h1, True)
 
     p_units = width // UNIT
@@ -892,17 +889,20 @@
 
         def act_back(t, carry, i=i):
             r = block(t, TILE)
-            first = dot(cgs[r, RANK : 2 * RANK], odown_ref[...]) if i == 0 else ag[r, :]
-            ag[r, :] = first + act_part(r, i)
+            if i == 1:
+                v = dot(cgs[r, RANK : 2 * RANK], odown_ref[...]) + act_part(r, 0)
+                ag[r, :] = v + act_part(r, 1)
+            else:
+                ag[r, :] += act_part(r, i)
             return carry
 
-        lax.fori_loop(0, tiles, act_back, 0)
-        if i == 0:
+        if i > 0:
+            lax.fori_loop(0, tiles, act_back, 0)
+        if i == 1:
             hop2(0, a_h1, a_h2)
-    pipeline(0, early, early + 5, None, None, early)
     zfinish(11, 12)
 
-    pipeline(early, early, p_units, stage0_branch)
+    pipeline(0, early, p_units, stage0_branch)
 
     def act_last(t, carry):
         r = block(t, TILE)
@@ -948,7 +948,7 @@
                 if i == 2:
                     g = ADAPTER_SCALE * dot(coeff_t[RANK : 2 * RANK, :], pgrad[...])
                     for j in range(4):
-                        b_msg[j, :, :256] = g[:, j * 256 : (j + 1) * 256]
+                        b_msg[j, :, :256] = g[:, j * 256 : (j + 1) * 256].astype(BF16)
                 if i == 3:
                     g = None
                     span = 8 * planes * RANK
@@ -962,13 +962,13 @@
                         for j in range(4):
                             b_msg[j, :, 256 + m * 128 : 384 + m * 128] = g[
                                 m * RANK : (m + 1) * RANK, (j // 2) * 128 : (j // 2 + 1) * 128
-                            ]
+                            ].astype(BF16)
                     hop1(1, b_msg, b_h1, True)
 
-    pipeline(early, p_units, total, stage0_back, rounds)
-    pipeline(early, total, total + 3, None, None, total)
+    pipeline(0, p_units, total, stage0_back, rounds)
+    pipeline(0, total, total + 3, None, None, total)
     hop2(1, b_h1, b_h2)
-    pipeline(early, total + 3, total + 5, None, None, total)
+    pipeline(0, total + 3, total + 5, None, None, total)
 
     first_t = ar_send[0, :, block(s, rows)].astype(BF16)
     late_t = ar_send[1, :, block(s, rows)].astype(BF16)
@@ -1040,15 +1040,15 @@
             pltpu.VMEM((RANK, 3 * width), BF16),
             pltpu.VMEM((RANK, units), BF16),
             pltpu.VMEM((RANK, units), BF16),
-            pltpu.VMEM((6, RANK, 128), F32),
-            pltpu.VMEM((4, RANK, 640), F32),
-            pltpu.VMEM((planes, RANK, 640), F32),
-            pltpu.VMEM((planes, RANK, 640), F32),
-            pltpu.VMEM((4, RANK, 512), F32),
-            pltpu.VMEM((planes, RANK, 512), F32),
-            pltpu.VMEM((planes, RANK, 512), F32),
-            pltpu.VMEM((planes, 2, RANK, 128), F32),
-            pltpu.VMEM((planes, 2, RANK, 128), F32),
+            pltpu.VMEM((6, RANK, 128), BF16),
+            pltpu.VMEM((4, RANK, 640), BF16),
+            pltpu.VMEM((planes, RANK, 640), BF16),
+            pltpu.VMEM((planes, RANK, 640), BF16),
+            pltpu.VMEM((4, RANK, 512), BF16),
+            pltpu.VMEM((planes, RANK, 512), BF16),
+            pltpu.VMEM((planes, RANK, 512), BF16),
+            pltpu.VMEM((planes, 2, RANK, 128), BF16),
+            pltpu.VMEM((planes, 2, RANK, 128), BF16),
             pltpu.VMEM((length, width), BF16),
             pltpu.VMEM((length, width), BF16),
             pltpu.VMEM((planes, 3, fan, mine), BF16),

time: 270 us -> 260 us (0.963)
  Pallas kernels: 269 us -> 259 us
    pallas_call x1, Pallas kernels: 266 us -> 256 us  [run_layer(): pl.pallas_call(entry, out_shape=(jax.ShapeDtypeStruct((rows, width), BF16...]
where the time goes in v6:
time: 260 us
  Pallas kernels  259 us (100%)
    pallas_call x1, Pallas kernels, run_layer(): pl.pallas_call(entry, out_shape=(jax.ShapeDtypeStruct((rows, width), BF16...  256 us

profile of v6, /device:TPU:0, one launch (start us, length us, event | category | flops | bytes accessed | tf_op | source)
XLA Modules:
  0.0 259.8 jit_solution(3787610221898061019)
XLA Ops:
  0.7 256.2 %shard_map.294 = (bf16[128,2048]{1,0:T(8,128)(2,1)}, f32[128,2048]{1,0:T(8,128)}, f32[64,128]{1,0:T(8,128)}, f32[192,128]{1,0:T(8,128)}, f32[64,128]{1,0:T(8,128...) custom-call(bf16[128,2048]{1,0:T(8,128)(2,1)} %refs_0_.1, ...), custom_call_target="tpu_custom_call" | custom-call | tf_op jit(solution)/shard_map/pallas_call | solution.py:1021
  256.8 2.9 %shard_map.295 = (bf16[128,2048]{1,0:T(8,128)(2,1)}, f32[128,2048]{1,0:T(8,128)}, f32[64,128]{1,0:T(8,128)}, f32[192,128]{1,0:T(8,128)}, f32[64,128]{1,0:T(8,128...) custom-call(bf16[128,2048]{1,0:T(8,128)(2,1)} %get-tuple-element.20., ...), custom_call_target="tpu_custom_call" | custom-call | tf_op jit(solution)/shard_map/pallas_call | solution.py:1112

commit v7 on v6

--- a/solution.py
+++ b/solution.py
@@ -374,14 +374,15 @@
     for i in range(3):
         c_sends[i].start()
 
-    counts = [m.shape[0] for m in map_refs]
-    spans = [2 * n if n % 128 else n for n in counts]
-    bases = [sum(spans[:i]) for i in range(8)]
-    stack[...] = jnp.zeros_like(stack)
-    odd = s % 2
-    for m, n, span, base in zip(map_refs, counts, spans, bases):
-        at = base + (odd * n if span != n else 0)
-        stack[pl.ds(pl.multiple_of(at, 64), n), :] = m[...]
+    n_in = map_refs[5].shape[0]
+    spots = ((0, 0), (4, 64), (3, 128), (7, 192), (2, 256))
+    for m, at in spots:
+        stack[at : at + 64, :] = map_refs[m][...]
+    stack[320:384, :] = map_refs[1][128:, :]
+    stack[384:512, :] = map_refs[1][:128, :]
+    base_in, base_out = 512, 512 + n_in
+    stack[base_in : base_in + n_in, :] = map_refs[5][...]
+    stack[base_out : base_out + n_in, :] = map_refs[6][...]
     lane = lax.broadcasted_iota(jnp.int32, (RANK, ADAPT * RANK), 1)
     column = lax.broadcasted_iota(jnp.int32, (RANK, ADAPT * RANK), 0)
     picks = []
@@ -433,27 +434,43 @@
     zstep(5)
 
     def order(f, carry):
+        low_half = lax.broadcasted_iota(jnp.int32, (RANK, 128), 1) < 64
+
+        def swap(v):
+            return pltpu.roll(v, 64, 1)
+
         for pair in range(4):
 
-            def both(i):
-                cols = slice(bases[i], bases[i] + spans[i])
-                return adm[2 * pair, f, :, cols] + adm[2 * pair + 1, f, :, cols]
+            def tile(odd, i):
+                return adm[2 * pair + odd, f, :, i * 128 : (i + 1) * 128].astype(F32)
+
+            def first(i):
+                return jnp.where(low_half, tile(0, i), swap(tile(1, i))).astype(BF16)
+
+            def second(i):
+                return jnp.where(low_half, swap(tile(0, i)), tile(1, i)).astype(BF16)
 
             where = block(f * 4 + pair, 128)
-            downs_ref[:RANK, where] = both(0)
-            downs_ref[RANK:, where] = both(4)
-            ups_ref[:RANK, where] = both(3)
-            ups_ref[RANK:, where] = both(7)
-            ddown_all[:, where] = both(2)
-            qup_all[:, block(f * 4 + pair, spans[1])] = both(1)
+            downs_ref[:RANK, where] = first(0)
+            downs_ref[RANK:, where] = second(0)
+            ups_ref[:RANK, where] = first(1)
+            ups_ref[RANK:, where] = second(1)
+            ddown_all[:, where] = first(2)
+            turned = swap(tile(1, 3))
+            at = (f * 4 + pair) * 3
+            qup_all[:, block(at, 128)] = tile(0, 3).astype(BF16)
+            qup_all[:, block(at + 1, 128)] = jnp.where(
+                low_half, swap(tile(0, 2)), turned
+            ).astype(BF16)
+            qup_all[:, block(at + 2, 128)] = jnp.where(low_half, turned, tile(1, 2)).astype(BF16)
         return carry
 
     lax.fori_loop(0, planes, order, 0)
     for j in range(4):
         q = s * 4 + j
-        n = counts[5]
-        iup_ref[:, j * n : (j + 1) * n] = adm[q % 8, q // 8, :, bases[5] : bases[5] + n]
-        odown_ref[:, j * n : (j + 1) * n] = adm[q % 8, q // 8, :, bases[6] : bases[6] + n]
+        n = n_in
+        iup_ref[:, j * n : (j + 1) * n] = adm[q % 8, q // 8, :, base_in : base_in + n]
+        odown_ref[:, j * n : (j + 1) * n] = adm[q % 8, q // 8, :, base_out : base_out + n]
 
     def qup(c):
         return qup_all[:, pl.ds(pl.multiple_of(c * width + s * mine, mine), mine)]
@@ -699,7 +716,6 @@
     g = dot(cgs_t[RANK : 2 * RANK, :], act[...])
     for j in range(4):
         a_msg[j, :, :256] = g[:, j * 256 : (j + 1) * 256].astype(BF16)
-    qkv_hop2()
     zstep(12)
 
     partners = (to_core, to_x, to_y)
@@ -721,9 +737,22 @@
 
     ar_send[0, :RANK, :] = dot_nt(ddown(), att[...])
     ar_send[0, RANK : 2 * RANK, :] = dot_nt(odown_ref[...], act[...])
+    p_units = width // UNIT
+    per = fan // UNIT
+    def attention_back(u, carry):
+        j = u // per
+        rws = block(u % per, UNIT)
+        for h in range(2):
+            r = slice(h * length // 2, (h + 1) * length // 2)
+            v = dot_nt(pg[0, r, :], wq[j, 0, rws, :])
+            for c in range(1, 3):
+                v = v + dot_nt(pg[c, r, :], wq[j, c, rws, :])
+            normed[r, block(u, UNIT)] = v.astype(BF16)
+        return carry
+
     for i in range(4):
         reduce_round(0, i)
-        pass
+        lax.fori_loop(2 * i, 2 * i + 2, attention_back, 0)
     coeff_dense = ar_send[0].astype(BF16)
     for i in range(2):
         g = ADAPTER_SCALE * dot(
@@ -869,19 +898,6 @@
         w = [wo[j, :, i * PART : (i + 1) * PART] for j in range(planes)]
         return dot_nt(g, jnp.concatenate(w, axis=1))
 
-    def attention_back(u, carry):
-        j = u // per
-        rws = block(u % per, UNIT)
-        for h in range(2):
-            r = slice(h * length // 2, (h + 1) * length // 2)
-            v = dot_nt(pg[0, r, :], wq[j, 0, rws, :])
-            for c in range(1, 3):
-                v = v + dot_nt(pg[c, r, :], wq[j, c, rws, :])
-            normed[r, block(u, UNIT)] = v.astype(BF16)
-        return carry
-
-    lax.fori_loop(0, p_units, attention_back, 0)
-
     per_part = planes // 2
     for i in range(fan // PART - 1):
         zfinish(8 + i, 9 + i)
@@ -898,8 +914,6 @@
 
         if i > 0:
             lax.fori_loop(0, tiles, act_back, 0)
-        if i == 1:
-            hop2(0, a_h1, a_h2)
     zfinish(11, 12)
 
     pipeline(0, early, p_units, stage0_branch)
@@ -922,8 +936,10 @@
             ar_send[1, :RANK, :] = ADAPTER_SCALE * q_part
             ar_send[1, RANK : 2 * RANK, :] = ADAPTER_SCALE * up_part
             reduce_round(1, 0)
-
-        @pl.when(n == p_units + 1)
+            qkv_hop2()
+            hop2(0, a_h1, a_h2)
+
+        @pl.when(n == p_units + 4)
         def _():
             qkv_landed()
             full = [spread(q_h2[:, i]) for i in range(2)]
@@ -1013,7 +1029,7 @@
     total = 2 * width // UNIT
     dma = pltpu.SemaphoreType.DMA
     maps = args[13:21]
-    lanes = sum(2 * m.shape[0] if m.shape[0] % 128 else m.shape[0] for m in maps)
+    lanes = sum(m.shape[0] for m in maps)
 
     def entry(*refs):
         layer_kernel(planes, *refs[:13], refs[13:21], *refs[21:25], refs[25:33], *refs[33:])

time: 260 us -> 258 us (level)
  no operation moved by 1% of the time
where the time goes in v7:
time: 258 us
  Pallas kernels  257 us (100%)
    pallas_call x1, Pallas kernels, run_layer(): pl.pallas_call(entry, out_shape=(jax.ShapeDtypeStruct((rows, width), BF16...  254 us

profile of v7, /device:TPU:0, one launch (start us, length us, event | category | flops | bytes accessed | tf_op | source)
XLA Modules:
  0.0 258.1 jit_solution(3259128402638177890)
XLA Ops:
  0.7 254.5 %shard_map.294 = (bf16[128,2048]{1,0:T(8,128)(2,1)}, f32[128,2048]{1,0:T(8,128)}, f32[64,128]{1,0:T(8,128)}, f32[192,128]{1,0:T(8,128)}, f32[64,128]{1,0:T(8,128...) custom-call(bf16[128,2048]{1,0:T(8,128)(2,1)} %refs_0_.1, ...), custom_call_target="tpu_custom_call" | custom-call | tf_op jit(solution)/shard_map/pallas_call | solution.py:1037
  255.1 2.9 %shard_map.295 = (bf16[128,2048]{1,0:T(8,128)(2,1)}, f32[128,2048]{1,0:T(8,128)}, f32[64,128]{1,0:T(8,128)}, f32[192,128]{1,0:T(8,128)}, f32[64,128]{1,0:T(8,128...) custom-call(bf16[128,2048]{1,0:T(8,128)(2,1)} %get-tuple-element.20., ...), custom_call_target="tpu_custom_call" | custom-call | tf_op jit(solution)/shard_map/pallas_call | solution.py:1128

commit v8 on v7

--- a/solution.py
+++ b/solution.py
@@ -397,6 +397,7 @@
     for k in range(1, planes):
         adapter_copy(k).start()
     adm[s, z] = sel[z]
+    zstep(1)
 
     x = tok_ref[...].astype(F32)
     mean = jnp.mean(x, axis=-1, keepdims=True)
@@ -411,7 +412,6 @@
         pltpu.make_async_copy(adm.at[s, g], adm.at[s, g], adz_rsem.at[g]).wait()
     m_sends, m_arrived = gather_copies(2, adm, lead_view)
     gathers = ((c_sends, c_arrived), (n_sends, n_arrived), (m_sends, m_arrived))
-    zstep(1)
     for m, (sends, arrived) in enumerate(gathers):
         arrived(0)
         sends[3].start()

time: 258 us -> 256 us (level)
  no operation moved by 1% of the time
where the time goes in v8:
time: 256 us
  Pallas kernels  255 us (100%)
    pallas_call x1, Pallas kernels, run_layer(): pl.pallas_call(entry, out_shape=(jax.ShapeDtypeStruct((rows, width), BF16...  252 us

profile of v8, /device:TPU:0, one launch (start us, length us, event | category | flops | bytes accessed | tf_op | source)
XLA Modules:
  0.0 255.8 jit_solution(169048540196369896)
XLA Ops:
  0.7 252.1 %shard_map.294 = (bf16[128,2048]{1,0:T(8,128)(2,1)}, f32[128,2048]{1,0:T(8,128)}, f32[64,128]{1,0:T(8,128)}, f32[192,128]{1,0:T(8,128)}, f32[64,128]{1,0:T(8,128...) custom-call(bf16[128,2048]{1,0:T(8,128)(2,1)} %refs_0_.1, ...), custom_call_target="tpu_custom_call" | custom-call | tf_op jit(solution)/shard_map/pallas_call | solution.py:1037
  252.8 2.9 %shard_map.295 = (bf16[128,2048]{1,0:T(8,128)(2,1)}, f32[128,2048]{1,0:T(8,128)}, f32[64,128]{1,0:T(8,128)}, f32[192,128]{1,0:T(8,128)}, f32[64,128]{1,0:T(8,128...) custom-call(bf16[128,2048]{1,0:T(8,128)(2,1)} %get-tuple-element.20., ...), custom_call_target="tpu_custom_call" | custom-call | tf_op jit(solution)/shard_map/pallas_call | solution.py:1128
